TPU v7x, 32 devices: a whole 2x2x4 slice. The times are simulated.
32 devices in a mesh: gx: 2 (over y), gy: 4 (over z), gz: 4 (over x, core).
Axes of the slice: x: 2, y: 2, z: 4, core: 2. Of those that a mesh axis runs over, the one named last changes fastest.
Arguments:
- populations: float32 [19, 32, 64, 512], P(None, 'gx', 'gy', 'gz'), may hold values from 0.02 to 0.1
- solid_flags: int32 [32, 64, 512], P('gx', 'gy', 'gz'), may hold values 0 or 1
- positions: float32 [448, 3, 128], P(('gx', 'gy', 'gz')), may hold values from -4 to 4
- anchors: float32 [448, 3, 128], P(('gx', 'gy', 'gz')), may hold values from -4 to 4
- base_cell: int32 [448, 3, 128], P(('gx', 'gy', 'gz')), may hold values from 0 to 510, as said below
- weights: float32 [448, 8, 128], P(('gx', 'gy', 'gz')), may hold values from 0.1 to 0.2
- intersection: int32 [448, 2], P(('gx', 'gy', 'gz')), may hold values from 0 to 15, as said below
Outputs:
- read: float32 [19, 32, 64, 512], P(None, 'gx', 'gy', 'gz')
- vertex_velocity: float32 [448, 3, 128], P(('gx', 'gy', 'gz'))
Inputs may be any that keep to these rules, and one draw needn't show every extreme that they name: `intersection`: patch p's two bricks differ and lie in its owner's slab. For every owner, no brick is listed by more than 4 of its patches, and in every slab a quarter of the bricks are listed by exactly 4 patches of every owner of that slab. `base_cell`: all eight kernel cells of a vertex lie in one brick, in the slab of the patch's owner, and that brick is on the patch's list.
All inputs are finite; a program needn't handle non-finite values. No bound on the sum of `solid_flags` on one device may be relied on, other than what follows from the above.
Results may differ from a plain program's by a relative error of at most 0.00011.
Values sent between devices are 32-bit elements; how exact they have to be, the bound alone decides.
No kernel may reach another device: no remote copies, remote signals or barrier semaphores. Data moves between devices by JAX's collectives and lax.ppermute only.
A program may use at most 320 MiB of HBM per device.

v0:
```python
import functools

import jax
import jax.numpy as jnp
from jax import lax
from jax.experimental import pallas as pl
from jax.experimental.pallas import tpu as pltpu
from jax.sharding import PartitionSpec as P

SLOT_CAP = 4
GROUPS = 7
EDGE_LANE = 80

RELAXATION = 0.8
TENSION = 0.05
TETHER = 0.5
VELOCITIES = [
    (0, 0, 0),
    (1, 0, 0),
    (-1, 0, 0),
    (0, 1, 0),
    (0, -1, 0),
    (0, 0, 1),
    (0, 0, -1),
    (1, 1, 0),
    (-1, -1, 0),
    (1, -1, 0),
    (-1, 1, 0),
    (1, 0, 1),
    (-1, 0, -1),
    (1, 0, -1),
    (-1, 0, 1),
    (0, 1, 1),
    (0, -1, -1),
    (0, 1, -1),
    (0, -1, 1),
]
LATTICE_WEIGHTS = [1.0 / 3.0] + [1.0 / 18.0] * 6 + [1.0 / 36.0] * 12


def crossing(axis, sign):
    return [q for q in range(19) if VELOCITIES[q][axis] == sign]


X_LISTS = {1: crossing(0, 1), -1: crossing(0, -1)}
Y_LISTS = {1: crossing(1, 1), -1: crossing(1, -1)}
Z_LISTS = {1: crossing(2, 1), -1: crossing(2, -1)}
Y_EDGES = {s: [q for q in Y_LISTS[s] if VELOCITIES[q][0] != 0] for s in (1, -1)}
Z_EDGES = {
    s: [q for q in Z_LISTS[s] if VELOCITIES[q][0] != 0 or VELOCITIES[q][1] != 0] for s in (1, -1)
}

BF = jnp.bfloat16
F32 = jnp.float32
MIB = 1024 * 1024
NT = (((1,), (1,)), ((), ()))
NN = (((1,), (0,)), ((), ()))


def settings(mib):
    return pltpu.CompilerParams(vmem_limit_bytes=mib * MIB)


def cost(flops, size):
    return pl.CostEstimate(flops=flops, bytes_accessed=size, transcendentals=0)


def vmem():
    return pl.BlockSpec(memory_space=pltpu.VMEM)


def smem():
    return pl.BlockSpec(memory_space=pltpu.SMEM)


def list_kernel(
    bricks_z,
    inter_ref,
    pos_ref,
    anchor_ref,
    cell_ref,
    weight_ref,
    out_ref,
    rank_ref,
    base_ref,
    payload,
    lists,
    count_ref,
    extent,
):
    patches, verts = pos_ref.shape[1:]
    bricks = out_ref.shape[0]
    pos = pos_ref[...]
    cycle_term = pltpu.roll(pos, 1, 2) + pltpu.roll(pos, verts - 1, 2) - 2.0 * pos
    forces = TENSION * cycle_term + TETHER * (anchor_ref[...] - pos)
    cells = cell_ref[...].astype(F32)
    payload[:, 0:8, :] = weight_ref[...]
    for p in range(patches):
        payload[p, 8:11, :] = forces[:, p, :]
        payload[p, 11:14, :] = cells[:, p, :] + 1.0
        payload[p, 14:16, :] = jnp.zeros((2, verts), F32)
    lists[...] = jnp.zeros(lists.shape, F32)

    @pl.loop(0, bricks)
    def _(b):
        count_ref[b] = 0

    lane = lax.broadcasted_iota(jnp.int32, (patches, verts), 1)
    row = lax.broadcasted_iota(jnp.int32, (patches, verts), 0)
    upper = (
        lax.broadcasted_iota(jnp.int32, (verts, verts), 0)
        <= lax.broadcasted_iota(jnp.int32, (verts, verts), 1)
    ).astype(F32)
    codes, sums = [], []
    for i in range(2):
        first_y = jnp.zeros((patches, verts), F32)
        first_z = jnp.zeros((patches, verts), F32)
        for p in range(patches):
            brick = inter_ref[i, p]
            first_y = jnp.where(row == p, (brick // bricks_z * extent[1]).astype(F32), first_y)
            first_z = jnp.where(row == p, (brick % bricks_z * extent[2]).astype(F32), first_z)
        live = (
            (cells[1] >= first_y)
            & (cells[1] < first_y + extent[1])
            & (cells[2] >= first_z)
            & (cells[2] < first_z + extent[2])
        )
        mask = live.astype(F32)
        total = jnp.dot(mask.astype(BF), upper.astype(BF), preferred_element_type=F32)
        rank = (total - mask).astype(jnp.int32)
        rank_ref[i] = jnp.where(live, rank, -1)
        code = jnp.where(live, (lane - rank) + lane * 256 + 65536, 0)
        step = 1
        while step < verts:
            moving = jnp.where((code & step) != 0, code, 0)
            code = (code - moving) + pltpu.roll(moving, verts - step, 1)
            step *= 2
        codes.append(code)
        sums.append(total)
    wide_lane = lax.broadcasted_iota(jnp.int32, (16, verts), 1)
    for p in range(patches):
        for i in range(2):
            brick = inter_ref[i, p]
            base = count_ref[brick]
            base_ref[2 * p + i] = base
            count_ref[brick] = base + jnp.max(sums[i][p : p + 1, :]).astype(jnp.int32)
            block = lax.shift_right_logical(base, 7)
            shift = base & (verts - 1)
            code = jnp.broadcast_to(codes[i][p : p + 1, :], (8, verts))
            code = pltpu.roll(code, shift, 1)
            code = jnp.concatenate([code, code], axis=0)
            source = lax.shift_right_logical(code, 8) & (verts - 1)
            moved = jnp.take_along_axis(payload[p], source, axis=1)
            moved = jnp.where(code >= 65536, moved, 0.0)
            lists[brick, block] += jnp.where(wide_lane >= shift, moved, 0.0)
            lists[brick, block + 1] += jnp.where(wide_lane < shift, moved, 0.0)

    @pl.loop(0, bricks)
    def _(b):
        for j in range(SLOT_CAP):
            value = lists[b, j]
            first = j // 2 * GROUPS
            for g in range(3):
                out_ref[b, first + j % 2 * 3 + g] = value[4 * g : 4 * g + 4]
            out_ref[b, first + 6, j % 2 * 2 : j % 2 * 2 + 2] = value[12:14]


def build_lists(intersection, positions, anchors, base_cell, weights, bricks, bricks_z, extent):
    _, patches, verts = positions.shape

    def kernel(*refs):
        list_kernel(bricks_z, *refs, extent)

    return pl.pallas_call(
        kernel,
        out_shape=(
            jax.ShapeDtypeStruct((bricks, 2 * GROUPS, 4, verts), F32),
            jax.ShapeDtypeStruct((2, patches, verts), jnp.int32),
            jax.ShapeDtypeStruct((2 * patches,), jnp.int32),
        ),
        in_specs=[smem(), vmem(), vmem(), vmem(), vmem()],
        out_specs=(vmem(), vmem(), smem()),
        scratch_shapes=[
            pltpu.VMEM((patches, 16, verts), F32),
            pltpu.VMEM((bricks, SLOT_CAP + 1, 16, verts), F32),
            pltpu.SMEM((bricks,), jnp.int32),
        ],
        compiler_params=settings(56),
        name="vertex_lists",
    )(intersection, positions, anchors, base_cell, weights)


def block_rows(table_ref, owner, j):
    first = j // 2 * GROUPS
    group = first + j % 2 * 3
    weight = jnp.concatenate([table_ref[owner, group], table_ref[owner, group + 1]], axis=0)
    third = table_ref[owner, group + 2]
    line = j % 2 * 2
    last = table_ref[owner, first + 6, line : line + 2]
    return weight, third[0:3], jnp.concatenate([third[3:4], last], axis=0)


def pack_far(table_ref, packed, spot_ref):
    owners, _, _, verts = table_ref.shape
    packed[...] = jnp.zeros(packed.shape, F32)
    lane = lax.broadcasted_iota(jnp.int32, (16, verts), 1)
    counts = []
    for owner in range(owners):
        for j in range(2):
            held = (table_ref[owner, GROUPS + 3 * j + 2, 3:4, :] > 0.0).astype(F32)
            counts.append(jnp.sum(held).astype(jnp.int32))
    spot = jnp.int32(0)
    for owner in range(owners):
        for j in range(2):
            count = counts[2 * owner + j]
            spot_ref[2 * owner + j] = spot

            @pl.when(count > 0)
            def _(owner=owner, j=j, spot=spot):
                weight, force, cells = block_rows(table_ref, owner, 2 + j)
                rows = jnp.concatenate(
                    [weight, force, cells, jnp.zeros((2, verts), F32)], axis=0
                )
                block = lax.shift_right_logical(spot, 7)
                shift = spot & (verts - 1)
                rows = pltpu.roll(rows, shift, 1)
                packed[block] += jnp.where(lane >= shift, rows, 0.0)
                packed[block + 1] += jnp.where(lane < shift, rows, 0.0)

            spot = spot + count
    spot_ref[2 * owners] = spot


def packed_blocks(spot, verts):
    return lax.shift_right_logical(spot + verts - 1, 7)


def packed_rows(packed, block):
    return packed[block, 0:8], packed[block, 8:11], packed[block, 11:14]


def place_rows(place_ref, rows, extent):
    weight, force, cells = rows
    local, inside = [], None
    for d in range(3):
        value = cells[d : d + 1] - (place_ref[d] + 1).astype(F32)
        ok = (value >= 0.0) & (value < float(extent[d]))
        inside = ok if inside is None else inside & ok
        local.append(value)
    weight = weight * jnp.broadcast_to(inside.astype(F32), weight.shape)
    return weight, force, local


def halves(value):
    high = value.astype(BF).astype(F32)
    return high, value - high


def spread_scratch(extent, verts):
    size_x, size_y, size_z = extent
    depth = SLOT_CAP * 2 * verts
    return [
        pltpu.VMEM((2, 2, size_x * size_y, depth), BF),
        pltpu.VMEM((2, 6 * size_z, depth), BF),
        pltpu.VMEM((2, SLOT_CAP, 16, verts), F32),
        pltpu.VMEM((2, SLOT_CAP, 8, verts), F32),
        pltpu.VMEM((2, SLOT_CAP, 8, verts), F32),
    ]


def spread_tools(place_ref, extent, verts, total, a_buf, zf_buf, w_rows, f_rows, c_rows):
    size_x, size_y, size_z = extent
    iota_y = lax.broadcasted_iota(jnp.int32, (16, verts), 0).astype(F32).astype(BF)
    zero = jnp.zeros((16, verts), BF)

    def wide(ref, slot, j, row):
        return jnp.broadcast_to(ref[slot, j, row : row + 1, :], (16, verts)).astype(BF)

    def build(blocks, slot):
        for j, rows in enumerate(blocks):
            weight, force, local = place_rows(place_ref, rows, extent)
            w_hi, w_lo = halves(weight)
            f_hi, f_lo = halves(force)
            w_rows[slot, j, 0:8] = w_hi
            w_rows[slot, j, 8:16] = w_lo
            f_rows[slot, j, 0:3] = f_hi
            f_rows[slot, j, 4:7] = f_lo
            for d in range(3):
                c_rows[slot, j, d : d + 1] = local[d]
        for j in range(len(blocks)):
            xl = wide(c_rows, slot, j, 0)
            yl = wide(c_rows, slot, j, 1)
            zl = wide(c_rows, slot, j, 2)
            at_y0 = iota_y == yl
            at_y1 = iota_y == yl + 1.0
            lines = {}
            for part in range(2):
                for dx in range(2):
                    for dz in range(2):
                        first = part * 8 + dx * 4 + dz
                        lines[part, dx, dz] = jnp.where(
                            at_y0,
                            wide(w_rows, slot, j, first),
                            jnp.where(at_y1, wide(w_rows, slot, j, first + 2), zero),
                        )
            before = None
            for x in range(size_x):
                here = xl == float(x)
                for part in range(2):
                    for dz in range(2):
                        value = jnp.where(here, lines[part, 0, dz], zero)
                        if before is not None:
                            value = jnp.where(before, lines[part, 1, dz], value)
                        column = (j * 2 + dz) * verts
                        a_buf[slot, part, x * 16 : (x + 1) * 16, column : column + verts] = value
                before = here
            force = [wide(f_rows, slot, j, part * 4 + c) for part in range(2) for c in range(3)]
            for zb in range(size_z // 16):
                for dz in range(2):
                    at_z = iota_y == zl + float(dz - 16 * zb)
                    column = (j * 2 + dz) * verts
                    for part in range(2):
                        for c in range(3):
                            line = (part * 3 + c) * size_z + zb * 16
                            zf_buf[slot, line : line + 16, column : column + verts] = jnp.where(
                                at_z, force[part * 3 + c], zero
                            )

    def product(slot, blocks=SLOT_CAP):
        lines = 3 * size_z
        depth = blocks * 2 * verts
        high = lax.dot_general(
            zf_buf[slot, :, :depth], a_buf[slot, 0, :, :depth], NT, preferred_element_type=F32
        )
        low = lax.dot_general(
            zf_buf[slot, :lines, :depth],
            a_buf[slot, 1, :, :depth],
            NT,
            preferred_element_type=F32,
        )
        total[...] += high[:lines] + high[lines:] + low

    return build, product


def pair_blocks(table_ref, step):
    return [block_rows(table_ref, 2 * step + oo, j) for oo in range(2) for j in range(2)]


def settle_kernel(pop, solid, base_ref, fluid_ref):
    keep = 1.0 - 1.0 / RELAXATION

    @pl.loop(0, solid.shape[0], unroll=2)
    def _(x):
        wall = solid[x] == 1
        fluid_ref[x] = jnp.where(wall, 0.0, 1.0)
        base_ref[0, x] = jnp.where(wall, pop[0, x], keep * pop[0, x])
        for q in range(1, 19, 2):
            one, two = pop[q, x], pop[q + 1, x]
            base_ref[q, x] = jnp.where(wall, two, keep * one)
            base_ref[q + 1, x] = jnp.where(wall, one, keep * two)


def settle(populations, solid):
    return pl.pallas_call(
        settle_kernel,
        out_shape=(
            jax.ShapeDtypeStruct(populations.shape, F32),
            jax.ShapeDtypeStruct(solid.shape, F32),
        ),
        in_specs=[vmem(), vmem()],
        out_specs=(vmem(), vmem()),
        compiler_params=settings(12),
        cost_estimate=cost(16 * MIB, 8 * MIB),
        name="settle",
    )(populations, solid)


def collide_kernel(
    place_ref,
    table_ref,
    base_ref,
    fluid_ref,
    post,
    xface_ref,
    yfp_ref,
    yfm_ref,
    zfp_ref,
    zfm_ref,
    unit_ref,
    packed,
    spot_ref,
    total,
    field,
    *scratch,
):
    _, size_x, size_y, size_z = post.shape
    owners, _, _, verts = table_ref.shape
    build, product = spread_tools(
        place_ref, (size_x, size_y, size_z), verts, total, *scratch
    )
    steps = owners // 2
    total[...] = jnp.zeros(total.shape, F32)
    pack_far(table_ref, packed, spot_ref)
    build(pair_blocks(table_ref, 0), 0)

    @pl.loop(0, steps // 2)
    def _(i):
        build(pair_blocks(table_ref, 2 * i + 1), 1)
        product(0)
        build(pair_blocks(table_ref, jnp.minimum(2 * i + 2, steps - 1)), 0)
        product(1)

    @pl.loop(0, packed_blocks(spot_ref[2 * owners], verts))
    def _(block):
        build([packed_rows(packed, block)], 0)
        product(0, 1)

    for c in range(3):
        for half in range(size_x * size_y // 128):
            field[c, half * 128 : (half + 1) * 128, :] = jnp.transpose(
                total[c * size_z : (c + 1) * size_z, half * 128 : (half + 1) * 128]
            )

    lane = lax.broadcasted_iota(jnp.int32, (size_y, size_z), 1)
    factor = 1.0 - 0.5 / RELAXATION
    rate = 1.0 / RELAXATION
    keep = 1.0 - rate

    def plane(x, z_out):
        z_out = dict(zip((1, -1), z_out))
        lines = pl.ds(pl.multiple_of(x * 16, 16), 16)
        force = [field[c, lines, :] for c in range(3)]
        fluid = fluid_ref[x]
        cells = [base_ref[q, x] for q in range(19)]
        rho = cells[0]
        for q in range(1, 19):
            rho = rho + cells[q]
        moment = []
        for c in range(3):
            value = None
            for q in range(1, 19, 2):
                if VELOCITIES[q][c] != 0:
                    term = cells[q] - cells[q + 1]
                    if VELOCITIES[q][c] < 0:
                        term = -term
                    value = term if value is None else value + term
            moment.append(value)
        rho = rho * jnp.where(fluid > 0.0, 1.0 / keep, 1.0)
        sign = jnp.where(fluid > 0.0, 1.0 / keep, -1.0)
        inverse = 1.0 / rho
        rho = rho * fluid
        vel = [(moment[c] * sign + 0.5 * force[c]) * inverse for c in range(3)]
        for c in range(3):
            high, low = halves(vel[c])
            first = pl.ds(pl.multiple_of((x * 3 + c) * 16, 16), 16)
            unit_ref[first, 0:size_z] = high.astype(BF)
            unit_ref[first, size_z : 2 * size_z] = low.astype(BF)
        speed = vel[0] * vel[0] + vel[1] * vel[1] + vel[2] * vel[2]
        u_dot_f = vel[0] * force[0] + vel[1] * force[1] + vel[2] * force[2]
        three = (3.0 * factor) * fluid
        nine = (9.0 * factor) * fluid
        rest = (rate * rho) * (1.0 - 1.5 * speed) - three * u_dot_f
        quad = (4.5 * rate) * rho
        linear = (3.0 * rate) * rho
        results = [None] * 19
        results[0] = cells[0] + LATTICE_WEIGHTS[0] * rest

        def along(vector, q):
            value = None
            for c in range(3):
                move = VELOCITIES[q][c]
                if move == 0:
                    continue
                if value is None:
                    value = vector[c] if move > 0 else -vector[c]
                else:
                    value = value + vector[c] if move > 0 else value - vector[c]
            return value

        for q in range(1, 19, 2):
            a = along(vel, q)
            b = along(force, q)
            weight = LATTICE_WEIGHTS[q]
            even = weight * (rest + a * (quad * a + nine * b))
            odd = weight * (linear * a + three * b)
            results[q] = cells[q] + (even + odd)
            results[q + 1] = cells[q + 1] + (even - odd)
        for q in range(19):
            post[q, x] = results[q]
        for sign, line, face in ((1, size_y - 1, yfp_ref), (-1, 0, yfm_ref)):
            for k, q in enumerate(Y_LISTS[sign]):
                face[k, pl.ds(x, 1), :] = results[q][line : line + 1, :]
        for sign, column in ((1, size_z - 1), (-1, 0)):
            for k, q in enumerate(Z_LISTS[sign]):
                place = k * 16 + x
                moved = pltpu.roll(results[q], (place - column + size_z) & (size_z - 1), 1)
                z_out[sign] = jnp.where(lane == place, moved, z_out[sign])
        return z_out[1], z_out[-1]

    empty = jnp.zeros((size_y, size_z), F32)
    zfp_ref[...], zfm_ref[...] = lax.fori_loop(0, size_x, plane, (empty, empty), unroll=2)
    for k, q in enumerate(X_LISTS[1]):
        xface_ref[k] = post[q, size_x - 1]
    for k, q in enumerate(X_LISTS[-1]):
        xface_ref[5 + k] = post[q, 0]


def collide(place, table, base, fluid):
    _, size_x, size_y, size_z = base.shape
    owners, _, _, verts = table.shape
    cross = size_x * size_y
    face_y = jax.ShapeDtypeStruct((5, size_x, size_z), F32)
    face_z = jax.ShapeDtypeStruct((size_y, size_z), F32)
    return pl.pallas_call(
        collide_kernel,
        out_shape=(
            jax.ShapeDtypeStruct(base.shape, F32),
            jax.ShapeDtypeStruct((10, size_y, size_z), F32),
            face_y,
            face_y,
            face_z,
            face_z,
            jax.ShapeDtypeStruct((cross * 3, 2 * size_z), BF),
            jax.ShapeDtypeStruct((2 * owners + 1, 16, verts), F32),
            jax.ShapeDtypeStruct((2 * owners + 1,), jnp.int32),
        ),
        in_specs=[smem()] + [vmem()] * 3,
        out_specs=(vmem(),) * 8 + (smem(),),
        scratch_shapes=[
            pltpu.VMEM((3 * size_z, cross), F32),
            pltpu.VMEM((3, cross, size_z), F32),
        ]
        + spread_scratch((size_x, size_y, size_z), verts),
        compiler_params=settings(24),
        cost_estimate=cost(6 * owners * 3 * size_z * cross * 4 * verts, 6 * MIB),
        name="spread_collide",
    )(place, table, base, fluid)


def sample_scratch(extent, verts):
    size_x, size_y, size_z = extent
    return [
        pltpu.VMEM((2, SLOT_CAP, 2 * size_z, 2 * verts), BF),
        pltpu.VMEM((2, 3 * size_x * size_y, 2 * verts), F32),
        pltpu.VMEM((2, SLOT_CAP, 8, verts), F32),
        pltpu.VMEM((2, SLOT_CAP, 8, verts), F32),
    ]


def sample_tools(place_ref, unit_ref, extent, verts, hot, grid_buf, w_rows, c_rows):
    size_x, size_y, size_z = extent
    iota_y = lax.broadcasted_iota(jnp.int32, (16, verts), 0).astype(F32)
    iota_b = iota_y.astype(BF)
    one = jnp.ones((16, verts), BF)
    zero_b = jnp.zeros((16, verts), BF)
    zero = jnp.zeros((16, verts), F32)

    def wide(ref, slot, j, row):
        return jnp.broadcast_to(ref[slot, j, row : row + 1, :], (16, verts))

    def prepare(blocks, slot):
        for j, rows in enumerate(blocks):
            weight, _, local = place_rows(place_ref, rows, extent)
            w_rows[slot, j] = weight
            for d in range(3):
                c_rows[slot, j, d : d + 1] = local[d]
        for j in range(len(blocks)):
            zl = wide(c_rows, slot, j, 2).astype(BF)
            for zb in range(size_z // 16):
                for dz in range(2):
                    value = jnp.where(iota_b == zl + float(dz - 16 * zb), one, zero_b)
                    for part in range(2):
                        line = part * size_z + zb * 16
                        hot[slot, j, line : line + 16, dz * verts : (dz + 1) * verts] = value

    def product(slot, j):
        grid_buf[j % 2] = lax.dot_general(unit_ref[...], hot[slot, j], NN, preferred_element_type=F32)

    def select(slot, j):
        xl = wide(c_rows, slot, j, 0)
        yl = wide(c_rows, slot, j, 1)
        at_y0 = iota_y == yl
        at_y1 = iota_y == yl + 1.0
        lines = {}
        for dx in range(2):
            for dz in range(2):
                first = dx * 4 + dz
                lines[dx, dz] = jnp.where(
                    at_y0,
                    wide(w_rows, slot, j, first),
                    jnp.where(at_y1, wide(w_rows, slot, j, first + 2), zero),
                )
        sums = [zero, zero, zero]
        before = None
        for x in range(size_x):
            here = xl == float(x)
            for dz in range(2):
                value = jnp.where(here, lines[0, dz], zero)
                if before is not None:
                    value = jnp.where(before, lines[1, dz], value)
                for c in range(3):
                    first = (x * 3 + c) * 16
                    part = grid_buf[j % 2, first : first + 16, dz * verts : (dz + 1) * verts]
                    sums[c] = sums[c] + value * part
            before = here
        return [jnp.sum(value, axis=0, keepdims=True) for value in sums]

    def work(slot, store):
        product(slot, 0)
        for j in range(SLOT_CAP):
            if j + 1 < SLOT_CAP:
                product(slot, j + 1)
            store(j, select(slot, j))

    return prepare, product, select, work


def x_plane(xr_ref, q):
    sign = VELOCITIES[q][0]
    return xr_ref[(0 if sign > 0 else 5) + X_LISTS[sign].index(q)]


def sample_kernel(extent, place_ref, spot_ref, table_ref, packed, unit_ref, out_ref, found, *scratch):
    owners, _, _, verts = table_ref.shape
    prepare, product, select, work = sample_tools(place_ref, unit_ref, extent, verts, *scratch)
    steps = owners // 2
    out_ref[...] = jnp.zeros(out_ref.shape, F32)

    def store(step):
        def put(j, values):
            for c in range(3):
                out_ref[2 * step + j // 2, j % 2, c : c + 1, :] = values[c]

        return put

    prepare(pair_blocks(table_ref, 0), 0)

    @pl.loop(0, steps // 2)
    def _(i):
        prepare(pair_blocks(table_ref, 2 * i + 1), 1)
        work(0, store(2 * i))
        prepare(pair_blocks(table_ref, jnp.minimum(2 * i + 2, steps - 1)), 0)
        work(1, store(2 * i + 1))

    @pl.loop(0, packed_blocks(spot_ref[2 * owners], verts))
    def _(block):
        prepare([packed_rows(packed, block)], 0)
        product(0, 0)
        values = select(0, 0)
        for c in range(3):
            found[block, c : c + 1, :] = values[c]

    lane = lax.broadcasted_iota(jnp.int32, (4, verts), 1)
    for owner in range(owners):
        for j in range(2):
            spot = spot_ref[2 * owner + j]

            @pl.when(spot_ref[2 * owner + j + 1] > spot)
            def _(owner=owner, j=j, spot=spot):
                block = lax.shift_right_logical(spot, 7)
                shift = spot & (verts - 1)
                back = (verts - shift) & (verts - 1)
                first = pltpu.roll(found[block, 0:4], back, 1)
                second = pltpu.roll(found[block + 1, 0:4], back, 1)
                value = jnp.where(lane < verts - shift, first, second)
                out_ref[owner, 2 + j, 0:3, :] = value[0:3]


def sample(place, spots, table, packed, unit, extent):
    owners, _, _, verts = table.shape
    size_x, size_y, size_z = extent
    return pl.pallas_call(
        functools.partial(sample_kernel, extent),
        out_shape=jax.ShapeDtypeStruct((owners, SLOT_CAP, 4, verts), F32),
        in_specs=[smem(), smem()] + [vmem()] * 3,
        out_specs=vmem(),
        scratch_shapes=[pltpu.VMEM((2 * owners + 2, 8, verts), F32)]
        + sample_scratch(extent, verts),
        compiler_params=settings(12),
        cost_estimate=cost(16 * owners * 3 * size_x * size_y * size_z * verts, MIB),
        name="sample_velocity",
    )(place, spots, table, packed, unit)


def y_message_kernel(xr_ref, yfp_ref, yfm_ref, plus_ref, minus_ref):
    size_y = xr_ref.shape[1]
    for sign, face, out in ((1, yfp_ref, plus_ref), (-1, yfm_ref, minus_ref)):
        out[0:5] = face[...]
        line = size_y - 1 if sign > 0 else 0
        for e, q in enumerate(Y_EDGES[sign]):
            out[5, e : e + 1, :] = x_plane(xr_ref, q)[line : line + 1, :]


def y_messages(x_halo, y_plus, y_minus):
    shape = jax.ShapeDtypeStruct((6,) + y_plus.shape[1:], F32)
    return pl.pallas_call(
        y_message_kernel,
        out_shape=(shape, shape),
        in_specs=[vmem()] * 3,
        out_specs=(vmem(), vmem()),
        compiler_params=settings(4),
        name="y_messages",
    )(x_halo, y_plus, y_minus)


def z_message_kernel(xr_ref, yrp_ref, yrm_ref, zfp_ref, zfm_ref, plus_ref, minus_ref):
    size_y, size_z = zfp_ref.shape
    y_halo = {1: yrp_ref, -1: yrm_ref}
    lane = lax.broadcasted_iota(jnp.int32, (size_y, size_z), 1)
    for sign, face, out in ((1, zfp_ref, plus_ref), (-1, zfm_ref, minus_ref)):
        column = size_z - 1 if sign > 0 else 0
        block = face[...]
        for e, q in enumerate(Z_EDGES[sign]):
            if VELOCITIES[q][0] != 0:
                plane = x_plane(xr_ref, q)
            else:
                y_sign = VELOCITIES[q][1]
                plane = y_halo[y_sign][Y_LISTS[y_sign].index(q)]
            spot = EDGE_LANE + e
            block = jnp.where(lane == spot, pltpu.roll(plane, (spot - column) % size_z, 1), block)
        out[...] = block


def z_messages(x_halo, y_plus, y_minus, z_plus, z_minus):
    shape = jax.ShapeDtypeStruct(z_plus.shape, F32)
    return pl.pallas_call(
        z_message_kernel,
        out_shape=(shape, shape),
        in_specs=[vmem()] * 5,
        out_specs=(vmem(), vmem()),
        compiler_params=settings(4),
        name="z_messages",
    )(x_halo, y_plus, y_minus, z_plus, z_minus)


def stream_kernel(
    post,
    xr_ref,
    yrp_ref,
    yrm_ref,
    zrp_ref,
    zrm_ref,
    read_hbm,
    read,
    out_sem,
):
    _, size_x, size_y, size_z = post.shape
    y_halo = {1: yrp_ref, -1: yrm_ref}
    z_halo = {1: zrp_ref, -1: zrm_ref}
    stores = [pltpu.make_async_copy(read.at[q], read_hbm.at[q], out_sem.at[q]) for q in range(19)]
    lane = lax.broadcasted_iota(jnp.int32, (size_y, size_z), 1)
    row = lax.broadcasted_iota(jnp.int32, (size_y, size_z), 0)

    def shift_z(plane, cz, place):
        moved = pltpu.roll(plane, cz % size_z, 1)
        target = 0 if cz > 0 else size_z - 1
        column = pltpu.roll(z_halo[cz][...], (target - place) % size_z, 1)
        return jnp.where(lane == target, column, moved)

    for q in range(19):
        cx, cy, cz = VELOCITIES[q]
        rows = None
        if cy != 0:
            rows = y_halo[cy][Y_LISTS[cy].index(q)]
            if cz != 0:
                rows = shift_z(rows, cz, EDGE_LANE + Z_EDGES[cz].index(q))
        for x in range(size_x):
            source = x - cx
            outside = source < 0 or source >= size_x
            plane = x_plane(xr_ref, q) if outside else post[q, source]
            if cz != 0:
                if outside:
                    place = EDGE_LANE + Z_EDGES[cz].index(q)
                else:
                    place = Z_LISTS[cz].index(q) * 16 + source
                plane = shift_z(plane, cz, place)
            if cy != 0:
                moved = pltpu.roll(plane, cy % size_y, 0)
                target = 0 if cy > 0 else size_y - 1
                if outside:
                    e = Y_EDGES[cy].index(q)
                    line = y_halo[cy][5, e : e + 1, :]
                else:
                    line = rows[source : source + 1, :]
                plane = jnp.where(row == target, jnp.broadcast_to(line, moved.shape), moved)
            read[q, x] = plane
        stores[q].start()
    for store in stores:
        store.wait()


def stream(post, x_halo, y_plus, y_minus, z_plus, z_minus):
    anyspace = pl.BlockSpec(memory_space=pl.ANY)
    return pl.pallas_call(
        stream_kernel,
        out_shape=jax.ShapeDtypeStruct(post.shape, F32),
        in_specs=[vmem()] * 6,
        out_specs=anyspace,
        scratch_shapes=[
            pltpu.VMEM(post.shape, F32),
            pltpu.SemaphoreType.DMA((19,)),
        ],
        compiler_params=settings(10),
        cost_estimate=cost(MIB, 16 * MIB),
        name="stream_populations",
    )(post, x_halo, y_plus, y_minus, z_plus, z_minus)


def collect_kernel(inter_ref, base_ref, rank_ref, back_ref, out_ref):
    patches, verts = rank_ref.shape[1:]
    for p in range(patches):
        value = None
        for i in range(2):
            brick = inter_ref[i, p]
            base = base_ref[2 * p + i]
            rank = jnp.broadcast_to(rank_ref[i, p : p + 1, :], (8, verts))
            spot = rank + base
            block = lax.shift_right_logical(base, 7)
            other = jnp.minimum(block + 1, SLOT_CAP - 1)
            both = jnp.concatenate([back_ref[brick, block], back_ref[brick, other]], axis=0)
            picked = jnp.take_along_axis(both, spot & (verts - 1), axis=1)
            here = lax.shift_right_arithmetic(spot, 7)[0:3] == block
            picked = jnp.where(here, picked[0:3], picked[4:7])
            picked = jnp.where(rank[0:3] >= 0, picked, 0.0)
            value = picked if value is None else value + picked
        out_ref[:, p, :] = value


def collect(intersection, bases, ranks, back):
    _, patches, verts = ranks.shape
    return pl.pallas_call(
        collect_kernel,
        out_shape=jax.ShapeDtypeStruct((3, patches, verts), F32),
        in_specs=[smem()] * 2 + [vmem()] * 2,
        out_specs=vmem(),
        compiler_params=settings(4),
        name="collect_velocity",
    )(intersection, bases, ranks, back)


def shifted(value, axis, step):
    count = lax.axis_size(axis)
    return lax.ppermute(value, axis, [(i, (i + step) % count) for i in range(count)])


def exchanged(value):
    return lax.all_to_all(value, ("gy", "gz"), split_axis=0, concat_axis=0, tiled=True)


def body(populations, solid_flags, positions, anchors, base_cell, weights, intersection):
    extent = populations.shape[1:]
    axes = ("gx", "gy", "gz")
    bricks = lax.axis_size("gy") * lax.axis_size("gz")
    here = [lax.axis_index(axis) for axis in axes]
    place = jnp.stack(
        [here[d] * extent[d] for d in range(3)]
        + here
        + [jnp.int32(lax.axis_size(axis)) for axis in axes]
    ).astype(jnp.int32)
    lists = intersection.T
    outgoing, ranks, bases = build_lists(
        lists,
        jnp.transpose(positions, (1, 0, 2)),
        jnp.transpose(anchors, (1, 0, 2)),
        jnp.transpose(base_cell, (1, 0, 2)),
        weights,
        bricks,
        lax.axis_size("gz"),
        extent,
    )
    table = exchanged(outgoing)
    base, fluid = settle(populations, solid_flags)
    post, x_face, y_plus, y_minus, z_plus, z_minus, unit, packed, spots = collide(
        place, table, base, fluid
    )
    if lax.axis_size("gx") == 2:
        x_halo = shifted(x_face, "gx", 1)
    else:
        x_halo = jnp.concatenate(
            [shifted(x_face[:5], "gx", 1), shifted(x_face[5:], "gx", -1)], axis=0
        )
    sampled = sample(place, spots, table, packed, unit, extent)
    back = exchanged(sampled)
    y_plus, y_minus = y_messages(x_halo, y_plus, y_minus)
    y_plus = shifted(y_plus, "gy", 1)
    y_minus = shifted(y_minus, "gy", -1)
    z_plus, z_minus = z_messages(x_halo, y_plus, y_minus, z_plus, z_minus)
    z_plus = shifted(z_plus, "gz", 1)
    z_minus = shifted(z_minus, "gz", -1)
    read = stream(post, x_halo, y_plus, y_minus, z_plus, z_minus)
    velocity = collect(lists, bases, ranks, back)
    return read, jnp.transpose(velocity, (1, 0, 2))


def solution(mesh):
    return jax.shard_map(
        body,
        mesh=mesh,
        in_specs=(
            P(None, "gx", "gy", "gz"),
            P("gx", "gy", "gz"),
            P(("gx", "gy", "gz"), None, None),
            P(("gx", "gy", "gz"), None, None),
            P(("gx", "gy", "gz"), None, None),
            P(("gx", "gy", "gz"), None, None),
            P(("gx", "gy", "gz"), None),
        ),
        out_specs=(P(None, "gx", "gy", "gz"), P(("gx", "gy", "gz"), None, None)),
        check_vma=False,
    )
```

profile of v0, /device:TPU:1, one launch (start us, length us, event | category | flops | bytes accessed | tf_op | source)
XLA Modules:
  0.0 66.9 jit_solution(18155701493981908298)
XLA Ops:
  0.6 3.3 %vertex_lists.1 = (f32[16,14,4,128]{3,2,1,0:T(4,128)}, s32[2,14,128]{2,1,0:T(8,128)}, s32[28]{0:T(128)}) custom-call(s32[2,14]{1,0:T(2,128)} %bitcast.11, f32[3,14,128]{2,1,0:T(8,128)} %bitcast.13, f32[3,14,128]{2,1,0:T(8,128)} %bitcast.14, s32[3,14,128]{2,1,0:T(8,128)} %bitcast.15, f32[14,8,128]{2,1,0:T(8,128)} %refs_4_.1), custom_call_target="tpu_custom_call" | custom-call | tf_op jit(solution)/shard_map/vertex_lists/pallas_call | solution.py:174
  3.9 7.3 %all-to-all-start = ((f32[16,14,4,128]{3,2,1,0:T(4,128)}), f32[16,14,4,128]{3,2,1,0:T(4,128)S(1)}, u32[]{:S(2)}, u32[]{:S(2)}) async-start(f32[16,14,4,128]{3,2,1,0:T(4,128)} %get-tuple-element.20), calls=%async_computation | async-start | bytes 917504 | tf_op jit(solution)/shard_map/all_to_all | solution.py:848
  11.3 0.1 stack.27.place_ref
  11.4 0.0 copy-start
  11.4 1.7 %copy-done = f32[19,16,16,128]{3,2,1,0:T(8,128)S(1)} copy-done((f32[19,16,16,128]{3,2,1,0:T(8,128)S(1)}, f32[19,16,16,128]{3,2,1,0:T(8,128)}, u32[]{:S(2)}) %copy-start) | copy-done | bytes 2490392
  13.1 0.0 copy-start.1
  13.1 0.9 %copy-done.1 = s32[16,16,128]{2,1,0:T(8,128)S(1)} copy-done((s32[16,16,128]{2,1,0:T(8,128)S(1)}, s32[16,16,128]{2,1,0:T(8,128)}, u32[]{:S(2)}) %copy-start.1) | copy-done | bytes 131096
  14.0 0.2 settle.1
  14.2 0.0 copy-start.5
  14.3 1.4 %copy-done.5 = f32[19,16,16,128]{3,2,1,0:T(8,128)} copy-done((f32[19,16,16,128]{3,2,1,0:T(8,128)}, f32[19,16,16,128]{3,2,1,0:T(8,128)S(1)}, u32[]{:S(2)}) %copy-start.5) | copy-done | bytes 2490392
  15.7 8.5 %all-to-all-done.table_ref = f32[16,14,4,128]{3,2,1,0:T(4,128)S(1)} async-done(((f32[16,14,4,128]{3,2,1,0:T(4,128)}), f32[16,14,4,128]{3,2,1,0:T(4,128)S(1)}, u32[]{:S(2)}, u32[]{:S(2)}) %all-to-all-start) | async-done | bytes 458784 | tf_op jit(solution)/shard_map/all_to_all | solution.py:848
  24.2 0.0 copy-start.6
  24.2 1.7 %copy-done.6 = f32[19,16,16,128]{3,2,1,0:T(8,128)S(1)} copy-done((f32[19,16,16,128]{3,2,1,0:T(8,128)S(1)}, f32[19,16,16,128]{3,2,1,0:T(8,128)}, u32[]{:S(2)}) %copy-start.6) | copy-done | bytes 2490392
  25.9 11.2 %spread_collide.1 = (f32[19,16,16,128]{3,2,1,0:T(8,128)S(1)}, f32[10,16,128]{2,1,0:T(8,128)S(1)}, f32[5,16,128]{2,1,0:T(8,128)S(1)}, f32[5,16,128]{2,1,0:T(8,128...) custom-call(s32[9]{0:T(128)S(1)} %stack.27.place_ref, ...), custom_call_target="tpu_custom_call" | custom-call | flops 4831838208 | bytes 6291456 | tf_op jit(solution)/shard_map/spread_collide/pallas_call | solution.py:515
  37.2 6.6 %sample_velocity.1 = f32[16,4,4,128]{3,2,1,0:T(4,128)} custom-call(s32[9]{0:T(128)S(1)} %stack.27.place_ref, s32[33]{0:T(128)S(1)} %get-tuple-element.35.spot_ref, f32[16,14,4,128]{3,2,1,0:T(4,128)S(1)} %all-to-all-done.table_ref, f32[33,16,128]{2,1,0:T(8,128)S(1)} %get-tuple-element.36.packed, bf16[768,256]{1,0:T(8,128)(2,1)S(1)} %get-tuple-element.37.unit_ref), custom_call_target="tpu_custom_call" | custom-call | flops 3221225472 | bytes 1048576 | tf_op jit(solution)/shard_map/sample_velocity/pallas_call | solution.py:673
  43.8 4.5 %all-to-all-start.1 = ((f32[16,4,4,128]{3,2,1,0:T(4,128)}), f32[16,4,4,128]{3,2,1,0:T(4,128)S(1)}, u32[]{:S(2)}, u32[]{:S(2)}) async-start(f32[16,4,4,128]{3,2,1,0:T(4,128)} %sample_velocity.1), calls=%async_computation.1 | async-start | bytes 262144 | tf_op jit(solution)/shard_map/all_to_all | solution.py:848
  48.3 0.7 %collective-permute-start = (f32[10,16,128]{2,1,0:T(8,128)S(1)}, f32[10,16,128]{2,1,0:T(8,128)S(1)}, u32[]{:S(2)}, u32[]{:S(2)}) collective-permute-start(f32[10,16,128]{2,1,0:T(8,128)S(1)} %get-tuple-element.24), channel_id=1, source_target_pairs={{0,16},{16,0},{1,17},{17,1},{2,18},{18,2},{3,19},{19,3},{4,20},{20... | collective-permute-start | bytes 245768 | tf_op jit(solution)/shard_map/ppermute | solution.py:844
  49.1 3.2 %collective-permute-done.xr_ref = f32[10,16,128]{2,1,0:T(8,128)S(1)} collective-permute-done((f32[10,16,128]{2,1,0:T(8,128)S(1)}, f32[10,16,128]{2,1,0:T(8,128)S(1)}, u32[]{:S(2)}, u32[]{:S(2)}) %collective-permute-start) | collective-permute-done | bytes 81952 | tf_op jit(solution)/shard_map/ppermute | solution.py:844
  52.2 1.2 %collective-permute-start.1 = (f32[6,16,128]{2,1,0:T(8,128)S(1)}, f32[6,16,128]{2,1,0:T(8,128)S(1)}, u32[]{:S(2)}, u32[]{:S(2)}) collective-permute-start(f32[6,16,128]{2,1,0:T(8,128)S(1)} %get-tuple-element.27), channel_id=1, source_target_pairs={{0,4},{4,8},{8,12},{12,0},{1,5},{5,9},{9,13},{13,1},{2,6},{6,10},{... | collective-permute-start | bytes 147464 | tf_op jit(solution)/shard_map/ppermute | solution.py:844
  53.5 2.1 %collective-permute-start.2 = (f32[6,16,128]{2,1,0:T(8,128)S(1)}, f32[6,16,128]{2,1,0:T(8,128)S(1)}, u32[]{:S(2)}, u32[]{:S(2)}) collective-permute-start(f32[6,16,128]{2,1,0:T(8,128)S(1)} %get-tuple-element.28), channel_id=1, source_target_pairs={{0,12},{4,0},{8,4},{12,8},{1,13},{5,1},{9,5},{13,9},{2,14},{6,2},{... | collective-permute-start | bytes 147464 | tf_op jit(solution)/shard_map/ppermute | solution.py:844
  55.6 1.5 %collective-permute-done.1.yrp_ref = f32[6,16,128]{2,1,0:T(8,128)S(1)} collective-permute-done((f32[6,16,128]{2,1,0:T(8,128)S(1)}, f32[6,16,128]{2,1,0:T(8,128)S(1)}, u32[]{:S(2)}, u32[]{:S(2)}) %collective-permute-start.1) | collective-permute-done | bytes 49184 | tf_op jit(solution)/shard_map/ppermute | solution.py:844
  57.1 0.0 collective-permute-done.2.yrm_ref
  57.1 0.1 z_messages.1
  57.1 3.6 %collective-permute-start.3 = (f32[16,128]{1,0:T(8,128)S(1)}, f32[16,128]{1,0:T(8,128)S(1)}, u32[]{:S(2)}, u32[]{:S(2)}) collective-permute-start(f32[16,128]{1,0:T(8,128)S(1)} %get-tuple-element.31), channel_id=1, source_target_pairs={{0,1},{1,2},{2,3},{3,0},{4,5},{5,6},{6,7},{7,4},{8,9},{9,10},{10,1... | collective-permute-start | bytes 24584 | tf_op jit(solution)/shard_map/ppermute | solution.py:844
  60.7 0.0 collective-permute-start.4
  60.7 0.8 %collective-permute-done.3.zrp_ref = f32[16,128]{1,0:T(8,128)S(1)} collective-permute-done((f32[16,128]{1,0:T(8,128)S(1)}, f32[16,128]{1,0:T(8,128)S(1)}, u32[]{:S(2)}, u32[]{:S(2)}) %collective-permute-start.3) | collective-permute-done | bytes 8224 | tf_op jit(solution)/shard_map/ppermute | solution.py:844
  61.5 2.3 %collective-permute-done.4.zrm_ref = f32[16,128]{1,0:T(8,128)S(1)} collective-permute-done((f32[16,128]{1,0:T(8,128)S(1)}, f32[16,128]{1,0:T(8,128)S(1)}, u32[]{:S(2)}, u32[]{:S(2)}) %collective-permute-start.4) | collective-permute-done | bytes 8224 | tf_op jit(solution)/shard_map/ppermute | solution.py:844
  63.8 0.0 copy-start.2
  63.8 0.0 copy-start.3
  63.8 0.0 copy-start.4
  63.8 1.6 %stream_populations.1 = f32[19,16,16,128]{3,2,1,0:T(8,128)} custom-call(f32[19,16,16,128]{3,2,1,0:T(8,128)S(1)} %get-tuple-element.23.post, f32[10,16,128]{2,1,0:T(8,128)S(1)} %collective-permute-done.xr_ref, f32[6,16,128]{2,1,0:T(8,128)S(1)} %collective-permute-done.1.yrp_ref, f32[6,16,128]{2,1,0:T(8,128)S(1)} %collective-permute-done.2.yrm_ref, ...), custom_call_target="tpu_custom_call" | custom-call | flops 1048576 | bytes 16777216 | tf_op jit(solution)/shard_map/stream_populations/pallas_call | solution.py:795
  65.5 0.0 all-to-all-done.1.back_ref
  65.5 0.0 copy-done.2
  65.5 0.0 copy-done.3
  65.5 0.0 copy-done.4
  65.5 1.3 %collect_velocity.1 = f32[3,14,128]{2,1,0:T(8,128)} custom-call(s32[2,14]{1,0:T(2,128)S(1)} %bitcast.12, s32[28]{0:T(128)S(1)} %copy-done.4, s32[2,14,128]{2,1,0:T(8,128)S(1)} %copy-done.2, f32[16,4,4,128]{3,2,1,0:T(4,128)S(1)} %all-to-all-done.1.back_ref), custom_call_target="tpu_custom_call" | custom-call | tf_op jit(solution)/shard_map/collect_velocity/pallas_call | solution.py:832
  (2 shorter events, 0.0 us)
Async XLA Ops:
  3.9 20.3 %all-to-all-start = ((f32[16,14,4,128]{3,2,1,0:T(4,128)}), f32[16,14,4,128]{3,2,1,0:T(4,128)S(1)}, u32[]{:S(2)}, u32[]{:S(2)}) async-start(f32[16,14,4,128]{3,2,1,0:T(4,128)} %get-tuple-element.20), calls=%async_computation | async-start | bytes 917504 | tf_op jit(solution)/shard_map/all_to_all | solution.py:848
  11.4 1.7 %copy-start = (f32[19,16,16,128]{3,2,1,0:T(8,128)S(1)}, f32[19,16,16,128]{3,2,1,0:T(8,128)}, u32[]{:S(2)}) copy-start(f32[19,16,16,128]{3,2,1,0:T(8,128)} %pop.1) | copy-start | bytes 7471108
  13.1 0.9 %copy-start.1 = (s32[16,16,128]{2,1,0:T(8,128)S(1)}, s32[16,16,128]{2,1,0:T(8,128)}, u32[]{:S(2)}) copy-start(s32[16,16,128]{2,1,0:T(8,128)} %solid.1) | copy-start | bytes 393220
  14.2 1.5 %copy-start.5 = (f32[19,16,16,128]{3,2,1,0:T(8,128)}, f32[19,16,16,128]{3,2,1,0:T(8,128)S(1)}, u32[]{:S(2)}) copy-start(f32[19,16,16,128]{3,2,1,0:T(8,128)S(1)} %get-tuple-element.21.base_ref) | copy-start | bytes 7471108
  24.2 1.7 %copy-start.6 = (f32[19,16,16,128]{3,2,1,0:T(8,128)S(1)}, f32[19,16,16,128]{3,2,1,0:T(8,128)}, u32[]{:S(2)}) copy-start(f32[19,16,16,128]{3,2,1,0:T(8,128)} %copy-done.5) | copy-start | bytes 7471108
  43.8 21.7 %all-to-all-start.1 = ((f32[16,4,4,128]{3,2,1,0:T(4,128)}), f32[16,4,4,128]{3,2,1,0:T(4,128)S(1)}, u32[]{:S(2)}, u32[]{:S(2)}) async-start(f32[16,4,4,128]{3,2,1,0:T(4,128)} %sample_velocity.1), calls=%async_computation.1 | async-start | bytes 262144 | tf_op jit(solution)/shard_map/all_to_all | solution.py:848
  48.3 3.9 %collective-permute-start = (f32[10,16,128]{2,1,0:T(8,128)S(1)}, f32[10,16,128]{2,1,0:T(8,128)S(1)}, u32[]{:S(2)}, u32[]{:S(2)}) collective-permute-start(f32[10,16,128]{2,1,0:T(8,128)S(1)} %get-tuple-element.24), channel_id=1, source_target_pairs={{0,16},{16,0},{1,17},{17,1},{2,18},{18,2},{3,19},{19,3},{4,20},{20... | collective-permute-start | bytes 245768 | tf_op jit(solution)/shard_map/ppermute | solution.py:844
  52.2 4.8 %collective-permute-start.1 = (f32[6,16,128]{2,1,0:T(8,128)S(1)}, f32[6,16,128]{2,1,0:T(8,128)S(1)}, u32[]{:S(2)}, u32[]{:S(2)}) collective-permute-start(f32[6,16,128]{2,1,0:T(8,128)S(1)} %get-tuple-element.27), channel_id=1, source_target_pairs={{0,4},{4,8},{8,12},{12,0},{1,5},{5,9},{9,13},{13,1},{2,6},{6,10},{... | collective-permute-start | bytes 147464 | tf_op jit(solution)/shard_map/ppermute | solution.py:844
  53.5 3.6 %collective-permute-start.2 = (f32[6,16,128]{2,1,0:T(8,128)S(1)}, f32[6,16,128]{2,1,0:T(8,128)S(1)}, u32[]{:S(2)}, u32[]{:S(2)}) collective-permute-start(f32[6,16,128]{2,1,0:T(8,128)S(1)} %get-tuple-element.28), channel_id=1, source_target_pairs={{0,12},{4,0},{8,4},{12,8},{1,13},{5,1},{9,5},{13,9},{2,14},{6,2},{... | collective-permute-start | bytes 147464 | tf_op jit(solution)/shard_map/ppermute | solution.py:844
  57.1 4.4 %collective-permute-start.3 = (f32[16,128]{1,0:T(8,128)S(1)}, f32[16,128]{1,0:T(8,128)S(1)}, u32[]{:S(2)}, u32[]{:S(2)}) collective-permute-start(f32[16,128]{1,0:T(8,128)S(1)} %get-tuple-element.31), channel_id=1, source_target_pairs={{0,1},{1,2},{2,3},{3,0},{4,5},{5,6},{6,7},{7,4},{8,9},{9,10},{10,1... | collective-permute-start | bytes 24584 | tf_op jit(solution)/shard_map/ppermute | solution.py:844
  60.7 3.1 %collective-permute-start.4 = (f32[16,128]{1,0:T(8,128)S(1)}, f32[16,128]{1,0:T(8,128)S(1)}, u32[]{:S(2)}, u32[]{:S(2)}) collective-permute-start(f32[16,128]{1,0:T(8,128)S(1)} %get-tuple-element.32), channel_id=1, source_target_pairs={{0,3},{1,0},{2,1},{3,2},{4,7},{5,4},{6,5},{7,6},{8,11},{9,8},{10,9... | collective-permute-start | bytes 24584 | tf_op jit(solution)/shard_map/ppermute | solution.py:844
  63.8 1.7 %copy-start.2 = (s32[2,14,128]{2,1,0:T(8,128)S(1)}, s32[2,14,128]{2,1,0:T(8,128)}, u32[]{:S(2)}) copy-start(s32[2,14,128]{2,1,0:T(8,128)} %get-tuple-element.34.rank_ref) | copy-start | bytes 43012
  63.8 1.7 %copy-start.3 = (s32[14,2]{0,1:T(2,128)S(1)}, s32[14,2]{0,1:T(2,128)}, u32[]{:S(2)}) copy-start(s32[14,2]{0,1:T(2,128)} %param.13) | copy-start | bytes 340
  63.8 1.7 %copy-start.4 = (s32[28]{0:T(128)S(1)}, s32[28]{0:T(128)}, u32[]{:S(2)}) copy-start(s32[28]{0:T(128)} %get-tuple-element.33.base_ref) | copy-start | bytes 340
where the time goes:
time: 67.4 us; the launch traced here: 66.9 us
  Pallas kernels  24.5 us (36%)
  starting transfers between devices  19.5 us (29%)
  waiting for transfers between devices  16.3 us (24%)
  local copies, waits for them, and re-layouts  5.86 us (9%)
  between operations  0.72 us (1%)
    all_to_all x2, starting transfers between devices, exchanged(): lax.all_to_all(value, ('gy', 'gz'), split_axis=0, concat_axis=0, tiled=True)  11.9 us
    pallas_call x1, Pallas kernels, collide(): pl.pallas_call(collide_kernel, out_shape=(jax.ShapeDtypeStruct(base.shape...  11.2 us
    all_to_all x2, waiting for transfers between devices, exchanged(): lax.all_to_all(value, ('gy', 'gz'), split_axis=0, concat_axis=0, tiled=True)  8.55 us
    ppermute x5, waiting for transfers between devices, shifted(): lax.ppermute(value, axis, [(i, (i + step) % count) for i in range(count)])  7.74 us
    ppermute x5, starting transfers between devices, shifted(): lax.ppermute(value, axis, [(i, (i + step) % count) for i in range(count)])  7.64 us
    pallas_call x1, Pallas kernels, sample(): pl.pallas_call(functools.partial(sample_kernel, extent), out_shape=jax.Sh...  6.61 us
    unnamed x14, local copies, waits for them, and re-layouts  5.77 us
    pallas_call x1, Pallas kernels, build_lists(): pl.pallas_call(kernel, out_shape=(jax.ShapeDtypeStruct((bricks, 2 * GROUP...  3.31 us
  transfers between devices with their start and end apart: 7, of which 5 were waited for; matrix products, arithmetic and copies ran while one was open for 0% of the time, Pallas kernels for 3%

commit v1 on v0

--- a/solution.py
+++ b/solution.py
@@ -347,40 +347,51 @@
     return [block_rows(table_ref, 2 * step + oo, j) for oo in range(2) for j in range(2)]
 
 
-def settle_kernel(pop, solid, base_ref, fluid_ref):
-    keep = 1.0 - 1.0 / RELAXATION
-
-    @pl.loop(0, solid.shape[0], unroll=2)
-    def _(x):
-        wall = solid[x] == 1
-        fluid_ref[x] = jnp.where(wall, 0.0, 1.0)
-        base_ref[0, x] = jnp.where(wall, pop[0, x], keep * pop[0, x])
-        for q in range(1, 19, 2):
-            one, two = pop[q, x], pop[q + 1, x]
-            base_ref[q, x] = jnp.where(wall, two, keep * one)
-            base_ref[q + 1, x] = jnp.where(wall, one, keep * two)
-
-
-def settle(populations, solid):
+def spread_kernel(extent, place_ref, table_ref, total, packed, spot_ref, *scratch):
+    owners, _, _, verts = table_ref.shape
+    build, product = spread_tools(place_ref, extent, verts, total, *scratch)
+    steps = owners // 2
+    total[...] = jnp.zeros(total.shape, F32)
+    pack_far(table_ref, packed, spot_ref)
+    build(pair_blocks(table_ref, 0), 0)
+
+    @pl.loop(0, steps // 2)
+    def _(i):
+        build(pair_blocks(table_ref, 2 * i + 1), 1)
+        product(0)
+        build(pair_blocks(table_ref, jnp.minimum(2 * i + 2, steps - 1)), 0)
+        product(1)
+
+    @pl.loop(0, packed_blocks(spot_ref[2 * owners], verts))
+    def _(block):
+        build([packed_rows(packed, block)], 0)
+        product(0, 1)
+
+
+def spread(place, table, extent):
+    owners, _, _, verts = table.shape
+    size_x, size_y, size_z = extent
+    cross = size_x * size_y
     return pl.pallas_call(
-        settle_kernel,
+        functools.partial(spread_kernel, extent),
         out_shape=(
-            jax.ShapeDtypeStruct(populations.shape, F32),
-            jax.ShapeDtypeStruct(solid.shape, F32),
+            jax.ShapeDtypeStruct((3 * size_z, cross), F32),
+            jax.ShapeDtypeStruct((2 * owners + 1, 16, verts), F32),
+            jax.ShapeDtypeStruct((2 * owners + 1,), jnp.int32),
         ),
-        in_specs=[vmem(), vmem()],
-        out_specs=(vmem(), vmem()),
-        compiler_params=settings(12),
-        cost_estimate=cost(16 * MIB, 8 * MIB),
-        name="settle",
-    )(populations, solid)
+        in_specs=[smem(), vmem()],
+        out_specs=(vmem(), vmem(), smem()),
+        scratch_shapes=spread_scratch(extent, verts),
+        compiler_params=settings(16),
+        cost_estimate=cost(6 * owners * 3 * size_z * cross * 4 * verts, MIB),
+        name="spread",
+    )(place, table)
 
 
 def collide_kernel(
-    place_ref,
-    table_ref,
-    base_ref,
-    fluid_ref,
+    total,
+    pop,
+    solid,
     post,
     xface_ref,
     yfp_ref,
@@ -388,33 +399,9 @@
     zfp_ref,
     zfm_ref,
     unit_ref,
-    packed,
-    spot_ref,
-    total,
     field,
-    *scratch,
 ):
     _, size_x, size_y, size_z = post.shape
-    owners, _, _, verts = table_ref.shape
-    build, product = spread_tools(
-        place_ref, (size_x, size_y, size_z), verts, total, *scratch
-    )
-    steps = owners // 2
-    total[...] = jnp.zeros(total.shape, F32)
-    pack_far(table_ref, packed, spot_ref)
-    build(pair_blocks(table_ref, 0), 0)
-
-    @pl.loop(0, steps // 2)
-    def _(i):
-        build(pair_blocks(table_ref, 2 * i + 1), 1)
-        product(0)
-        build(pair_blocks(table_ref, jnp.minimum(2 * i + 2, steps - 1)), 0)
-        product(1)
-
-    @pl.loop(0, packed_blocks(spot_ref[2 * owners], verts))
-    def _(block):
-        build([packed_rows(packed, block)], 0)
-        product(0, 1)
 
     for c in range(3):
         for half in range(size_x * size_y // 128):
@@ -431,8 +418,8 @@
         z_out = dict(zip((1, -1), z_out))
         lines = pl.ds(pl.multiple_of(x * 16, 16), 16)
         force = [field[c, lines, :] for c in range(3)]
-        fluid = fluid_ref[x]
-        cells = [base_ref[q, x] for q in range(19)]
+        cells = [pop[q, x] for q in range(19)]
+        wall = solid[x] == 1
         rho = cells[0]
         for q in range(1, 19):
             rho = rho + cells[q]
@@ -446,11 +433,8 @@
                         term = -term
                     value = term if value is None else value + term
             moment.append(value)
-        rho = rho * jnp.where(fluid > 0.0, 1.0 / keep, 1.0)
-        sign = jnp.where(fluid > 0.0, 1.0 / keep, -1.0)
         inverse = 1.0 / rho
-        rho = rho * fluid
-        vel = [(moment[c] * sign + 0.5 * force[c]) * inverse for c in range(3)]
+        vel = [(moment[c] + 0.5 * force[c]) * inverse for c in range(3)]
         for c in range(3):
             high, low = halves(vel[c])
             first = pl.ds(pl.multiple_of((x * 3 + c) * 16, 16), 16)
@@ -458,13 +442,13 @@
             unit_ref[first, size_z : 2 * size_z] = low.astype(BF)
         speed = vel[0] * vel[0] + vel[1] * vel[1] + vel[2] * vel[2]
         u_dot_f = vel[0] * force[0] + vel[1] * force[1] + vel[2] * force[2]
-        three = (3.0 * factor) * fluid
-        nine = (9.0 * factor) * fluid
+        three = 3.0 * factor
+        nine = 9.0 * factor
         rest = (rate * rho) * (1.0 - 1.5 * speed) - three * u_dot_f
         quad = (4.5 * rate) * rho
         linear = (3.0 * rate) * rho
         results = [None] * 19
-        results[0] = cells[0] + LATTICE_WEIGHTS[0] * rest
+        results[0] = jnp.where(wall, cells[0], keep * cells[0] + LATTICE_WEIGHTS[0] * rest)
 
         def along(vector, q):
             value = None
@@ -484,8 +468,8 @@
             weight = LATTICE_WEIGHTS[q]
             even = weight * (rest + a * (quad * a + nine * b))
             odd = weight * (linear * a + three * b)
-            results[q] = cells[q] + (even + odd)
-            results[q + 1] = cells[q + 1] + (even - odd)
+            results[q] = jnp.where(wall, cells[q + 1], keep * cells[q] + (even + odd))
+            results[q + 1] = jnp.where(wall, cells[q], keep * cells[q + 1] + (even - odd))
         for q in range(19):
             post[q, x] = results[q]
         for sign, line, face in ((1, size_y - 1, yfp_ref), (-1, 0, yfm_ref)):
@@ -506,36 +490,29 @@
         xface_ref[5 + k] = post[q, 0]
 
 
-def collide(place, table, base, fluid):
-    _, size_x, size_y, size_z = base.shape
-    owners, _, _, verts = table.shape
+def collide(total, populations, solid):
+    _, size_x, size_y, size_z = populations.shape
     cross = size_x * size_y
     face_y = jax.ShapeDtypeStruct((5, size_x, size_z), F32)
     face_z = jax.ShapeDtypeStruct((size_y, size_z), F32)
     return pl.pallas_call(
         collide_kernel,
         out_shape=(
-            jax.ShapeDtypeStruct(base.shape, F32),
+            jax.ShapeDtypeStruct(populations.shape, F32),
             jax.ShapeDtypeStruct((10, size_y, size_z), F32),
             face_y,
             face_y,
             face_z,
             face_z,
             jax.ShapeDtypeStruct((cross * 3, 2 * size_z), BF),
-            jax.ShapeDtypeStruct((2 * owners + 1, 16, verts), F32),
-            jax.ShapeDtypeStruct((2 * owners + 1,), jnp.int32),
         ),
-        in_specs=[smem()] + [vmem()] * 3,
-        out_specs=(vmem(),) * 8 + (smem(),),
-        scratch_shapes=[
-            pltpu.VMEM((3 * size_z, cross), F32),
-            pltpu.VMEM((3, cross, size_z), F32),
-        ]
-        + spread_scratch((size_x, size_y, size_z), verts),
-        compiler_params=settings(24),
-        cost_estimate=cost(6 * owners * 3 * size_z * cross * 4 * verts, 6 * MIB),
-        name="spread_collide",
-    )(place, table, base, fluid)
+        in_specs=[vmem()] * 3,
+        out_specs=(vmem(),) * 7,
+        scratch_shapes=[pltpu.VMEM((3, cross, size_z), F32)],
+        compiler_params=settings(12),
+        cost_estimate=cost(16 * MIB, 8 * MIB),
+        name="collide",
+    )(total, populations, solid)
 
 
 def sample_scratch(extent, verts):
@@ -621,27 +598,64 @@
     return xr_ref[(0 if sign > 0 else 5) + X_LISTS[sign].index(q)]
 
 
-def sample_kernel(extent, place_ref, spot_ref, table_ref, packed, unit_ref, out_ref, found, *scratch):
-    owners, _, _, verts = table_ref.shape
-    prepare, product, select, work = sample_tools(place_ref, unit_ref, extent, verts, *scratch)
-    steps = owners // 2
-    out_ref[...] = jnp.zeros(out_ref.shape, F32)
-
+def sample_steps(table_ref, first, last, prepare, work, out_ref):
     def store(step):
         def put(j, values):
             for c in range(3):
-                out_ref[2 * step + j // 2, j % 2, c : c + 1, :] = values[c]
+                line = j % 2
+                out_ref[2 * (step - first) + j // 2, c, line : line + 1, :] = values[c]
 
         return put
 
-    prepare(pair_blocks(table_ref, 0), 0)
-
-    @pl.loop(0, steps // 2)
+    prepare(pair_blocks(table_ref, first), 0)
+
+    @pl.loop(0, (last - first) // 2)
     def _(i):
-        prepare(pair_blocks(table_ref, 2 * i + 1), 1)
-        work(0, store(2 * i))
-        prepare(pair_blocks(table_ref, jnp.minimum(2 * i + 2, steps - 1)), 0)
-        work(1, store(2 * i + 1))
+        step = first + 2 * i
+        prepare(pair_blocks(table_ref, step + 1), 1)
+        work(0, store(step))
+        prepare(pair_blocks(table_ref, jnp.minimum(step + 2, last - 1)), 0)
+        work(1, store(step + 1))
+
+
+def sample_part_kernel(extent, first, last, place_ref, table_ref, unit_ref, *refs):
+    out_ref, scratch = refs[-5], refs[-4:]
+    verts = table_ref.shape[3]
+    prepare, _, _, work = sample_tools(place_ref, unit_ref, extent, verts, *scratch)
+    sample_steps(table_ref, first, last, prepare, work, out_ref)
+
+
+def sample_part(place, table, unit, order, first, last, extent):
+    owners, _, _, verts = table.shape
+    size_x, size_y, size_z = extent
+    return pl.pallas_call(
+        functools.partial(sample_part_kernel, extent, first, last),
+        out_shape=jax.ShapeDtypeStruct((2 * (last - first), 3, 2, verts), F32),
+        in_specs=[smem(), vmem(), vmem()] + [pl.BlockSpec(memory_space=pl.ANY)] * len(order),
+        out_specs=vmem(),
+        scratch_shapes=sample_scratch(extent, verts),
+        compiler_params=settings(12),
+        cost_estimate=cost(
+            32 * (last - first) * 3 * size_x * size_y * size_z * verts, MIB
+        ),
+        name="sample_part",
+    )(place, table, unit, *order)
+
+
+def sample_kernel(
+    extent, place_ref, spot_ref, table_ref, packed, unit_ref, one_ref, two_ref, *refs
+):
+    out_ref, found, scratch = refs[-6], refs[-5], refs[-4:]
+    owners, _, _, verts = table_ref.shape
+    prepare, product, select, work = sample_tools(place_ref, unit_ref, extent, verts, *scratch)
+    middle = one_ref.shape[0]
+    done = middle + two_ref.shape[0]
+    for c in range(3):
+        out_ref[0:middle, c, 0:2] = one_ref[:, c]
+        out_ref[middle:done, c, 0:2] = two_ref[:, c]
+        out_ref[:, c, 2:4] = jnp.zeros((owners, 2, verts), F32)
+    rest = out_ref.at[pl.ds(done, owners - done)]
+    sample_steps(table_ref, done // 2, owners // 2, prepare, work, rest)
 
     @pl.loop(0, packed_blocks(spot_ref[2 * owners], verts))
     def _(block):
@@ -664,23 +678,26 @@
                 first = pltpu.roll(found[block, 0:4], back, 1)
                 second = pltpu.roll(found[block + 1, 0:4], back, 1)
                 value = jnp.where(lane < verts - shift, first, second)
-                out_ref[owner, 2 + j, 0:3, :] = value[0:3]
-
-
-def sample(place, spots, table, packed, unit, extent):
+                for c in range(3):
+                    out_ref[owner, c, 2 + j : 3 + j, :] = value[c : c + 1]
+
+
+def sample(place, spots, table, packed, unit, parts, order, extent):
     owners, _, _, verts = table.shape
     size_x, size_y, size_z = extent
     return pl.pallas_call(
         functools.partial(sample_kernel, extent),
-        out_shape=jax.ShapeDtypeStruct((owners, SLOT_CAP, 4, verts), F32),
-        in_specs=[smem(), smem()] + [vmem()] * 3,
+        out_shape=jax.ShapeDtypeStruct((owners, 3, SLOT_CAP, verts), F32),
+        in_specs=[smem(), smem()]
+        + [vmem()] * 5
+        + [pl.BlockSpec(memory_space=pl.ANY)] * len(order),
         out_specs=vmem(),
         scratch_shapes=[pltpu.VMEM((2 * owners + 2, 8, verts), F32)]
         + sample_scratch(extent, verts),
         compiler_params=settings(12),
-        cost_estimate=cost(16 * owners * 3 * size_x * size_y * size_z * verts, MIB),
+        cost_estimate=cost(8 * owners * 3 * size_x * size_y * size_z * verts, MIB),
         name="sample_velocity",
-    )(place, spots, table, packed, unit)
+    )(place, spots, table, packed, unit, *parts, *order)
 
 
 def y_message_kernel(xr_ref, yfp_ref, yfm_ref, plus_ref, minus_ref):
@@ -809,21 +826,23 @@
 
 def collect_kernel(inter_ref, base_ref, rank_ref, back_ref, out_ref):
     patches, verts = rank_ref.shape[1:]
+    line = lax.broadcasted_iota(jnp.int32, (16, verts), 0) & (SLOT_CAP - 1)
     for p in range(patches):
         value = None
         for i in range(2):
             brick = inter_ref[i, p]
             base = base_ref[2 * p + i]
             rank = jnp.broadcast_to(rank_ref[i, p : p + 1, :], (8, verts))
-            spot = rank + base
-            block = lax.shift_right_logical(base, 7)
-            other = jnp.minimum(block + 1, SLOT_CAP - 1)
-            both = jnp.concatenate([back_ref[brick, block], back_ref[brick, other]], axis=0)
-            picked = jnp.take_along_axis(both, spot & (verts - 1), axis=1)
-            here = lax.shift_right_arithmetic(spot, 7)[0:3] == block
-            picked = jnp.where(here, picked[0:3], picked[4:7])
-            picked = jnp.where(rank[0:3] >= 0, picked, 0.0)
+            spot = jnp.concatenate([rank + base] * 2, axis=0)
+            rows = [back_ref[brick, c] for c in range(3)] + [jnp.zeros((4, verts), F32)]
+            picked = jnp.concatenate(rows, axis=0)
+            picked = jnp.take_along_axis(picked, spot & (verts - 1), axis=1)
+            here = lax.shift_right_logical(spot, 7) == line
+            picked = jnp.where(here & (jnp.concatenate([rank] * 2, axis=0) >= 0), picked, 0.0)
             value = picked if value is None else value + picked
+        value = value + pltpu.roll(value, 15, 0)
+        value = value + pltpu.roll(value, 14, 0)
+        value = jnp.concatenate([value[4 * c : 4 * c + 1] for c in range(3)], axis=0)
         out_ref[:, p, :] = value
 
 
@@ -870,9 +889,9 @@
         extent,
     )
     table = exchanged(outgoing)
-    base, fluid = settle(populations, solid_flags)
-    post, x_face, y_plus, y_minus, z_plus, z_minus, unit, packed, spots = collide(
-        place, table, base, fluid
+    total, packed, spots = spread(place, table, extent)
+    post, x_face, y_plus, y_minus, z_plus, z_minus, unit = collide(
+        total, populations, solid_flags
     )
     if lax.axis_size("gx") == 2:
         x_halo = shifted(x_face, "gx", 1)
@@ -880,11 +899,15 @@
         x_halo = jnp.concatenate(
             [shifted(x_face[:5], "gx", 1), shifted(x_face[5:], "gx", -1)], axis=0
         )
-    sampled = sample(place, spots, table, packed, unit, extent)
-    back = exchanged(sampled)
+    steps = table.shape[0] // 2
+    one = sample_part(place, table, unit, (), 0, steps // 4, extent)
     y_plus, y_minus = y_messages(x_halo, y_plus, y_minus)
     y_plus = shifted(y_plus, "gy", 1)
     y_minus = shifted(y_minus, "gy", -1)
+    two = sample_part(place, table, unit, (x_halo,), steps // 4, steps // 4 * 3, extent)
+    order = (y_plus, y_minus)
+    sampled = sample(place, spots, table, packed, unit, (one, two), order, extent)
+    back = exchanged(sampled)
     z_plus, z_minus = z_messages(x_halo, y_plus, y_minus, z_plus, z_minus)
     z_plus = shifted(z_plus, "gz", 1)
     z_minus = shifted(z_minus, "gz", -1)

time: 67.4 us -> 63.9 us (0.948)
  the two profiles are of different devices: /device:TPU:1 before, /device:TPU:0 now
where the time goes in v1:
time: 63.9 us; the launch traced here: 63.8 us
  Pallas kernels  24.3 us (38%)
  starting transfers between devices  20.2 us (32%)
  waiting for transfers between devices  18.3 us (29%)
  between operations  0.76 us (1%)
    all_to_all x2, waiting for transfers between devices, exchanged(): lax.all_to_all(value, ('gy', 'gz'), split_axis=0, concat_axis=0, tiled=True)  15.5 us
    all_to_all x2, starting transfers between devices, exchanged(): lax.all_to_all(value, ('gy', 'gz'), split_axis=0, concat_axis=0, tiled=True)  12.5 us
    pallas_call x1, Pallas kernels, spread(): pl.pallas_call(functools.partial(spread_kernel, extent), out_shape=(jax.S...  8.66 us
    ppermute x5, starting transfers between devices, shifted(): lax.ppermute(value, axis, [(i, (i + step) % count) for i in range(count)])  7.78 us
    pallas_call x2, Pallas kernels, sample_part(): pl.pallas_call(functools.partial(sample_part_kernel, extent, first, last)...  4.4 us
    pallas_call x1, Pallas kernels, build_lists(): pl.pallas_call(kernel, out_shape=(jax.ShapeDtypeStruct((bricks, 2 * GROUP...  3.31 us
    ppermute x5, waiting for transfers between devices, shifted(): lax.ppermute(value, axis, [(i, (i + step) % count) for i in range(count)])  2.82 us
    pallas_call x1, Pallas kernels, sample(): pl.pallas_call(functools.partial(sample_kernel, extent), out_shape=jax.Sh...  2.69 us
  transfers between devices with their start and end apart: 7, of which 4 were waited for; matrix products, arithmetic and copies ran while one was open for 0% of the time, Pallas kernels for 10%

profile of v1, /device:TPU:0, one launch (start us, length us, event | category | flops | bytes accessed | tf_op | source)
XLA Modules:
  0.0 63.8 jit_solution(1326231392418935239)
XLA Ops:
  0.6 3.3 %vertex_lists.1 = (f32[16,14,4,128]{3,2,1,0:T(4,128)}, s32[2,14,128]{2,1,0:T(8,128)}, s32[28]{0:T(128)}) custom-call(s32[2,14]{1,0:T(2,128)} %bitcast.11, f32[3,14,128]{2,1,0:T(8,128)} %bitcast.13, f32[3,14,128]{2,1,0:T(8,128)} %bitcast.14, s32[3,14,128]{2,1,0:T(8,128)} %bitcast.15, f32[14,8,128]{2,1,0:T(8,128)} %refs_4_.1), custom_call_target="tpu_custom_call" | custom-call | tf_op jit(solution)/shard_map/vertex_lists/pallas_call | solution.py:174
  3.9 7.4 %all-to-all-start = ((f32[16,14,4,128]{3,2,1,0:T(4,128)}), f32[16,14,4,128]{3,2,1,0:T(4,128)S(1)}, u32[]{:S(2)}, u32[]{:S(2)}) async-start(f32[16,14,4,128]{3,2,1,0:T(4,128)} %get-tuple-element.19), calls=%async_computation | async-start | bytes 917504 | tf_op jit(solution)/shard_map/all_to_all | solution.py:867
  11.3 0.1 stack.27.place_ref
  11.4 0.0 copy-start.1
  11.4 13.1 %all-to-all-done.table_ref = f32[16,14,4,128]{3,2,1,0:T(4,128)S(1)} async-done(((f32[16,14,4,128]{3,2,1,0:T(4,128)}), f32[16,14,4,128]{3,2,1,0:T(4,128)S(1)}, u32[]{:S(2)}, u32[]{:S(2)}) %all-to-all-start) | async-done | bytes 458784 | tf_op jit(solution)/shard_map/all_to_all | solution.py:867
  24.6 0.0 copy-start
  24.6 8.7 %spread.1 = (f32[384,256]{1,0:T(8,128)S(1)}, f32[33,16,128]{2,1,0:T(8,128)S(1)}, s32[33]{0:T(128)S(1)}) custom-call(s32[9]{0:T(128)S(1)} %stack.27.place_ref, f32[16,14,4,128]{3,2,1,0:T(4,128)S(1)} %all-to-all-done.table_ref), custom_call_target="tpu_custom_call" | custom-call | flops 4831838208 | bytes 1048576 | tf_op jit(solution)/shard_map/spread/pallas_call | solution.py:375
  33.2 0.0 copy-done.1
  33.2 0.0 copy-done
  33.3 2.1 %collide.1 = (f32[19,16,16,128]{3,2,1,0:T(8,128)S(1)}, f32[10,16,128]{2,1,0:T(8,128)S(1)}, f32[5,16,128]{2,1,0:T(8,128)S(1)}, f32[5,16,128]{2,1,0:T(8,128)S(1)},...) custom-call(f32[384,256]{1,0:T(8,128)S(1)} %get-tuple-element.20.total, ...), custom_call_target="tpu_custom_call" | custom-call | flops 16777216 | bytes 8388608 | tf_op jit(solution)/shard_map/collide/pallas_call | solution.py:498
  35.4 2.1 %collective-permute-start = (f32[10,16,128]{2,1,0:T(8,128)S(1)}, f32[10,16,128]{2,1,0:T(8,128)S(1)}, u32[]{:S(2)}, u32[]{:S(2)}) collective-permute-start(f32[10,16,128]{2,1,0:T(8,128)S(1)} %get-tuple-element.22), channel_id=1, source_target_pairs={{0,16},{16,0},{1,17},{17,1},{2,18},{18,2},{3,19},{19,3},{4,20},{20... | collective-permute-start | bytes 245768 | tf_op jit(solution)/shard_map/ppermute | solution.py:863
  37.5 1.7 %sample_part.2.one_ref = f32[4,3,2,128]{3,2,1,0:T(2,128)S(1)} custom-call(s32[9]{0:T(128)S(1)} %stack.27.place_ref, f32[16,14,4,128]{3,2,1,0:T(4,128)S(1)} %all-to-all-done.table_ref, bf16[768,256]{1,0:T(8,128)(2,1)S(1)} %get-tuple-element.35.unit_ref), custom_call_target="tpu_custom_call" | custom-call | flops 805306368 | bytes 1048576 | tf_op jit(solution)/shard_map/sample_part/pallas_call | solution.py:631
  39.2 1.3 %collective-permute-done.xr_ref.refs_0_ = f32[10,16,128]{2,1,0:T(8,128)S(1)} collective-permute-done((f32[10,16,128]{2,1,0:T(8,128)S(1)}, f32[10,16,128]{2,1,0:T(8,128)S(1)}, u32[]{:S(2)}, u32[]{:S(2)}) %collective-permute-start) | collective-permute-done | bytes 81952 | tf_op jit(solution)/shard_map/ppermute | solution.py:863
  40.5 0.9 %collective-permute-start.1 = (f32[6,16,128]{2,1,0:T(8,128)S(1)}, f32[6,16,128]{2,1,0:T(8,128)S(1)}, u32[]{:S(2)}, u32[]{:S(2)}) collective-permute-start(f32[6,16,128]{2,1,0:T(8,128)S(1)} %get-tuple-element.25), channel_id=1, source_target_pairs={{0,4},{4,8},{8,12},{12,0},{1,5},{5,9},{9,13},{13,1},{2,6},{6,10},{... | collective-permute-start | bytes 147464 | tf_op jit(solution)/shard_map/ppermute | solution.py:863
  41.5 3.0 %collective-permute-start.2 = (f32[6,16,128]{2,1,0:T(8,128)S(1)}, f32[6,16,128]{2,1,0:T(8,128)S(1)}, u32[]{:S(2)}, u32[]{:S(2)}) collective-permute-start(f32[6,16,128]{2,1,0:T(8,128)S(1)} %get-tuple-element.26), channel_id=1, source_target_pairs={{0,12},{4,0},{8,4},{12,8},{1,13},{5,1},{9,5},{13,9},{2,14},{6,2},{... | collective-permute-start | bytes 147464 | tf_op jit(solution)/shard_map/ppermute | solution.py:863
  44.4 2.7 %sample_part.3.two_ref = f32[8,3,2,128]{3,2,1,0:T(2,128)S(1)} custom-call(s32[9]{0:T(128)S(1)} %stack.27.place_ref, f32[16,14,4,128]{3,2,1,0:T(4,128)S(1)} %all-to-all-done.table_ref, bf16[768,256]{1,0:T(8,128)(2,1)S(1)} %get-tuple-element.35.unit_ref, f32[10,16,128]{2,1,0:T(8,128)S(1)} %collective-permute-done.xr_ref.refs_0_), custom_call_target="tpu_custom_call" | custom-call | flops 1610612736 | bytes 1048576 | tf_op jit(solution)/shard_map/sample_part/pallas_call | solution.py:631
  47.2 0.0 collective-permute-done.1.yrp_ref.refs_0_
  47.2 0.0 collective-permute-done.2.yrm_ref.refs_1_
  47.2 2.7 %sample_velocity.1 = f32[16,3,4,128]{3,2,1,0:T(4,128)} custom-call(s32[9]{0:T(128)S(1)} %stack.27.place_ref, s32[33]{0:T(128)S(1)} %get-tuple-element.33.spot_ref, f32[16,14,4,128]{3,2,1,0:T(4,128)S(1)} %all-to-all-done.table_ref, f32[33,16,128]{2,1,0:T(8,128)S(1)} %get-tuple-element.34.packed, bf16[768,256]{1,0:T(8,128)(2,1)S(1)} %get-tuple-element.35.unit_ref, ...), custom_call_target="tpu_custom_call" | custom-call | flops 1610612736 | bytes 1048576 | tf_op jit(solution)/shard_map/sample_velocity/pallas_call | solution.py:688
  49.9 5.1 %all-to-all-start.1 = ((f32[16,3,4,128]{3,2,1,0:T(4,128)}), f32[16,3,4,128]{3,2,1,0:T(4,128)S(1)}, u32[]{:S(2)}, u32[]{:S(2)}) async-start(f32[16,3,4,128]{3,2,1,0:T(4,128)} %sample_velocity.1), calls=%async_computation.1 | async-start | bytes 196608 | tf_op jit(solution)/shard_map/all_to_all | solution.py:867
  55.0 0.1 z_messages.1
  55.1 0.5 collective-permute-start.3
  55.5 1.3 %collective-permute-start.4 = (f32[16,128]{1,0:T(8,128)S(1)}, f32[16,128]{1,0:T(8,128)S(1)}, u32[]{:S(2)}, u32[]{:S(2)}) collective-permute-start(f32[16,128]{1,0:T(8,128)S(1)} %get-tuple-element.30), channel_id=1, source_target_pairs={{0,3},{1,0},{2,1},{3,2},{4,7},{5,4},{6,5},{7,6},{8,11},{9,8},{10,9... | collective-permute-start | bytes 24584 | tf_op jit(solution)/shard_map/ppermute | solution.py:863
  56.8 1.5 %collective-permute-done.3.zrp_ref = f32[16,128]{1,0:T(8,128)S(1)} collective-permute-done((f32[16,128]{1,0:T(8,128)S(1)}, f32[16,128]{1,0:T(8,128)S(1)}, u32[]{:S(2)}, u32[]{:S(2)}) %collective-permute-start.3) | collective-permute-done | bytes 8224 | tf_op jit(solution)/shard_map/ppermute | solution.py:863
  58.3 0.0 collective-permute-done.4.zrm_ref
  58.3 0.0 copy-start.2
  58.3 0.0 copy-start.3
  58.3 0.0 copy-start.4
  58.3 1.7 %stream_populations.1 = f32[19,16,16,128]{3,2,1,0:T(8,128)} custom-call(f32[19,16,16,128]{3,2,1,0:T(8,128)S(1)} %get-tuple-element.21.post, f32[10,16,128]{2,1,0:T(8,128)S(1)} %collective-permute-done.xr_ref.refs_0_, f32[6,16,128]{2,1,0:T(8,128)S(1)} %collective-permute-done.1.yrp_ref.refs_0_, f32[6,16,128]{2,1,0:T(8,128)S(1)} %collective-permute-done.2.yrm_ref.refs_1_, ...), custom_call_target="tpu_custom_call" | custom-call | flops 1048576 | bytes 16777216 | tf_op jit(solution)/shard_map/stream_populations/pallas_call | solution.py:812
  60.0 2.4 %all-to-all-done.1.back_ref = f32[16,3,4,128]{3,2,1,0:T(4,128)S(1)} async-done(((f32[16,3,4,128]{3,2,1,0:T(4,128)}), f32[16,3,4,128]{3,2,1,0:T(4,128)S(1)}, u32[]{:S(2)}, u32[]{:S(2)}) %all-to-all-start.1) | async-done | bytes 98336 | tf_op jit(solution)/shard_map/all_to_all | solution.py:867
  62.4 0.0 copy-done.2
  62.4 0.0 copy-done.3
  62.4 0.0 copy-done.4
  62.4 1.4 %collect_velocity.1 = f32[3,14,128]{2,1,0:T(8,128)} custom-call(s32[2,14]{1,0:T(2,128)S(1)} %bitcast.12, s32[28]{0:T(128)S(1)} %copy-done.4, s32[2,14,128]{2,1,0:T(8,128)S(1)} %copy-done.2, f32[16,3,4,128]{3,2,1,0:T(4,128)S(1)} %all-to-all-done.1.back_ref), custom_call_target="tpu_custom_call" | custom-call | tf_op jit(solution)/shard_map/collect_velocity/pallas_call | solution.py:851
  (2 shorter events, 0.0 us)
Async XLA Ops:
  3.9 20.6 %all-to-all-start = ((f32[16,14,4,128]{3,2,1,0:T(4,128)}), f32[16,14,4,128]{3,2,1,0:T(4,128)S(1)}, u32[]{:S(2)}, u32[]{:S(2)}) async-start(f32[16,14,4,128]{3,2,1,0:T(4,128)} %get-tuple-element.19), calls=%async_computation | async-start | bytes 917504 | tf_op jit(solution)/shard_map/all_to_all | solution.py:867
  11.4 21.8 %copy-start.1 = (s32[16,16,128]{2,1,0:T(8,128)S(1)}, s32[16,16,128]{2,1,0:T(8,128)}, u32[]{:S(2)}) copy-start(s32[16,16,128]{2,1,0:T(8,128)} %solid.1) | copy-start | bytes 393220
  24.6 8.7 %copy-start = (f32[19,16,16,128]{3,2,1,0:T(8,128)S(1)}, f32[19,16,16,128]{3,2,1,0:T(8,128)}, u32[]{:S(2)}) copy-start(f32[19,16,16,128]{3,2,1,0:T(8,128)} %pop.1) | copy-start | bytes 7471108
  35.4 5.1 %collective-permute-start = (f32[10,16,128]{2,1,0:T(8,128)S(1)}, f32[10,16,128]{2,1,0:T(8,128)S(1)}, u32[]{:S(2)}, u32[]{:S(2)}) collective-permute-start(f32[10,16,128]{2,1,0:T(8,128)S(1)} %get-tuple-element.22), channel_id=1, source_target_pairs={{0,16},{16,0},{1,17},{17,1},{2,18},{18,2},{3,19},{19,3},{4,20},{20... | collective-permute-start | bytes 245768 | tf_op jit(solution)/shard_map/ppermute | solution.py:863
  40.5 6.6 %collective-permute-start.1 = (f32[6,16,128]{2,1,0:T(8,128)S(1)}, f32[6,16,128]{2,1,0:T(8,128)S(1)}, u32[]{:S(2)}, u32[]{:S(2)}) collective-permute-start(f32[6,16,128]{2,1,0:T(8,128)S(1)} %get-tuple-element.25), channel_id=1, source_target_pairs={{0,4},{4,8},{8,12},{12,0},{1,5},{5,9},{9,13},{13,1},{2,6},{6,10},{... | collective-permute-start | bytes 147464 | tf_op jit(solution)/shard_map/ppermute | solution.py:863
  41.5 5.7 %collective-permute-start.2 = (f32[6,16,128]{2,1,0:T(8,128)S(1)}, f32[6,16,128]{2,1,0:T(8,128)S(1)}, u32[]{:S(2)}, u32[]{:S(2)}) collective-permute-start(f32[6,16,128]{2,1,0:T(8,128)S(1)} %get-tuple-element.26), channel_id=1, source_target_pairs={{0,12},{4,0},{8,4},{12,8},{1,13},{5,1},{9,5},{13,9},{2,14},{6,2},{... | collective-permute-start | bytes 147464 | tf_op jit(solution)/shard_map/ppermute | solution.py:863
  49.9 12.5 %all-to-all-start.1 = ((f32[16,3,4,128]{3,2,1,0:T(4,128)}), f32[16,3,4,128]{3,2,1,0:T(4,128)S(1)}, u32[]{:S(2)}, u32[]{:S(2)}) async-start(f32[16,3,4,128]{3,2,1,0:T(4,128)} %sample_velocity.1), calls=%async_computation.1 | async-start | bytes 196608 | tf_op jit(solution)/shard_map/all_to_all | solution.py:867
  55.1 3.3 %collective-permute-start.3 = (f32[16,128]{1,0:T(8,128)S(1)}, f32[16,128]{1,0:T(8,128)S(1)}, u32[]{:S(2)}, u32[]{:S(2)}) collective-permute-start(f32[16,128]{1,0:T(8,128)S(1)} %get-tuple-element.29), channel_id=1, source_target_pairs={{0,1},{1,2},{2,3},{3,0},{4,5},{5,6},{6,7},{7,4},{8,9},{9,10},{10,1... | collective-permute-start | bytes 24584 | tf_op jit(solution)/shard_map/ppermute | solution.py:863
  55.5 2.8 %collective-permute-start.4 = (f32[16,128]{1,0:T(8,128)S(1)}, f32[16,128]{1,0:T(8,128)S(1)}, u32[]{:S(2)}, u32[]{:S(2)}) collective-permute-start(f32[16,128]{1,0:T(8,128)S(1)} %get-tuple-element.30), channel_id=1, source_target_pairs={{0,3},{1,0},{2,1},{3,2},{4,7},{5,4},{6,5},{7,6},{8,11},{9,8},{10,9... | collective-permute-start | bytes 24584 | tf_op jit(solution)/shard_map/ppermute | solution.py:863
  58.3 4.1 %copy-start.2 = (s32[2,14,128]{2,1,0:T(8,128)S(1)}, s32[2,14,128]{2,1,0:T(8,128)}, u32[]{:S(2)}) copy-start(s32[2,14,128]{2,1,0:T(8,128)} %get-tuple-element.32.rank_ref) | copy-start | bytes 43012
  58.3 4.1 %copy-start.3 = (s32[14,2]{0,1:T(2,128)S(1)}, s32[14,2]{0,1:T(2,128)}, u32[]{:S(2)}) copy-start(s32[14,2]{0,1:T(2,128)} %param.13) | copy-start | bytes 340
  58.3 4.1 %copy-start.4 = (s32[28]{0:T(128)S(1)}, s32[28]{0:T(128)}, u32[]{:S(2)}) copy-start(s32[28]{0:T(128)} %get-tuple-element.31.base_ref) | copy-start | bytes 340

commit v2 on v1

--- a/solution.py
+++ b/solution.py
@@ -200,35 +200,21 @@
     return weight, third[0:3], jnp.concatenate([third[3:4], last], axis=0)
 
 
-def pack_far(table_ref, packed, spot_ref):
-    owners, _, _, verts = table_ref.shape
-    packed[...] = jnp.zeros(packed.shape, F32)
+def pack_far(table_ref, packed, spot_ref, owner, spot):
+    verts = table_ref.shape[3]
     lane = lax.broadcasted_iota(jnp.int32, (16, verts), 1)
-    counts = []
-    for owner in range(owners):
-        for j in range(2):
-            held = (table_ref[owner, GROUPS + 3 * j + 2, 3:4, :] > 0.0).astype(F32)
-            counts.append(jnp.sum(held).astype(jnp.int32))
-    spot = jnp.int32(0)
-    for owner in range(owners):
-        for j in range(2):
-            count = counts[2 * owner + j]
-            spot_ref[2 * owner + j] = spot
-
-            @pl.when(count > 0)
-            def _(owner=owner, j=j, spot=spot):
-                weight, force, cells = block_rows(table_ref, owner, 2 + j)
-                rows = jnp.concatenate(
-                    [weight, force, cells, jnp.zeros((2, verts), F32)], axis=0
-                )
-                block = lax.shift_right_logical(spot, 7)
-                shift = spot & (verts - 1)
-                rows = pltpu.roll(rows, shift, 1)
-                packed[block] += jnp.where(lane >= shift, rows, 0.0)
-                packed[block + 1] += jnp.where(lane < shift, rows, 0.0)
-
-            spot = spot + count
-    spot_ref[2 * owners] = spot
+    for j in range(2):
+        weight, force, cells = block_rows(table_ref, owner, 2 + j)
+        held = (cells[0:1] > 0.0).astype(F32)
+        rows = jnp.concatenate([weight, force, cells, jnp.zeros((2, verts), F32)], axis=0)
+        spot_ref[2 * owner + j] = spot
+        block = lax.shift_right_logical(spot, 7)
+        shift = spot & (verts - 1)
+        rows = pltpu.roll(rows, shift, 1)
+        packed[block] += jnp.where(lane >= shift, rows, 0.0)
+        packed[block + 1] += jnp.where(lane < shift, rows, 0.0)
+        spot = spot + jnp.sum(held).astype(jnp.int32)
+    return spot
 
 
 def packed_blocks(spot, verts):
@@ -352,15 +338,21 @@
     build, product = spread_tools(place_ref, extent, verts, total, *scratch)
     steps = owners // 2
     total[...] = jnp.zeros(total.shape, F32)
-    pack_far(table_ref, packed, spot_ref)
+    packed[...] = jnp.zeros(packed.shape, F32)
     build(pair_blocks(table_ref, 0), 0)
 
-    @pl.loop(0, steps // 2)
-    def _(i):
+    def near(i, spot):
         build(pair_blocks(table_ref, 2 * i + 1), 1)
         product(0)
+        for owner in range(2):
+            spot = pack_far(table_ref, packed, spot_ref, 4 * i + owner, spot)
         build(pair_blocks(table_ref, jnp.minimum(2 * i + 2, steps - 1)), 0)
         product(1)
+        for owner in range(2, 4):
+            spot = pack_far(table_ref, packed, spot_ref, 4 * i + owner, spot)
+        return spot
+
+    spot_ref[2 * owners] = lax.fori_loop(0, steps // 2, near, jnp.int32(0))
 
     @pl.loop(0, packed_blocks(spot_ref[2 * owners], verts))
     def _(block):
@@ -376,7 +368,7 @@
         functools.partial(spread_kernel, extent),
         out_shape=(
             jax.ShapeDtypeStruct((3 * size_z, cross), F32),
-            jax.ShapeDtypeStruct((2 * owners + 1, 16, verts), F32),
+            jax.ShapeDtypeStruct((2 * owners + 2, 16, verts), F32),
             jax.ShapeDtypeStruct((2 * owners + 1,), jnp.int32),
         ),
         in_specs=[smem(), vmem()],
@@ -388,88 +380,105 @@
     )(place, table)
 
 
-def collide_kernel(
-    total,
-    pop,
-    solid,
-    post,
-    xface_ref,
-    yfp_ref,
-    yfm_ref,
-    zfp_ref,
-    zfm_ref,
-    unit_ref,
-    field,
-):
-    _, size_x, size_y, size_z = post.shape
-
+def along(vector, q):
+    value = None
+    for c in range(3):
+        move = VELOCITIES[q][c]
+        if move == 0:
+            continue
+        if value is None:
+            value = vector[c] if move > 0 else -vector[c]
+        else:
+            value = value + vector[c] if move > 0 else value - vector[c]
+    return value
+
+
+def collide_plane(x, force, pop, solid):
+    factor = 1.0 - 0.5 / RELAXATION
+    rate = 1.0 / RELAXATION
+    keep = 1.0 - rate
+    cells = [pop[q, x] for q in range(19)]
+    wall = solid[x] == 1
+    rho = cells[0]
+    for q in range(1, 19):
+        rho = rho + cells[q]
+    moment = []
+    for c in range(3):
+        value = None
+        for q in range(1, 19, 2):
+            if VELOCITIES[q][c] != 0:
+                term = cells[q] - cells[q + 1]
+                if VELOCITIES[q][c] < 0:
+                    term = -term
+                value = term if value is None else value + term
+        moment.append(value)
+    inverse = 1.0 / rho
+    vel = [(moment[c] + 0.5 * force[c]) * inverse for c in range(3)]
+    speed = vel[0] * vel[0] + vel[1] * vel[1] + vel[2] * vel[2]
+    u_dot_f = vel[0] * force[0] + vel[1] * force[1] + vel[2] * force[2]
+    three = 3.0 * factor
+    nine = 9.0 * factor
+    rest = (rate * rho) * (1.0 - 1.5 * speed) - three * u_dot_f
+    quad = (4.5 * rate) * rho
+    linear = (3.0 * rate) * rho
+    results = [None] * 19
+    results[0] = jnp.where(wall, cells[0], keep * cells[0] + LATTICE_WEIGHTS[0] * rest)
+
+    for q in range(1, 19, 2):
+        a = along(vel, q)
+        b = along(force, q)
+        weight = LATTICE_WEIGHTS[q]
+        even = weight * (rest + a * (quad * a + nine * b))
+        odd = weight * (linear * a + three * b)
+        results[q] = jnp.where(wall, cells[q + 1], keep * cells[q] + (even + odd))
+        results[q + 1] = jnp.where(wall, cells[q], keep * cells[q + 1] + (even - odd))
+    return results, vel
+
+
+def face_kernel(total, pop, solid, xface_ref, field):
+    size_x, size_y, size_z = solid.shape
     for c in range(3):
         for half in range(size_x * size_y // 128):
             field[c, half * 128 : (half + 1) * 128, :] = jnp.transpose(
                 total[c * size_z : (c + 1) * size_z, half * 128 : (half + 1) * 128]
             )
-
+    for x, first, sign in ((size_x - 1, 0, 1), (0, 5, -1)):
+        force = [field[c, x * size_y : (x + 1) * size_y, :] for c in range(3)]
+        results, _ = collide_plane(x, force, pop, solid)
+        for k, q in enumerate(X_LISTS[sign]):
+            xface_ref[first + k] = results[q]
+
+
+def x_faces(total, populations, solid):
+    _, size_x, size_y, size_z = populations.shape
+    return pl.pallas_call(
+        face_kernel,
+        out_shape=(
+            jax.ShapeDtypeStruct((10, size_y, size_z), F32),
+            jax.ShapeDtypeStruct((3, size_x * size_y, size_z), F32),
+        ),
+        in_specs=[vmem()] * 3,
+        out_specs=(vmem(),) * 2,
+        compiler_params=settings(12),
+        cost_estimate=cost(2 * MIB, MIB),
+        name="x_faces",
+    )(total, populations, solid)
+
+
+def collide_kernel(field, pop, solid, post, yfp_ref, yfm_ref, zfp_ref, zfm_ref, unit_ref):
+    _, size_x, size_y, size_z = post.shape
     lane = lax.broadcasted_iota(jnp.int32, (size_y, size_z), 1)
-    factor = 1.0 - 0.5 / RELAXATION
-    rate = 1.0 / RELAXATION
-    keep = 1.0 - rate
 
     def plane(x, z_out):
         z_out = dict(zip((1, -1), z_out))
         lines = pl.ds(pl.multiple_of(x * 16, 16), 16)
         force = [field[c, lines, :] for c in range(3)]
-        cells = [pop[q, x] for q in range(19)]
-        wall = solid[x] == 1
-        rho = cells[0]
-        for q in range(1, 19):
-            rho = rho + cells[q]
-        moment = []
-        for c in range(3):
-            value = None
-            for q in range(1, 19, 2):
-                if VELOCITIES[q][c] != 0:
-                    term = cells[q] - cells[q + 1]
-                    if VELOCITIES[q][c] < 0:
-                        term = -term
-                    value = term if value is None else value + term
-            moment.append(value)
-        inverse = 1.0 / rho
-        vel = [(moment[c] + 0.5 * force[c]) * inverse for c in range(3)]
+        results, vel = collide_plane(x, force, pop, solid)
         for c in range(3):
             high, low = halves(vel[c])
             first = pl.ds(pl.multiple_of((x * 3 + c) * 16, 16), 16)
             unit_ref[first, 0:size_z] = high.astype(BF)
             unit_ref[first, size_z : 2 * size_z] = low.astype(BF)
-        speed = vel[0] * vel[0] + vel[1] * vel[1] + vel[2] * vel[2]
-        u_dot_f = vel[0] * force[0] + vel[1] * force[1] + vel[2] * force[2]
-        three = 3.0 * factor
-        nine = 9.0 * factor
-        rest = (rate * rho) * (1.0 - 1.5 * speed) - three * u_dot_f
-        quad = (4.5 * rate) * rho
-        linear = (3.0 * rate) * rho
-        results = [None] * 19
-        results[0] = jnp.where(wall, cells[0], keep * cells[0] + LATTICE_WEIGHTS[0] * rest)
-
-        def along(vector, q):
-            value = None
-            for c in range(3):
-                move = VELOCITIES[q][c]
-                if move == 0:
-                    continue
-                if value is None:
-                    value = vector[c] if move > 0 else -vector[c]
-                else:
-                    value = value + vector[c] if move > 0 else value - vector[c]
-            return value
-
-        for q in range(1, 19, 2):
-            a = along(vel, q)
-            b = along(force, q)
-            weight = LATTICE_WEIGHTS[q]
-            even = weight * (rest + a * (quad * a + nine * b))
-            odd = weight * (linear * a + three * b)
-            results[q] = jnp.where(wall, cells[q + 1], keep * cells[q] + (even + odd))
-            results[q + 1] = jnp.where(wall, cells[q], keep * cells[q + 1] + (even - odd))
         for q in range(19):
             post[q, x] = results[q]
         for sign, line, face in ((1, size_y - 1, yfp_ref), (-1, 0, yfm_ref)):
@@ -484,35 +493,28 @@
 
     empty = jnp.zeros((size_y, size_z), F32)
     zfp_ref[...], zfm_ref[...] = lax.fori_loop(0, size_x, plane, (empty, empty), unroll=2)
-    for k, q in enumerate(X_LISTS[1]):
-        xface_ref[k] = post[q, size_x - 1]
-    for k, q in enumerate(X_LISTS[-1]):
-        xface_ref[5 + k] = post[q, 0]
-
-
-def collide(total, populations, solid):
+
+
+def collide(field, populations, solid):
     _, size_x, size_y, size_z = populations.shape
-    cross = size_x * size_y
     face_y = jax.ShapeDtypeStruct((5, size_x, size_z), F32)
     face_z = jax.ShapeDtypeStruct((size_y, size_z), F32)
     return pl.pallas_call(
         collide_kernel,
         out_shape=(
             jax.ShapeDtypeStruct(populations.shape, F32),
-            jax.ShapeDtypeStruct((10, size_y, size_z), F32),
             face_y,
             face_y,
             face_z,
             face_z,
-            jax.ShapeDtypeStruct((cross * 3, 2 * size_z), BF),
+            jax.ShapeDtypeStruct((size_x * size_y * 3, 2 * size_z), BF),
         ),
         in_specs=[vmem()] * 3,
-        out_specs=(vmem(),) * 7,
-        scratch_shapes=[pltpu.VMEM((3, cross, size_z), F32)],
+        out_specs=(vmem(),) * 6,
         compiler_params=settings(12),
         cost_estimate=cost(16 * MIB, 8 * MIB),
         name="collide",
-    )(total, populations, solid)
+    )(field, populations, solid)
 
 
 def sample_scratch(extent, verts):
@@ -598,14 +600,9 @@
     return xr_ref[(0 if sign > 0 else 5) + X_LISTS[sign].index(q)]
 
 
-def sample_steps(table_ref, first, last, prepare, work, out_ref):
+def sample_steps(table_ref, first, last, prepare, work, put):
     def store(step):
-        def put(j, values):
-            for c in range(3):
-                line = j % 2
-                out_ref[2 * (step - first) + j // 2, c, line : line + 1, :] = values[c]
-
-        return put
+        return lambda j, values: put(2 * step + j // 2, j % 2, values)
 
     prepare(pair_blocks(table_ref, first), 0)
 
@@ -622,7 +619,12 @@
     out_ref, scratch = refs[-5], refs[-4:]
     verts = table_ref.shape[3]
     prepare, _, _, work = sample_tools(place_ref, unit_ref, extent, verts, *scratch)
-    sample_steps(table_ref, first, last, prepare, work, out_ref)
+
+    def put(owner, line, values):
+        for c in range(3):
+            out_ref[owner - 2 * first, c, line : line + 1, :] = values[c]
+
+    sample_steps(table_ref, first, last, prepare, work, put)
 
 
 def sample_part(place, table, unit, order, first, last, extent):
@@ -643,19 +645,21 @@
 
 
 def sample_kernel(
-    extent, place_ref, spot_ref, table_ref, packed, unit_ref, one_ref, two_ref, *refs
+    extent, place_ref, spot_ref, table_ref, packed, unit_ref, part_ref, *refs
 ):
     out_ref, found, scratch = refs[-6], refs[-5], refs[-4:]
     owners, _, _, verts = table_ref.shape
     prepare, product, select, work = sample_tools(place_ref, unit_ref, extent, verts, *scratch)
-    middle = one_ref.shape[0]
-    done = middle + two_ref.shape[0]
+    done = part_ref.shape[0]
     for c in range(3):
-        out_ref[0:middle, c, 0:2] = one_ref[:, c]
-        out_ref[middle:done, c, 0:2] = two_ref[:, c]
+        out_ref[0:done, c, 0:2] = part_ref[:, c]
         out_ref[:, c, 2:4] = jnp.zeros((owners, 2, verts), F32)
-    rest = out_ref.at[pl.ds(done, owners - done)]
-    sample_steps(table_ref, done // 2, owners // 2, prepare, work, rest)
+
+    def put(owner, line, values):
+        for c in range(3):
+            out_ref[owner, c, line : line + 1, :] = values[c]
+
+    sample_steps(table_ref, done // 2, owners // 2, prepare, work, put)
 
     @pl.loop(0, packed_blocks(spot_ref[2 * owners], verts))
     def _(block):
@@ -682,14 +686,14 @@
                     out_ref[owner, c, 2 + j : 3 + j, :] = value[c : c + 1]
 
 
-def sample(place, spots, table, packed, unit, parts, order, extent):
+def sample(place, spots, table, packed, unit, part, order, extent):
     owners, _, _, verts = table.shape
     size_x, size_y, size_z = extent
     return pl.pallas_call(
         functools.partial(sample_kernel, extent),
         out_shape=jax.ShapeDtypeStruct((owners, 3, SLOT_CAP, verts), F32),
         in_specs=[smem(), smem()]
-        + [vmem()] * 5
+        + [vmem()] * 4
         + [pl.BlockSpec(memory_space=pl.ANY)] * len(order),
         out_specs=vmem(),
         scratch_shapes=[pltpu.VMEM((2 * owners + 2, 8, verts), F32)]
@@ -697,7 +701,7 @@
         compiler_params=settings(12),
         cost_estimate=cost(8 * owners * 3 * size_x * size_y * size_z * verts, MIB),
         name="sample_velocity",
-    )(place, spots, table, packed, unit, *parts, *order)
+    )(place, spots, table, packed, unit, part, *order)
 
 
 def y_message_kernel(xr_ref, yfp_ref, yfm_ref, plus_ref, minus_ref):
@@ -890,23 +894,21 @@
     )
     table = exchanged(outgoing)
     total, packed, spots = spread(place, table, extent)
-    post, x_face, y_plus, y_minus, z_plus, z_minus, unit = collide(
-        total, populations, solid_flags
-    )
+    x_face, field = x_faces(total, populations, solid_flags)
+    post, y_plus, y_minus, z_plus, z_minus, unit = collide(field, populations, solid_flags)
     if lax.axis_size("gx") == 2:
         x_halo = shifted(x_face, "gx", 1)
     else:
         x_halo = jnp.concatenate(
             [shifted(x_face[:5], "gx", 1), shifted(x_face[5:], "gx", -1)], axis=0
         )
-    steps = table.shape[0] // 2
-    one = sample_part(place, table, unit, (), 0, steps // 4, extent)
     y_plus, y_minus = y_messages(x_halo, y_plus, y_minus)
     y_plus = shifted(y_plus, "gy", 1)
     y_minus = shifted(y_minus, "gy", -1)
-    two = sample_part(place, table, unit, (x_halo,), steps // 4, steps // 4 * 3, extent)
+    steps = table.shape[0] // 2
+    part = sample_part(place, table, unit, (x_halo,), 0, steps // 4 * 3, extent)
     order = (y_plus, y_minus)
-    sampled = sample(place, spots, table, packed, unit, (one, two), order, extent)
+    sampled = sample(place, spots, table, packed, unit, part, order, extent)
     back = exchanged(sampled)
     z_plus, z_minus = z_messages(x_halo, y_plus, y_minus, z_plus, z_minus)
     z_plus = shifted(z_plus, "gz", 1)

time: 63.9 us -> 61.6 us (0.964)
  starting transfers between devices: 20.2 us -> 18.1 us
  local copies, waits for them, and re-layouts: 0.11 us -> 1.56 us
  waiting for transfers between devices: 18.3 us -> 16.9 us
  Pallas kernels: 24.3 us -> 23.4 us
    all_to_all x2, starting transfers between devices: 12.5 us -> 10.9 us  [exchanged(): lax.all_to_all(value, ('gy', 'gz'), split_axis=0, concat_axis=0, tiled=True)]
    unnamed x10 -> x14, local copies, waits for them, and re-layouts: 0.02 us -> 1.47 us
    ppermute x5, waiting for transfers between devices: 2.82 us -> 1.43 us  [shifted(): lax.ppermute(value, axis, [(i, (i + step) % count) for i in range(count)])]
    pallas_call x2 -> x1, Pallas kernels: 4.4 us -> 3.77 us  [sample_part(): pl.pallas_call(functools.partial(sample_part_kernel, extent, first, last)...]
  transfers between devices with their start and end apart: 7 -> 7, of which waited for: 4 -> 3; matrix products, arithmetic and copies ran while one was open for 0% -> 0% of each run, Pallas kernels for 10% -> 12%
where the time goes in v2:
time: 61.6 us; the launch traced here: 60.9 us
  Pallas kernels  23.4 us (38%)
  starting transfers between devices  18.1 us (29%)
  waiting for transfers between devices  16.9 us (27%)
  local copies, waits for them, and re-layouts  1.56 us (3%)
  between operations  0.79 us (1%)
    all_to_all x2, waiting for transfers between devices, exchanged(): lax.all_to_all(value, ('gy', 'gz'), split_axis=0, concat_axis=0, tiled=True)  15.5 us
    all_to_all x2, starting transfers between devices, exchanged(): lax.all_to_all(value, ('gy', 'gz'), split_axis=0, concat_axis=0, tiled=True)  10.9 us
    pallas_call x1, Pallas kernels, spread(): pl.pallas_call(functools.partial(spread_kernel, extent), out_shape=(jax.S...  8.39 us
    ppermute x5, starting transfers between devices, shifted(): lax.ppermute(value, axis, [(i, (i + step) % count) for i in range(count)])  7.26 us
    pallas_call x1, Pallas kernels, sample_part(): pl.pallas_call(functools.partial(sample_part_kernel, extent, first, last)...  3.77 us
    pallas_call x1, Pallas kernels, build_lists(): pl.pallas_call(kernel, out_shape=(jax.ShapeDtypeStruct((bricks, 2 * GROUP...  3.31 us
    pallas_call x1, Pallas kernels, sample(): pl.pallas_call(functools.partial(sample_kernel, extent), out_shape=jax.Sh...  2.68 us
    pallas_call x1, Pallas kernels, collide(): pl.pallas_call(collide_kernel, out_shape=(jax.ShapeDtypeStruct(population...  1.97 us
  transfers between devices with their start and end apart: 7, of which 3 were waited for; matrix products, arithmetic and copies ran while one was open for 0% of the time, Pallas kernels for 12%

profile of v2, /device:TPU:0, one launch (start us, length us, event | category | flops | bytes accessed | tf_op | source)
XLA Modules:
  0.0 60.9 jit_solution(2903049248224553978)
XLA Ops:
  0.6 3.3 %vertex_lists.1 = (f32[16,14,4,128]{3,2,1,0:T(4,128)}, s32[2,14,128]{2,1,0:T(8,128)}, s32[28]{0:T(128)}) custom-call(s32[2,14]{1,0:T(2,128)} %bitcast.11, f32[3,14,128]{2,1,0:T(8,128)} %bitcast.13, f32[3,14,128]{2,1,0:T(8,128)} %bitcast.14, s32[3,14,128]{2,1,0:T(8,128)} %bitcast.15, f32[14,8,128]{2,1,0:T(8,128)} %refs_4_.1), custom_call_target="tpu_custom_call" | custom-call | tf_op jit(solution)/shard_map/vertex_lists/pallas_call | solution.py:174
  3.9 7.4 %all-to-all-start = ((f32[16,14,4,128]{3,2,1,0:T(4,128)}), f32[16,14,4,128]{3,2,1,0:T(4,128)S(1)}, u32[]{:S(2)}, u32[]{:S(2)}) async-start(f32[16,14,4,128]{3,2,1,0:T(4,128)} %get-tuple-element.20), calls=%async_computation | async-start | bytes 917504 | tf_op jit(solution)/shard_map/all_to_all | solution.py:871
  11.3 0.1 stack.27.place_ref
  11.4 0.0 copy-start
  11.4 0.0 copy-start.3
  11.4 13.1 %all-to-all-done.table_ref = f32[16,14,4,128]{3,2,1,0:T(4,128)S(1)} async-done(((f32[16,14,4,128]{3,2,1,0:T(4,128)}), f32[16,14,4,128]{3,2,1,0:T(4,128)S(1)}, u32[]{:S(2)}, u32[]{:S(2)}) %all-to-all-start) | async-done | bytes 458784 | tf_op jit(solution)/shard_map/all_to_all | solution.py:871
  24.6 8.4 %spread.1 = (f32[384,256]{1,0:T(8,128)S(1)}, f32[34,16,128]{2,1,0:T(8,128)S(1)}, s32[33]{0:T(128)S(1)}) custom-call(s32[9]{0:T(128)S(1)} %stack.27.place_ref, f32[16,14,4,128]{3,2,1,0:T(4,128)S(1)} %all-to-all-done.table_ref), custom_call_target="tpu_custom_call" | custom-call | flops 4831838208 | bytes 1048576 | tf_op jit(solution)/shard_map/spread/pallas_call | solution.py:367
  33.0 0.0 copy-done
  33.0 0.0 copy-done.3
  33.0 0.2 x_faces.1
  33.2 1.6 %collective-permute-start = (f32[10,16,128]{2,1,0:T(8,128)S(1)}, f32[10,16,128]{2,1,0:T(8,128)S(1)}, u32[]{:S(2)}, u32[]{:S(2)}) collective-permute-start(f32[10,16,128]{2,1,0:T(8,128)S(1)} %get-tuple-element.24), channel_id=1, source_target_pairs={{0,16},{16,0},{1,17},{17,1},{2,18},{18,2},{3,19},{19,3},{4,20},{20... | collective-permute-start | bytes 245768 | tf_op jit(solution)/shard_map/ppermute | solution.py:867
  34.8 2.0 %collide.1 = (f32[19,16,16,128]{3,2,1,0:T(8,128)S(1)}, f32[5,16,128]{2,1,0:T(8,128)S(1)}, f32[5,16,128]{2,1,0:T(8,128)S(1)}, f32[16,128]{1,0:T(8,128)S(1)}, f32[...) custom-call(f32[3,256,128]{2,1,0:T(8,128)S(1)} %get-tuple-element.22.field, f32[19,16,16,128]{3,2,1,0:T(8,128)S(1)} %copy-done, ...), custom_call_target="tpu_custom_call" | custom-call | flops 16777216 | bytes 8388608 | tf_op jit(solution)/shard_map/collide/pallas_call | solution.py:502
  36.8 0.0 copy-start.1
  36.8 1.4 %copy-done.1 = f32[19,16,16,128]{3,2,1,0:T(8,128)} copy-done((f32[19,16,16,128]{3,2,1,0:T(8,128)}, f32[19,16,16,128]{3,2,1,0:T(8,128)S(1)}, u32[]{:S(2)}) %copy-start.1) | copy-done | bytes 2490392
  38.2 0.0 collective-permute-done.xr_ref.refs_0_
  38.2 1.4 %collective-permute-start.1 = (f32[6,16,128]{2,1,0:T(8,128)S(1)}, f32[6,16,128]{2,1,0:T(8,128)S(1)}, u32[]{:S(2)}, u32[]{:S(2)}) collective-permute-start(f32[6,16,128]{2,1,0:T(8,128)S(1)} %get-tuple-element.27), channel_id=1, source_target_pairs={{0,4},{4,8},{8,12},{12,0},{1,5},{5,9},{9,13},{13,1},{2,6},{6,10},{... | collective-permute-start | bytes 147464 | tf_op jit(solution)/shard_map/ppermute | solution.py:867
  39.7 2.4 %collective-permute-start.2 = (f32[6,16,128]{2,1,0:T(8,128)S(1)}, f32[6,16,128]{2,1,0:T(8,128)S(1)}, u32[]{:S(2)}, u32[]{:S(2)}) collective-permute-start(f32[6,16,128]{2,1,0:T(8,128)S(1)} %get-tuple-element.28), channel_id=1, source_target_pairs={{0,12},{4,0},{8,4},{12,8},{1,13},{5,1},{9,5},{13,9},{2,14},{6,2},{... | collective-permute-start | bytes 147464 | tf_op jit(solution)/shard_map/ppermute | solution.py:867
  42.1 3.8 %sample_part.1.part_ref = f32[12,3,2,128]{3,2,1,0:T(2,128)S(1)} custom-call(s32[9]{0:T(128)S(1)} %stack.27.place_ref, f32[16,14,4,128]{3,2,1,0:T(4,128)S(1)} %all-to-all-done.table_ref, bf16[768,256]{1,0:T(8,128)(2,1)S(1)} %get-tuple-element.37.unit_ref, f32[10,16,128]{2,1,0:T(8,128)S(1)} %collective-permute-done.xr_ref.refs_0_), custom_call_target="tpu_custom_call" | custom-call | flops 2415919104 | bytes 1048576 | tf_op jit(solution)/shard_map/sample_part/pallas_call | solution.py:633
  45.9 0.0 collective-permute-done.1.yrp_ref.refs_0_
  45.9 0.0 collective-permute-done.2.yrm_ref.refs_1_
  45.9 0.0 copy-start.2
  45.9 2.7 %sample_velocity.1 = f32[16,3,4,128]{3,2,1,0:T(4,128)} custom-call(s32[9]{0:T(128)S(1)} %stack.27.place_ref, s32[33]{0:T(128)S(1)} %get-tuple-element.35.spot_ref, f32[16,14,4,128]{3,2,1,0:T(4,128)S(1)} %all-to-all-done.table_ref, f32[34,16,128]{2,1,0:T(8,128)S(1)} %get-tuple-element.36.packed, bf16[768,256]{1,0:T(8,128)(2,1)S(1)} %get-tuple-element.37.unit_ref, ...), custom_call_target="tpu_custom_call" | custom-call | flops 1610612736 | bytes 1048576 | tf_op jit(solution)/shard_map/sample_velocity/pallas_call | solution.py:692
  48.6 3.5 %all-to-all-start.1 = ((f32[16,3,4,128]{3,2,1,0:T(4,128)}), f32[16,3,4,128]{3,2,1,0:T(4,128)S(1)}, u32[]{:S(2)}, u32[]{:S(2)}) async-start(f32[16,3,4,128]{3,2,1,0:T(4,128)} %sample_velocity.1), calls=%async_computation.1 | async-start | bytes 196608 | tf_op jit(solution)/shard_map/all_to_all | solution.py:871
  52.1 0.1 z_messages.1
  52.2 0.4 collective-permute-start.3
  52.6 1.4 %collective-permute-start.4 = (f32[16,128]{1,0:T(8,128)S(1)}, f32[16,128]{1,0:T(8,128)S(1)}, u32[]{:S(2)}, u32[]{:S(2)}) collective-permute-start(f32[16,128]{1,0:T(8,128)S(1)} %get-tuple-element.32), channel_id=1, source_target_pairs={{0,3},{1,0},{2,1},{3,2},{4,7},{5,4},{6,5},{7,6},{8,11},{9,8},{10,9... | collective-permute-start | bytes 24584 | tf_op jit(solution)/shard_map/ppermute | solution.py:867
  54.0 1.4 %collective-permute-done.3.zrp_ref = f32[16,128]{1,0:T(8,128)S(1)} collective-permute-done((f32[16,128]{1,0:T(8,128)S(1)}, f32[16,128]{1,0:T(8,128)S(1)}, u32[]{:S(2)}, u32[]{:S(2)}) %collective-permute-start.3) | collective-permute-done | bytes 8224 | tf_op jit(solution)/shard_map/ppermute | solution.py:867
  55.4 0.0 collective-permute-done.4.zrm_ref
  55.4 0.0 copy-done.2
  55.4 0.0 copy-start.4
  55.4 0.0 copy-start.5
  55.4 0.0 copy-start.6
  55.4 1.7 %stream_populations.1 = f32[19,16,16,128]{3,2,1,0:T(8,128)} custom-call(f32[19,16,16,128]{3,2,1,0:T(8,128)S(1)} %copy-done.2, f32[10,16,128]{2,1,0:T(8,128)S(1)} %collective-permute-done.xr_ref.refs_0_, f32[6,16,128]{2,1,0:T(8,128)S(1)} %collective-permute-done.1.yrp_ref.refs_0_, f32[6,16,128]{2,1,0:T(8,128)S(1)} %collective-permute-done.2.yrm_ref.refs_1_, ...), custom_call_target="tpu_custom_call" | custom-call | flops 1048576 | bytes 16777216 | tf_op jit(solution)/shard_map/stream_populations/pallas_call | solution.py:816
  57.1 2.4 %all-to-all-done.1.back_ref = f32[16,3,4,128]{3,2,1,0:T(4,128)S(1)} async-done(((f32[16,3,4,128]{3,2,1,0:T(4,128)}), f32[16,3,4,128]{3,2,1,0:T(4,128)S(1)}, u32[]{:S(2)}, u32[]{:S(2)}) %all-to-all-start.1) | async-done | bytes 98336 | tf_op jit(solution)/shard_map/all_to_all | solution.py:871
  59.5 0.0 copy-done.4
  59.5 0.0 copy-done.5
  59.5 0.0 copy-done.6
  59.5 1.4 %collect_velocity.1 = f32[3,14,128]{2,1,0:T(8,128)} custom-call(s32[2,14]{1,0:T(2,128)S(1)} %bitcast.12, s32[28]{0:T(128)S(1)} %copy-done.6, s32[2,14,128]{2,1,0:T(8,128)S(1)} %copy-done.4, f32[16,3,4,128]{3,2,1,0:T(4,128)S(1)} %all-to-all-done.1.back_ref), custom_call_target="tpu_custom_call" | custom-call | tf_op jit(solution)/shard_map/collect_velocity/pallas_call | solution.py:855
  (2 shorter events, 0.0 us)
Async XLA Ops:
  3.9 20.6 %all-to-all-start = ((f32[16,14,4,128]{3,2,1,0:T(4,128)}), f32[16,14,4,128]{3,2,1,0:T(4,128)S(1)}, u32[]{:S(2)}, u32[]{:S(2)}) async-start(f32[16,14,4,128]{3,2,1,0:T(4,128)} %get-tuple-element.20), calls=%async_computation | async-start | bytes 917504 | tf_op jit(solution)/shard_map/all_to_all | solution.py:871
  11.4 21.5 %copy-start = (f32[19,16,16,128]{3,2,1,0:T(8,128)S(1)}, f32[19,16,16,128]{3,2,1,0:T(8,128)}, u32[]{:S(2)}) copy-start(f32[19,16,16,128]{3,2,1,0:T(8,128)} %pop.3) | copy-start | bytes 7471108
  11.4 21.6 %copy-start.3 = (s32[16,16,128]{2,1,0:T(8,128)S(1)}, s32[16,16,128]{2,1,0:T(8,128)}, u32[]{:S(2)}) copy-start(s32[16,16,128]{2,1,0:T(8,128)} %solid.3) | copy-start | bytes 393220
  33.2 5.0 %collective-permute-start = (f32[10,16,128]{2,1,0:T(8,128)S(1)}, f32[10,16,128]{2,1,0:T(8,128)S(1)}, u32[]{:S(2)}, u32[]{:S(2)}) collective-permute-start(f32[10,16,128]{2,1,0:T(8,128)S(1)} %get-tuple-element.24), channel_id=1, source_target_pairs={{0,16},{16,0},{1,17},{17,1},{2,18},{18,2},{3,19},{19,3},{4,20},{20... | collective-permute-start | bytes 245768 | tf_op jit(solution)/shard_map/ppermute | solution.py:867
  36.8 1.5 %copy-start.1 = (f32[19,16,16,128]{3,2,1,0:T(8,128)}, f32[19,16,16,128]{3,2,1,0:T(8,128)S(1)}, u32[]{:S(2)}) copy-start(f32[19,16,16,128]{3,2,1,0:T(8,128)S(1)} %get-tuple-element.23.post) | copy-start | bytes 7471108
  38.2 7.7 %collective-permute-start.1 = (f32[6,16,128]{2,1,0:T(8,128)S(1)}, f32[6,16,128]{2,1,0:T(8,128)S(1)}, u32[]{:S(2)}, u32[]{:S(2)}) collective-permute-start(f32[6,16,128]{2,1,0:T(8,128)S(1)} %get-tuple-element.27), channel_id=1, source_target_pairs={{0,4},{4,8},{8,12},{12,0},{1,5},{5,9},{9,13},{13,1},{2,6},{6,10},{... | collective-permute-start | bytes 147464 | tf_op jit(solution)/shard_map/ppermute | solution.py:867
  39.7 6.2 %collective-permute-start.2 = (f32[6,16,128]{2,1,0:T(8,128)S(1)}, f32[6,16,128]{2,1,0:T(8,128)S(1)}, u32[]{:S(2)}, u32[]{:S(2)}) collective-permute-start(f32[6,16,128]{2,1,0:T(8,128)S(1)} %get-tuple-element.28), channel_id=1, source_target_pairs={{0,12},{4,0},{8,4},{12,8},{1,13},{5,1},{9,5},{13,9},{2,14},{6,2},{... | collective-permute-start | bytes 147464 | tf_op jit(solution)/shard_map/ppermute | solution.py:867
  45.9 9.5 %copy-start.2 = (f32[19,16,16,128]{3,2,1,0:T(8,128)S(1)}, f32[19,16,16,128]{3,2,1,0:T(8,128)}, u32[]{:S(2)}) copy-start(f32[19,16,16,128]{3,2,1,0:T(8,128)} %copy-done.1) | copy-start | bytes 7471108
  48.6 10.9 %all-to-all-start.1 = ((f32[16,3,4,128]{3,2,1,0:T(4,128)}), f32[16,3,4,128]{3,2,1,0:T(4,128)S(1)}, u32[]{:S(2)}, u32[]{:S(2)}) async-start(f32[16,3,4,128]{3,2,1,0:T(4,128)} %sample_velocity.1), calls=%async_computation.1 | async-start | bytes 196608 | tf_op jit(solution)/shard_map/all_to_all | solution.py:871
  52.2 3.2 %collective-permute-start.3 = (f32[16,128]{1,0:T(8,128)S(1)}, f32[16,128]{1,0:T(8,128)S(1)}, u32[]{:S(2)}, u32[]{:S(2)}) collective-permute-start(f32[16,128]{1,0:T(8,128)S(1)} %get-tuple-element.31), channel_id=1, source_target_pairs={{0,1},{1,2},{2,3},{3,0},{4,5},{5,6},{6,7},{7,4},{8,9},{9,10},{10,1... | collective-permute-start | bytes 24584 | tf_op jit(solution)/shard_map/ppermute | solution.py:867
  52.6 2.8 %collective-permute-start.4 = (f32[16,128]{1,0:T(8,128)S(1)}, f32[16,128]{1,0:T(8,128)S(1)}, u32[]{:S(2)}, u32[]{:S(2)}) collective-permute-start(f32[16,128]{1,0:T(8,128)S(1)} %get-tuple-element.32), channel_id=1, source_target_pairs={{0,3},{1,0},{2,1},{3,2},{4,7},{5,4},{6,5},{7,6},{8,11},{9,8},{10,9... | collective-permute-start | bytes 24584 | tf_op jit(solution)/shard_map/ppermute | solution.py:867
  55.4 4.1 %copy-start.4 = (s32[2,14,128]{2,1,0:T(8,128)S(1)}, s32[2,14,128]{2,1,0:T(8,128)}, u32[]{:S(2)}) copy-start(s32[2,14,128]{2,1,0:T(8,128)} %get-tuple-element.34.rank_ref) | copy-start | bytes 43012
  55.4 4.1 %copy-start.5 = (s32[14,2]{0,1:T(2,128)S(1)}, s32[14,2]{0,1:T(2,128)}, u32[]{:S(2)}) copy-start(s32[14,2]{0,1:T(2,128)} %param.13) | copy-start | bytes 340
  55.4 4.1 %copy-start.6 = (s32[28]{0:T(128)S(1)}, s32[28]{0:T(128)}, u32[]{:S(2)}) copy-start(s32[28]{0:T(128)} %get-tuple-element.33.base_ref) | copy-start | bytes 340

commit v3 on v2

--- a/solution.py
+++ b/solution.py
@@ -375,7 +375,7 @@
         out_specs=(vmem(), vmem(), smem()),
         scratch_shapes=spread_scratch(extent, verts),
         compiler_params=settings(16),
-        cost_estimate=cost(6 * owners * 3 * size_z * cross * 4 * verts, MIB),
+        cost_estimate=cost(18 * owners * 3 * size_z * cross * 4 * verts, MIB),
         name="spread",
     )(place, table)
 

time: 61.6 us -> 61.4 us (level)
  no operation moved by 1% of the time
where the time goes in v3:
time: 61.4 us; the launch traced here: 60.9 us
  Pallas kernels  23.4 us (38%)
  starting transfers between devices  18.1 us (29%)
  waiting for transfers between devices  16.9 us (28%)
  local copies, waits for them, and re-layouts  1.56 us (3%)
  between operations  0.79 us (1%)
    all_to_all x2, waiting for transfers between devices, exchanged(): lax.all_to_all(value, ('gy', 'gz'), split_axis=0, concat_axis=0, tiled=True)  15.5 us
    all_to_all x2, starting transfers between devices, exchanged(): lax.all_to_all(value, ('gy', 'gz'), split_axis=0, concat_axis=0, tiled=True)  10.9 us
    pallas_call x1, Pallas kernels, spread(): pl.pallas_call(functools.partial(spread_kernel, extent), out_shape=(jax.S...  8.39 us
    ppermute x5, starting transfers between devices, shifted(): lax.ppermute(value, axis, [(i, (i + step) % count) for i in range(count)])  7.26 us
    pallas_call x1, Pallas kernels, sample_part(): pl.pallas_call(functools.partial(sample_part_kernel, extent, first, last)...  3.77 us
    pallas_call x1, Pallas kernels, build_lists(): pl.pallas_call(kernel, out_shape=(jax.ShapeDtypeStruct((bricks, 2 * GROUP...  3.31 us
    pallas_call x1, Pallas kernels, sample(): pl.pallas_call(functools.partial(sample_kernel, extent), out_shape=jax.Sh...  2.68 us
    pallas_call x1, Pallas kernels, collide(): pl.pallas_call(collide_kernel, out_shape=(jax.ShapeDtypeStruct(population...  1.97 us
  transfers between devices with their start and end apart: 7, of which 3 were waited for; matrix products, arithmetic and copies ran while one was open for 0% of the time, Pallas kernels for 12%

profile of v3, /device:TPU:0, one launch (start us, length us, event | category | flops | bytes accessed | tf_op | source)
XLA Modules:
  0.0 60.9 jit_solution(2903049248224553978)
XLA Ops:
  0.6 3.3 %vertex_lists.1 = (f32[16,14,4,128]{3,2,1,0:T(4,128)}, s32[2,14,128]{2,1,0:T(8,128)}, s32[28]{0:T(128)}) custom-call(s32[2,14]{1,0:T(2,128)} %bitcast.11, f32[3,14,128]{2,1,0:T(8,128)} %bitcast.13, f32[3,14,128]{2,1,0:T(8,128)} %bitcast.14, s32[3,14,128]{2,1,0:T(8,128)} %bitcast.15, f32[14,8,128]{2,1,0:T(8,128)} %refs_4_.1), custom_call_target="tpu_custom_call" | custom-call | tf_op jit(solution)/shard_map/vertex_lists/pallas_call | solution.py:174
  3.9 7.4 %all-to-all-start = ((f32[16,14,4,128]{3,2,1,0:T(4,128)}), f32[16,14,4,128]{3,2,1,0:T(4,128)S(1)}, u32[]{:S(2)}, u32[]{:S(2)}) async-start(f32[16,14,4,128]{3,2,1,0:T(4,128)} %get-tuple-element.20), calls=%async_computation | async-start | bytes 917504 | tf_op jit(solution)/shard_map/all_to_all | solution.py:871
  11.3 0.1 stack.27.place_ref
  11.4 0.0 copy-start
  11.4 0.0 copy-start.3
  11.4 13.1 %all-to-all-done.table_ref = f32[16,14,4,128]{3,2,1,0:T(4,128)S(1)} async-done(((f32[16,14,4,128]{3,2,1,0:T(4,128)}), f32[16,14,4,128]{3,2,1,0:T(4,128)S(1)}, u32[]{:S(2)}, u32[]{:S(2)}) %all-to-all-start) | async-done | bytes 458784 | tf_op jit(solution)/shard_map/all_to_all | solution.py:871
  24.6 8.4 %spread.1 = (f32[384,256]{1,0:T(8,128)S(1)}, f32[34,16,128]{2,1,0:T(8,128)S(1)}, s32[33]{0:T(128)S(1)}) custom-call(s32[9]{0:T(128)S(1)} %stack.27.place_ref, f32[16,14,4,128]{3,2,1,0:T(4,128)S(1)} %all-to-all-done.table_ref), custom_call_target="tpu_custom_call" | custom-call | flops 14495514624 | bytes 1048576 | tf_op jit(solution)/shard_map/spread/pallas_call | solution.py:367
  33.0 0.0 copy-done
  33.0 0.0 copy-done.3
  33.0 0.2 x_faces.1
  33.2 1.6 %collective-permute-start = (f32[10,16,128]{2,1,0:T(8,128)S(1)}, f32[10,16,128]{2,1,0:T(8,128)S(1)}, u32[]{:S(2)}, u32[]{:S(2)}) collective-permute-start(f32[10,16,128]{2,1,0:T(8,128)S(1)} %get-tuple-element.24), channel_id=1, source_target_pairs={{0,16},{16,0},{1,17},{17,1},{2,18},{18,2},{3,19},{19,3},{4,20},{20... | collective-permute-start | bytes 245768 | tf_op jit(solution)/shard_map/ppermute | solution.py:867
  34.8 2.0 %collide.1 = (f32[19,16,16,128]{3,2,1,0:T(8,128)S(1)}, f32[5,16,128]{2,1,0:T(8,128)S(1)}, f32[5,16,128]{2,1,0:T(8,128)S(1)}, f32[16,128]{1,0:T(8,128)S(1)}, f32[...) custom-call(f32[3,256,128]{2,1,0:T(8,128)S(1)} %get-tuple-element.22.field, f32[19,16,16,128]{3,2,1,0:T(8,128)S(1)} %copy-done, ...), custom_call_target="tpu_custom_call" | custom-call | flops 16777216 | bytes 8388608 | tf_op jit(solution)/shard_map/collide/pallas_call | solution.py:502
  36.8 0.0 copy-start.1
  36.8 1.4 %copy-done.1 = f32[19,16,16,128]{3,2,1,0:T(8,128)} copy-done((f32[19,16,16,128]{3,2,1,0:T(8,128)}, f32[19,16,16,128]{3,2,1,0:T(8,128)S(1)}, u32[]{:S(2)}) %copy-start.1) | copy-done | bytes 2490392
  38.2 0.0 collective-permute-done.xr_ref.refs_0_
  38.2 1.4 %collective-permute-start.1 = (f32[6,16,128]{2,1,0:T(8,128)S(1)}, f32[6,16,128]{2,1,0:T(8,128)S(1)}, u32[]{:S(2)}, u32[]{:S(2)}) collective-permute-start(f32[6,16,128]{2,1,0:T(8,128)S(1)} %get-tuple-element.27), channel_id=1, source_target_pairs={{0,4},{4,8},{8,12},{12,0},{1,5},{5,9},{9,13},{13,1},{2,6},{6,10},{... | collective-permute-start | bytes 147464 | tf_op jit(solution)/shard_map/ppermute | solution.py:867
  39.6 2.5 %collective-permute-start.2 = (f32[6,16,128]{2,1,0:T(8,128)S(1)}, f32[6,16,128]{2,1,0:T(8,128)S(1)}, u32[]{:S(2)}, u32[]{:S(2)}) collective-permute-start(f32[6,16,128]{2,1,0:T(8,128)S(1)} %get-tuple-element.28), channel_id=1, source_target_pairs={{0,12},{4,0},{8,4},{12,8},{1,13},{5,1},{9,5},{13,9},{2,14},{6,2},{... | collective-permute-start | bytes 147464 | tf_op jit(solution)/shard_map/ppermute | solution.py:867
  42.1 3.8 %sample_part.1.part_ref = f32[12,3,2,128]{3,2,1,0:T(2,128)S(1)} custom-call(s32[9]{0:T(128)S(1)} %stack.27.place_ref, f32[16,14,4,128]{3,2,1,0:T(4,128)S(1)} %all-to-all-done.table_ref, bf16[768,256]{1,0:T(8,128)(2,1)S(1)} %get-tuple-element.37.unit_ref, f32[10,16,128]{2,1,0:T(8,128)S(1)} %collective-permute-done.xr_ref.refs_0_), custom_call_target="tpu_custom_call" | custom-call | flops 2415919104 | bytes 1048576 | tf_op jit(solution)/shard_map/sample_part/pallas_call | solution.py:633
  45.9 0.0 collective-permute-done.1.yrp_ref.refs_0_
  45.9 0.0 collective-permute-done.2.yrm_ref.refs_1_
  45.9 0.0 copy-start.2
  45.9 2.7 %sample_velocity.1 = f32[16,3,4,128]{3,2,1,0:T(4,128)} custom-call(s32[9]{0:T(128)S(1)} %stack.27.place_ref, s32[33]{0:T(128)S(1)} %get-tuple-element.35.spot_ref, f32[16,14,4,128]{3,2,1,0:T(4,128)S(1)} %all-to-all-done.table_ref, f32[34,16,128]{2,1,0:T(8,128)S(1)} %get-tuple-element.36.packed, bf16[768,256]{1,0:T(8,128)(2,1)S(1)} %get-tuple-element.37.unit_ref, ...), custom_call_target="tpu_custom_call" | custom-call | flops 1610612736 | bytes 1048576 | tf_op jit(solution)/shard_map/sample_velocity/pallas_call | solution.py:692
  48.6 3.5 %all-to-all-start.1 = ((f32[16,3,4,128]{3,2,1,0:T(4,128)}), f32[16,3,4,128]{3,2,1,0:T(4,128)S(1)}, u32[]{:S(2)}, u32[]{:S(2)}) async-start(f32[16,3,4,128]{3,2,1,0:T(4,128)} %sample_velocity.1), calls=%async_computation.1 | async-start | bytes 196608 | tf_op jit(solution)/shard_map/all_to_all | solution.py:871
  52.1 0.1 z_messages.1
  52.2 0.4 collective-permute-start.3
  52.6 1.4 %collective-permute-start.4 = (f32[16,128]{1,0:T(8,128)S(1)}, f32[16,128]{1,0:T(8,128)S(1)}, u32[]{:S(2)}, u32[]{:S(2)}) collective-permute-start(f32[16,128]{1,0:T(8,128)S(1)} %get-tuple-element.32), channel_id=1, source_target_pairs={{0,3},{1,0},{2,1},{3,2},{4,7},{5,4},{6,5},{7,6},{8,11},{9,8},{10,9... | collective-permute-start | bytes 24584 | tf_op jit(solution)/shard_map/ppermute | solution.py:867
  54.0 1.4 %collective-permute-done.3.zrp_ref = f32[16,128]{1,0:T(8,128)S(1)} collective-permute-done((f32[16,128]{1,0:T(8,128)S(1)}, f32[16,128]{1,0:T(8,128)S(1)}, u32[]{:S(2)}, u32[]{:S(2)}) %collective-permute-start.3) | collective-permute-done | bytes 8224 | tf_op jit(solution)/shard_map/ppermute | solution.py:867
  55.4 0.0 collective-permute-done.4.zrm_ref
  55.4 0.0 copy-done.2
  55.4 0.0 copy-start.4
  55.4 0.0 copy-start.5
  55.4 0.0 copy-start.6
  55.4 1.7 %stream_populations.1 = f32[19,16,16,128]{3,2,1,0:T(8,128)} custom-call(f32[19,16,16,128]{3,2,1,0:T(8,128)S(1)} %copy-done.2, f32[10,16,128]{2,1,0:T(8,128)S(1)} %collective-permute-done.xr_ref.refs_0_, f32[6,16,128]{2,1,0:T(8,128)S(1)} %collective-permute-done.1.yrp_ref.refs_0_, f32[6,16,128]{2,1,0:T(8,128)S(1)} %collective-permute-done.2.yrm_ref.refs_1_, ...), custom_call_target="tpu_custom_call" | custom-call | flops 1048576 | bytes 16777216 | tf_op jit(solution)/shard_map/stream_populations/pallas_call | solution.py:816
  57.1 2.4 %all-to-all-done.1.back_ref = f32[16,3,4,128]{3,2,1,0:T(4,128)S(1)} async-done(((f32[16,3,4,128]{3,2,1,0:T(4,128)}), f32[16,3,4,128]{3,2,1,0:T(4,128)S(1)}, u32[]{:S(2)}, u32[]{:S(2)}) %all-to-all-start.1) | async-done | bytes 98336 | tf_op jit(solution)/shard_map/all_to_all | solution.py:871
  59.5 0.0 copy-done.4
  59.5 0.0 copy-done.5
  59.5 0.0 copy-done.6
  59.5 1.4 %collect_velocity.1 = f32[3,14,128]{2,1,0:T(8,128)} custom-call(s32[2,14]{1,0:T(2,128)S(1)} %bitcast.12, s32[28]{0:T(128)S(1)} %copy-done.6, s32[2,14,128]{2,1,0:T(8,128)S(1)} %copy-done.4, f32[16,3,4,128]{3,2,1,0:T(4,128)S(1)} %all-to-all-done.1.back_ref), custom_call_target="tpu_custom_call" | custom-call | tf_op jit(solution)/shard_map/collect_velocity/pallas_call | solution.py:855
  (2 shorter events, 0.0 us)
Async XLA Ops:
  3.9 20.6 %all-to-all-start = ((f32[16,14,4,128]{3,2,1,0:T(4,128)}), f32[16,14,4,128]{3,2,1,0:T(4,128)S(1)}, u32[]{:S(2)}, u32[]{:S(2)}) async-start(f32[16,14,4,128]{3,2,1,0:T(4,128)} %get-tuple-element.20), calls=%async_computation | async-start | bytes 917504 | tf_op jit(solution)/shard_map/all_to_all | solution.py:871
  11.4 21.5 %copy-start = (f32[19,16,16,128]{3,2,1,0:T(8,128)S(1)}, f32[19,16,16,128]{3,2,1,0:T(8,128)}, u32[]{:S(2)}) copy-start(f32[19,16,16,128]{3,2,1,0:T(8,128)} %pop.3) | copy-start | bytes 7471108
  11.4 21.6 %copy-start.3 = (s32[16,16,128]{2,1,0:T(8,128)S(1)}, s32[16,16,128]{2,1,0:T(8,128)}, u32[]{:S(2)}) copy-start(s32[16,16,128]{2,1,0:T(8,128)} %solid.3) | copy-start | bytes 393220
  33.2 5.0 %collective-permute-start = (f32[10,16,128]{2,1,0:T(8,128)S(1)}, f32[10,16,128]{2,1,0:T(8,128)S(1)}, u32[]{:S(2)}, u32[]{:S(2)}) collective-permute-start(f32[10,16,128]{2,1,0:T(8,128)S(1)} %get-tuple-element.24), channel_id=1, source_target_pairs={{0,16},{16,0},{1,17},{17,1},{2,18},{18,2},{3,19},{19,3},{4,20},{20... | collective-permute-start | bytes 245768 | tf_op jit(solution)/shard_map/ppermute | solution.py:867
  36.8 1.5 %copy-start.1 = (f32[19,16,16,128]{3,2,1,0:T(8,128)}, f32[19,16,16,128]{3,2,1,0:T(8,128)S(1)}, u32[]{:S(2)}) copy-start(f32[19,16,16,128]{3,2,1,0:T(8,128)S(1)} %get-tuple-element.23.post) | copy-start | bytes 7471108
  38.2 7.7 %collective-permute-start.1 = (f32[6,16,128]{2,1,0:T(8,128)S(1)}, f32[6,16,128]{2,1,0:T(8,128)S(1)}, u32[]{:S(2)}, u32[]{:S(2)}) collective-permute-start(f32[6,16,128]{2,1,0:T(8,128)S(1)} %get-tuple-element.27), channel_id=1, source_target_pairs={{0,4},{4,8},{8,12},{12,0},{1,5},{5,9},{9,13},{13,1},{2,6},{6,10},{... | collective-permute-start | bytes 147464 | tf_op jit(solution)/shard_map/ppermute | solution.py:867
  39.6 6.3 %collective-permute-start.2 = (f32[6,16,128]{2,1,0:T(8,128)S(1)}, f32[6,16,128]{2,1,0:T(8,128)S(1)}, u32[]{:S(2)}, u32[]{:S(2)}) collective-permute-start(f32[6,16,128]{2,1,0:T(8,128)S(1)} %get-tuple-element.28), channel_id=1, source_target_pairs={{0,12},{4,0},{8,4},{12,8},{1,13},{5,1},{9,5},{13,9},{2,14},{6,2},{... | collective-permute-start | bytes 147464 | tf_op jit(solution)/shard_map/ppermute | solution.py:867
  45.9 9.5 %copy-start.2 = (f32[19,16,16,128]{3,2,1,0:T(8,128)S(1)}, f32[19,16,16,128]{3,2,1,0:T(8,128)}, u32[]{:S(2)}) copy-start(f32[19,16,16,128]{3,2,1,0:T(8,128)} %copy-done.1) | copy-start | bytes 7471108
  48.6 10.9 %all-to-all-start.1 = ((f32[16,3,4,128]{3,2,1,0:T(4,128)}), f32[16,3,4,128]{3,2,1,0:T(4,128)S(1)}, u32[]{:S(2)}, u32[]{:S(2)}) async-start(f32[16,3,4,128]{3,2,1,0:T(4,128)} %sample_velocity.1), calls=%async_computation.1 | async-start | bytes 196608 | tf_op jit(solution)/shard_map/all_to_all | solution.py:871
  52.2 3.2 %collective-permute-start.3 = (f32[16,128]{1,0:T(8,128)S(1)}, f32[16,128]{1,0:T(8,128)S(1)}, u32[]{:S(2)}, u32[]{:S(2)}) collective-permute-start(f32[16,128]{1,0:T(8,128)S(1)} %get-tuple-element.31), channel_id=1, source_target_pairs={{0,1},{1,2},{2,3},{3,0},{4,5},{5,6},{6,7},{7,4},{8,9},{9,10},{10,1... | collective-permute-start | bytes 24584 | tf_op jit(solution)/shard_map/ppermute | solution.py:867
  52.6 2.8 %collective-permute-start.4 = (f32[16,128]{1,0:T(8,128)S(1)}, f32[16,128]{1,0:T(8,128)S(1)}, u32[]{:S(2)}, u32[]{:S(2)}) collective-permute-start(f32[16,128]{1,0:T(8,128)S(1)} %get-tuple-element.32), channel_id=1, source_target_pairs={{0,3},{1,0},{2,1},{3,2},{4,7},{5,4},{6,5},{7,6},{8,11},{9,8},{10,9... | collective-permute-start | bytes 24584 | tf_op jit(solution)/shard_map/ppermute | solution.py:867
  55.4 4.1 %copy-start.4 = (s32[2,14,128]{2,1,0:T(8,128)S(1)}, s32[2,14,128]{2,1,0:T(8,128)}, u32[]{:S(2)}) copy-start(s32[2,14,128]{2,1,0:T(8,128)} %get-tuple-element.34.rank_ref) | copy-start | bytes 43012
  55.4 4.1 %copy-start.5 = (s32[14,2]{0,1:T(2,128)S(1)}, s32[14,2]{0,1:T(2,128)}, u32[]{:S(2)}) copy-start(s32[14,2]{0,1:T(2,128)} %param.13) | copy-start | bytes 340
  55.4 4.1 %copy-start.6 = (s32[28]{0:T(128)S(1)}, s32[28]{0:T(128)}, u32[]{:S(2)}) copy-start(s32[28]{0:T(128)} %get-tuple-element.33.base_ref) | copy-start | bytes 340

commit v4 on v3

--- a/solution.py
+++ b/solution.py
@@ -333,7 +333,20 @@
     return [block_rows(table_ref, 2 * step + oo, j) for oo in range(2) for j in range(2)]
 
 
-def spread_kernel(extent, place_ref, table_ref, total, packed, spot_ref, *scratch):
+def spread_kernel(
+    extent,
+    place_ref,
+    table_ref,
+    pop_any,
+    total,
+    packed,
+    spot_ref,
+    pop,
+    sem,
+    *scratch,
+):
+    load = pltpu.make_async_copy(pop_any, pop, sem)
+    load.start()
     owners, _, _, verts = table_ref.shape
     build, product = spread_tools(place_ref, extent, verts, total, *scratch)
     steps = owners // 2
@@ -359,10 +372,14 @@
         build([packed_rows(packed, block)], 0)
         product(0, 1)
 
-
-def spread(place, table, extent):
+    load.wait()
+
+
+def spread(place, table, populations):
     owners, _, _, verts = table.shape
+    extent = populations.shape[1:]
     size_x, size_y, size_z = extent
+    anyspace = pl.BlockSpec(memory_space=pl.ANY)
     cross = size_x * size_y
     return pl.pallas_call(
         functools.partial(spread_kernel, extent),
@@ -370,14 +387,15 @@
             jax.ShapeDtypeStruct((3 * size_z, cross), F32),
             jax.ShapeDtypeStruct((2 * owners + 2, 16, verts), F32),
             jax.ShapeDtypeStruct((2 * owners + 1,), jnp.int32),
+            jax.ShapeDtypeStruct(populations.shape, F32),
         ),
-        in_specs=[smem(), vmem()],
-        out_specs=(vmem(), vmem(), smem()),
-        scratch_shapes=spread_scratch(extent, verts),
-        compiler_params=settings(16),
+        in_specs=[smem(), vmem(), anyspace],
+        out_specs=(vmem(), vmem(), smem(), vmem()),
+        scratch_shapes=[pltpu.SemaphoreType.DMA] + spread_scratch(extent, verts),
+        compiler_params=settings(48),
         cost_estimate=cost(18 * owners * 3 * size_z * cross * 4 * verts, MIB),
         name="spread",
-    )(place, table)
+    )(place, table, populations)
 
 
 def along(vector, q):
@@ -893,7 +911,7 @@
         extent,
     )
     table = exchanged(outgoing)
-    total, packed, spots = spread(place, table, extent)
+    total, packed, spots, populations = spread(place, table, populations)
     x_face, field = x_faces(total, populations, solid_flags)
     post, y_plus, y_minus, z_plus, z_minus, unit = collide(field, populations, solid_flags)
     if lax.axis_size("gx") == 2:

time: 61.4 us -> 63.8 us (1.039)
  Pallas kernels: 23.4 us -> 24.9 us
  waiting for transfers between devices: 16.9 us -> 18 us
    ppermute x5, waiting for transfers between devices: 1.43 us -> 2.43 us  [shifted(): lax.ppermute(value, axis, [(i, (i + step) % count) for i in range(count)])]
    pallas_call x1, Pallas kernels: 8.39 us -> 9.14 us  [spread(): pl.pallas_call(functools.partial(spread_kernel, extent), out_shape=(jax.S...]
    pallas_call x1, Pallas kernels: 2.68 us -> 3.4 us  [sample(): pl.pallas_call(functools.partial(sample_kernel, extent), out_shape=jax.Sh...]
    unnamed x14 -> x10, local copies, waits for them, and re-layouts: 1.47 us -> 1.72 us
  transfers between devices with their start and end apart: 7 -> 7, of which waited for: 3 -> 4; matrix products, arithmetic and copies ran while one was open for 0% -> 0% of each run, Pallas kernels for 12% -> 12%
where the time goes in v4:
time: 63.8 us; the launch traced here: 63.7 us
  Pallas kernels  24.9 us (39%)
  starting transfers between devices  18.3 us (29%)
  waiting for transfers between devices  18 us (28%)
  local copies, waits for them, and re-layouts  1.81 us (3%)
  between operations  0.75 us (1%)
    all_to_all x2, waiting for transfers between devices, exchanged(): lax.all_to_all(value, ('gy', 'gz'), split_axis=0, concat_axis=0, tiled=True)  15.5 us
    all_to_all x2, starting transfers between devices, exchanged(): lax.all_to_all(value, ('gy', 'gz'), split_axis=0, concat_axis=0, tiled=True)  11 us
    pallas_call x1, Pallas kernels, spread(): pl.pallas_call(functools.partial(spread_kernel, extent), out_shape=(jax.S...  9.14 us
    ppermute x5, starting transfers between devices, shifted(): lax.ppermute(value, axis, [(i, (i + step) % count) for i in range(count)])  7.25 us
    pallas_call x1, Pallas kernels, sample_part(): pl.pallas_call(functools.partial(sample_part_kernel, extent, first, last)...  3.77 us
    pallas_call x1, Pallas kernels, sample(): pl.pallas_call(functools.partial(sample_kernel, extent), out_shape=jax.Sh...  3.4 us
    pallas_call x1, Pallas kernels, build_lists(): pl.pallas_call(kernel, out_shape=(jax.ShapeDtypeStruct((bricks, 2 * GROUP...  3.31 us
    ppermute x5, waiting for transfers between devices, shifted(): lax.ppermute(value, axis, [(i, (i + step) % count) for i in range(count)])  2.43 us
  transfers between devices with their start and end apart: 7, of which 4 were waited for; matrix products, arithmetic and copies ran while one was open for 0% of the time, Pallas kernels for 12%

profile of v4, /device:TPU:0, one launch (start us, length us, event | category | flops | bytes accessed | tf_op | source)
XLA Modules:
  0.0 63.7 jit_solution(12277361372981957347)
XLA Ops:
  0.6 3.3 %vertex_lists.1 = (f32[16,14,4,128]{3,2,1,0:T(4,128)}, s32[2,14,128]{2,1,0:T(8,128)}, s32[28]{0:T(128)}) custom-call(s32[2,14]{1,0:T(2,128)} %bitcast.11, f32[3,14,128]{2,1,0:T(8,128)} %bitcast.13, f32[3,14,128]{2,1,0:T(8,128)} %bitcast.14, s32[3,14,128]{2,1,0:T(8,128)} %bitcast.15, f32[14,8,128]{2,1,0:T(8,128)} %refs_4_.1), custom_call_target="tpu_custom_call" | custom-call | tf_op jit(solution)/shard_map/vertex_lists/pallas_call | solution.py:174
  3.9 7.4 %all-to-all-start = ((f32[16,14,4,128]{3,2,1,0:T(4,128)}), f32[16,14,4,128]{3,2,1,0:T(4,128)S(1)}, u32[]{:S(2)}, u32[]{:S(2)}) async-start(f32[16,14,4,128]{3,2,1,0:T(4,128)} %get-tuple-element.21), calls=%async_computation | async-start | bytes 917504 | tf_op jit(solution)/shard_map/all_to_all | solution.py:889
  11.3 0.1 stack.27.place_ref
  11.4 0.0 copy-start
  11.4 13.1 %all-to-all-done.table_ref = f32[16,14,4,128]{3,2,1,0:T(4,128)S(1)} async-done(((f32[16,14,4,128]{3,2,1,0:T(4,128)}), f32[16,14,4,128]{3,2,1,0:T(4,128)S(1)}, u32[]{:S(2)}, u32[]{:S(2)}) %all-to-all-start) | async-done | bytes 458784 | tf_op jit(solution)/shard_map/all_to_all | solution.py:889
  24.6 0.0 copy-start.4
  24.6 1.7 %copy-done.4 = f32[19,16,16,128]{3,2,1,0:T(8,128)S(1)} copy-done((f32[19,16,16,128]{3,2,1,0:T(8,128)S(1)}, f32[19,16,16,128]{3,2,1,0:T(8,128)}, u32[]{:S(2)}) %copy-start.4) | copy-done | bytes 2490392
  26.3 9.1 %spread.1 = (f32[384,256]{1,0:T(8,128)S(1)}, f32[34,16,128]{2,1,0:T(8,128)S(1)}, s32[33]{0:T(128)S(1)}, f32[19,16,16,128]{3,2,1,0:T(8,128)S(1)}) custom-call(s32[9]{0:T(128)S(1)} %stack.27.place_ref, f32[16,14,4,128]{3,2,1,0:T(4,128)S(1)} %all-to-all-done.table_ref, f32[19,16,16,128]{3,2,1,0:T(8,128)S(1)} %copy-done.4), custom_call_target="tpu_custom_call" | custom-call | flops 14495514624 | bytes 1048576 | tf_op jit(solution)/shard_map/spread/pallas_call | solution.py:384
  35.4 0.0 copy-done
  35.4 0.2 x_faces.1
  35.6 1.6 %collective-permute-start = (f32[10,16,128]{2,1,0:T(8,128)S(1)}, f32[10,16,128]{2,1,0:T(8,128)S(1)}, u32[]{:S(2)}, u32[]{:S(2)}) collective-permute-start(f32[10,16,128]{2,1,0:T(8,128)S(1)} %get-tuple-element.26), channel_id=1, source_target_pairs={{0,16},{16,0},{1,17},{17,1},{2,18},{18,2},{3,19},{19,3},{4,20},{20... | collective-permute-start | bytes 245768 | tf_op jit(solution)/shard_map/ppermute | solution.py:885
  37.2 2.0 %collide.1 = (f32[19,16,16,128]{3,2,1,0:T(8,128)S(1)}, f32[5,16,128]{2,1,0:T(8,128)S(1)}, f32[5,16,128]{2,1,0:T(8,128)S(1)}, f32[16,128]{1,0:T(8,128)S(1)}, f32[...) custom-call(f32[3,256,128]{2,1,0:T(8,128)S(1)} %get-tuple-element.24.field, ...), custom_call_target="tpu_custom_call" | custom-call | flops 16777216 | bytes 8388608 | tf_op jit(solution)/shard_map/collide/pallas_call | solution.py:520
  39.2 0.9 %collective-permute-done.xr_ref.refs_0_ = f32[10,16,128]{2,1,0:T(8,128)S(1)} collective-permute-done((f32[10,16,128]{2,1,0:T(8,128)S(1)}, f32[10,16,128]{2,1,0:T(8,128)S(1)}, u32[]{:S(2)}, u32[]{:S(2)}) %collective-permute-start) | collective-permute-done | bytes 81952 | tf_op jit(solution)/shard_map/ppermute | solution.py:885
  40.2 1.1 %collective-permute-start.1 = (f32[6,16,128]{2,1,0:T(8,128)S(1)}, f32[6,16,128]{2,1,0:T(8,128)S(1)}, u32[]{:S(2)}, u32[]{:S(2)}) collective-permute-start(f32[6,16,128]{2,1,0:T(8,128)S(1)} %get-tuple-element.29), channel_id=1, source_target_pairs={{0,4},{4,8},{8,12},{12,0},{1,5},{5,9},{9,13},{13,1},{2,6},{6,10},{... | collective-permute-start | bytes 147464 | tf_op jit(solution)/shard_map/ppermute | solution.py:885
  41.3 2.7 %collective-permute-start.2 = (f32[6,16,128]{2,1,0:T(8,128)S(1)}, f32[6,16,128]{2,1,0:T(8,128)S(1)}, u32[]{:S(2)}, u32[]{:S(2)}) collective-permute-start(f32[6,16,128]{2,1,0:T(8,128)S(1)} %get-tuple-element.30), channel_id=1, source_target_pairs={{0,12},{4,0},{8,4},{12,8},{1,13},{5,1},{9,5},{13,9},{2,14},{6,2},{... | collective-permute-start | bytes 147464 | tf_op jit(solution)/shard_map/ppermute | solution.py:885
  44.0 3.8 %sample_part.1.part_ref = f32[12,3,2,128]{3,2,1,0:T(2,128)S(1)} custom-call(s32[9]{0:T(128)S(1)} %stack.27.place_ref, f32[16,14,4,128]{3,2,1,0:T(4,128)S(1)} %all-to-all-done.table_ref, bf16[768,256]{1,0:T(8,128)(2,1)S(1)} %get-tuple-element.39.unit_ref, f32[10,16,128]{2,1,0:T(8,128)S(1)} %collective-permute-done.xr_ref.refs_0_), custom_call_target="tpu_custom_call" | custom-call | flops 2415919104 | bytes 1048576 | tf_op jit(solution)/shard_map/sample_part/pallas_call | solution.py:651
  47.8 0.0 collective-permute-done.1.yrp_ref.refs_0_
  47.8 0.0 collective-permute-done.2.yrm_ref.refs_1_
  47.8 3.4 %sample_velocity.1 = f32[16,3,4,128]{3,2,1,0:T(4,128)} custom-call(s32[9]{0:T(128)S(1)} %stack.27.place_ref, s32[33]{0:T(128)S(1)} %get-tuple-element.37.spot_ref, f32[16,14,4,128]{3,2,1,0:T(4,128)S(1)} %all-to-all-done.table_ref, f32[34,16,128]{2,1,0:T(8,128)S(1)} %get-tuple-element.38.packed, bf16[768,256]{1,0:T(8,128)(2,1)S(1)} %get-tuple-element.39.unit_ref, ...), custom_call_target="tpu_custom_call" | custom-call | flops 1610612736 | bytes 1048576 | tf_op jit(solution)/shard_map/sample_velocity/pallas_call | solution.py:710
  51.2 3.6 %all-to-all-start.1 = ((f32[16,3,4,128]{3,2,1,0:T(4,128)}), f32[16,3,4,128]{3,2,1,0:T(4,128)S(1)}, u32[]{:S(2)}, u32[]{:S(2)}) async-start(f32[16,3,4,128]{3,2,1,0:T(4,128)} %sample_velocity.1), calls=%async_computation.1 | async-start | bytes 196608 | tf_op jit(solution)/shard_map/all_to_all | solution.py:889
  54.9 0.1 z_messages.1
  55.0 0.5 collective-permute-start.3
  55.4 1.3 %collective-permute-start.4 = (f32[16,128]{1,0:T(8,128)S(1)}, f32[16,128]{1,0:T(8,128)S(1)}, u32[]{:S(2)}, u32[]{:S(2)}) collective-permute-start(f32[16,128]{1,0:T(8,128)S(1)} %get-tuple-element.34), channel_id=1, source_target_pairs={{0,3},{1,0},{2,1},{3,2},{4,7},{5,4},{6,5},{7,6},{8,11},{9,8},{10,9... | collective-permute-start | bytes 24584 | tf_op jit(solution)/shard_map/ppermute | solution.py:885
  56.8 1.5 %collective-permute-done.3.zrp_ref = f32[16,128]{1,0:T(8,128)S(1)} collective-permute-done((f32[16,128]{1,0:T(8,128)S(1)}, f32[16,128]{1,0:T(8,128)S(1)}, u32[]{:S(2)}, u32[]{:S(2)}) %collective-permute-start.3) | collective-permute-done | bytes 8224 | tf_op jit(solution)/shard_map/ppermute | solution.py:885
  58.2 0.0 collective-permute-done.4.zrm_ref
  58.2 0.0 copy-start.1
  58.2 0.0 copy-start.2
  58.2 0.0 copy-start.3
  58.2 1.7 %stream_populations.1 = f32[19,16,16,128]{3,2,1,0:T(8,128)} custom-call(f32[19,16,16,128]{3,2,1,0:T(8,128)S(1)} %get-tuple-element.25.post, f32[10,16,128]{2,1,0:T(8,128)S(1)} %collective-permute-done.xr_ref.refs_0_, f32[6,16,128]{2,1,0:T(8,128)S(1)} %collective-permute-done.1.yrp_ref.refs_0_, f32[6,16,128]{2,1,0:T(8,128)S(1)} %collective-permute-done.2.yrm_ref.refs_1_, ...), custom_call_target="tpu_custom_call" | custom-call | flops 1048576 | bytes 16777216 | tf_op jit(solution)/shard_map/stream_populations/pallas_call | solution.py:834
  59.9 2.4 %all-to-all-done.1.back_ref = f32[16,3,4,128]{3,2,1,0:T(4,128)S(1)} async-done(((f32[16,3,4,128]{3,2,1,0:T(4,128)}), f32[16,3,4,128]{3,2,1,0:T(4,128)S(1)}, u32[]{:S(2)}, u32[]{:S(2)}) %all-to-all-start.1) | async-done | bytes 98336 | tf_op jit(solution)/shard_map/all_to_all | solution.py:889
  62.3 0.0 copy-done.1
  62.3 0.0 copy-done.2
  62.3 0.0 copy-done.3
  62.3 1.4 %collect_velocity.1 = f32[3,14,128]{2,1,0:T(8,128)} custom-call(s32[2,14]{1,0:T(2,128)S(1)} %bitcast.12, s32[28]{0:T(128)S(1)} %copy-done.3, s32[2,14,128]{2,1,0:T(8,128)S(1)} %copy-done.1, f32[16,3,4,128]{3,2,1,0:T(4,128)S(1)} %all-to-all-done.1.back_ref), custom_call_target="tpu_custom_call" | custom-call | tf_op jit(solution)/shard_map/collect_velocity/pallas_call | solution.py:873
  (2 shorter events, 0.0 us)
Async XLA Ops:
  3.9 20.6 %all-to-all-start = ((f32[16,14,4,128]{3,2,1,0:T(4,128)}), f32[16,14,4,128]{3,2,1,0:T(4,128)S(1)}, u32[]{:S(2)}, u32[]{:S(2)}) async-start(f32[16,14,4,128]{3,2,1,0:T(4,128)} %get-tuple-element.21), calls=%async_computation | async-start | bytes 917504 | tf_op jit(solution)/shard_map/all_to_all | solution.py:889
  11.4 24.0 %copy-start = (s32[16,16,128]{2,1,0:T(8,128)S(1)}, s32[16,16,128]{2,1,0:T(8,128)}, u32[]{:S(2)}) copy-start(s32[16,16,128]{2,1,0:T(8,128)} %solid.3) | copy-start | bytes 393220
  24.6 1.7 %copy-start.4 = (f32[19,16,16,128]{3,2,1,0:T(8,128)S(1)}, f32[19,16,16,128]{3,2,1,0:T(8,128)}, u32[]{:S(2)}) copy-start(f32[19,16,16,128]{3,2,1,0:T(8,128)} %pop_any.1) | copy-start | bytes 7471108
  35.6 4.5 %collective-permute-start = (f32[10,16,128]{2,1,0:T(8,128)S(1)}, f32[10,16,128]{2,1,0:T(8,128)S(1)}, u32[]{:S(2)}, u32[]{:S(2)}) collective-permute-start(f32[10,16,128]{2,1,0:T(8,128)S(1)} %get-tuple-element.26), channel_id=1, source_target_pairs={{0,16},{16,0},{1,17},{17,1},{2,18},{18,2},{3,19},{19,3},{4,20},{20... | collective-permute-start | bytes 245768 | tf_op jit(solution)/shard_map/ppermute | solution.py:885
  40.2 7.7 %collective-permute-start.1 = (f32[6,16,128]{2,1,0:T(8,128)S(1)}, f32[6,16,128]{2,1,0:T(8,128)S(1)}, u32[]{:S(2)}, u32[]{:S(2)}) collective-permute-start(f32[6,16,128]{2,1,0:T(8,128)S(1)} %get-tuple-element.29), channel_id=1, source_target_pairs={{0,4},{4,8},{8,12},{12,0},{1,5},{5,9},{9,13},{13,1},{2,6},{6,10},{... | collective-permute-start | bytes 147464 | tf_op jit(solution)/shard_map/ppermute | solution.py:885
  41.3 6.5 %collective-permute-start.2 = (f32[6,16,128]{2,1,0:T(8,128)S(1)}, f32[6,16,128]{2,1,0:T(8,128)S(1)}, u32[]{:S(2)}, u32[]{:S(2)}) collective-permute-start(f32[6,16,128]{2,1,0:T(8,128)S(1)} %get-tuple-element.30), channel_id=1, source_target_pairs={{0,12},{4,0},{8,4},{12,8},{1,13},{5,1},{9,5},{13,9},{2,14},{6,2},{... | collective-permute-start | bytes 147464 | tf_op jit(solution)/shard_map/ppermute | solution.py:885
  51.2 11.1 %all-to-all-start.1 = ((f32[16,3,4,128]{3,2,1,0:T(4,128)}), f32[16,3,4,128]{3,2,1,0:T(4,128)S(1)}, u32[]{:S(2)}, u32[]{:S(2)}) async-start(f32[16,3,4,128]{3,2,1,0:T(4,128)} %sample_velocity.1), calls=%async_computation.1 | async-start | bytes 196608 | tf_op jit(solution)/shard_map/all_to_all | solution.py:889
  55.0 3.3 %collective-permute-start.3 = (f32[16,128]{1,0:T(8,128)S(1)}, f32[16,128]{1,0:T(8,128)S(1)}, u32[]{:S(2)}, u32[]{:S(2)}) collective-permute-start(f32[16,128]{1,0:T(8,128)S(1)} %get-tuple-element.33), channel_id=1, source_target_pairs={{0,1},{1,2},{2,3},{3,0},{4,5},{5,6},{6,7},{7,4},{8,9},{9,10},{10,1... | collective-permute-start | bytes 24584 | tf_op jit(solution)/shard_map/ppermute | solution.py:885
  55.4 2.8 %collective-permute-start.4 = (f32[16,128]{1,0:T(8,128)S(1)}, f32[16,128]{1,0:T(8,128)S(1)}, u32[]{:S(2)}, u32[]{:S(2)}) collective-permute-start(f32[16,128]{1,0:T(8,128)S(1)} %get-tuple-element.34), channel_id=1, source_target_pairs={{0,3},{1,0},{2,1},{3,2},{4,7},{5,4},{6,5},{7,6},{8,11},{9,8},{10,9... | collective-permute-start | bytes 24584 | tf_op jit(solution)/shard_map/ppermute | solution.py:885
  58.2 4.1 %copy-start.1 = (s32[2,14,128]{2,1,0:T(8,128)S(1)}, s32[2,14,128]{2,1,0:T(8,128)}, u32[]{:S(2)}) copy-start(s32[2,14,128]{2,1,0:T(8,128)} %get-tuple-element.36.rank_ref) | copy-start | bytes 43012
  58.2 4.1 %copy-start.2 = (s32[14,2]{0,1:T(2,128)S(1)}, s32[14,2]{0,1:T(2,128)}, u32[]{:S(2)}) copy-start(s32[14,2]{0,1:T(2,128)} %param.13) | copy-start | bytes 340
  58.2 4.1 %copy-start.3 = (s32[28]{0:T(128)S(1)}, s32[28]{0:T(128)}, u32[]{:S(2)}) copy-start(s32[28]{0:T(128)} %get-tuple-element.35.base_ref) | copy-start | bytes 340

commit v5 on v4

--- a/solution.py
+++ b/solution.py
@@ -58,7 +58,7 @@
 
 
 def settings(mib):
-    return pltpu.CompilerParams(vmem_limit_bytes=mib * MIB)
+    return pltpu.CompilerParams(vmem_limit_bytes=int(mib * MIB))
 
 
 def cost(flops, size):
@@ -392,7 +392,7 @@
         in_specs=[smem(), vmem(), anyspace],
         out_specs=(vmem(), vmem(), smem(), vmem()),
         scratch_shapes=[pltpu.SemaphoreType.DMA] + spread_scratch(extent, verts),
-        compiler_params=settings(48),
+        compiler_params=settings(49.5),
         cost_estimate=cost(18 * owners * 3 * size_z * cross * 4 * verts, MIB),
         name="spread",
     )(place, table, populations)

time: 63.8 us -> 61.5 us (0.964)
  local copies, waits for them, and re-layouts: 1.81 us -> 0.11 us
    unnamed x10 -> x8, local copies, waits for them, and re-layouts: 1.72 us -> 0.01 us
where the time goes in v5:
time: 61.5 us; the launch traced here: 61.4 us
  Pallas kernels  24.5 us (40%)
  waiting for transfers between devices  18.3 us (30%)
  starting transfers between devices  17.7 us (29%)
  between operations  0.75 us (1%)
    all_to_all x2, waiting for transfers between devices, exchanged(): lax.all_to_all(value, ('gy', 'gz'), split_axis=0, concat_axis=0, tiled=True)  15.6 us
    all_to_all x2, starting transfers between devices, exchanged(): lax.all_to_all(value, ('gy', 'gz'), split_axis=0, concat_axis=0, tiled=True)  10.9 us
    pallas_call x1, Pallas kernels, spread(): pl.pallas_call(functools.partial(spread_kernel, extent), out_shape=(jax.S...  8.81 us
    ppermute x5, starting transfers between devices, shifted(): lax.ppermute(value, axis, [(i, (i + step) % count) for i in range(count)])  6.85 us
    pallas_call x1, Pallas kernels, sample_part(): pl.pallas_call(functools.partial(sample_part_kernel, extent, first, last)...  3.77 us
    pallas_call x1, Pallas kernels, sample(): pl.pallas_call(functools.partial(sample_kernel, extent), out_shape=jax.Sh...  3.37 us
    pallas_call x1, Pallas kernels, build_lists(): pl.pallas_call(kernel, out_shape=(jax.ShapeDtypeStruct((bricks, 2 * GROUP...  3.31 us
    ppermute x5, waiting for transfers between devices, shifted(): lax.ppermute(value, axis, [(i, (i + step) % count) for i in range(count)])  2.73 us
  transfers between devices with their start and end apart: 7, of which 4 were waited for; matrix products, arithmetic and copies ran while one was open for 0% of the time, Pallas kernels for 12%

profile of v5, /device:TPU:0, one launch (start us, length us, event | category | flops | bytes accessed | tf_op | source)
XLA Modules:
  0.0 61.4 jit_solution(17071383859451176946)
XLA Ops:
  0.6 3.3 %vertex_lists.1 = (f32[16,14,4,128]{3,2,1,0:T(4,128)}, s32[2,14,128]{2,1,0:T(8,128)}, s32[28]{0:T(128)}) custom-call(s32[2,14]{1,0:T(2,128)} %bitcast.11, f32[3,14,128]{2,1,0:T(8,128)} %bitcast.13, f32[3,14,128]{2,1,0:T(8,128)} %bitcast.14, s32[3,14,128]{2,1,0:T(8,128)} %bitcast.15, f32[14,8,128]{2,1,0:T(8,128)} %refs_4_.1), custom_call_target="tpu_custom_call" | custom-call | tf_op jit(solution)/shard_map/vertex_lists/pallas_call | solution.py:174
  3.9 7.4 %all-to-all-start = ((f32[16,14,4,128]{3,2,1,0:T(4,128)}), f32[16,14,4,128]{3,2,1,0:T(4,128)S(1)}, u32[]{:S(2)}, u32[]{:S(2)}) async-start(f32[16,14,4,128]{3,2,1,0:T(4,128)} %get-tuple-element.21), calls=%async_computation | async-start | bytes 917504 | tf_op jit(solution)/shard_map/all_to_all | solution.py:889
  11.3 0.1 stack.27.place_ref
  11.4 0.0 copy-start
  11.4 13.1 %all-to-all-done.table_ref = f32[16,14,4,128]{3,2,1,0:T(4,128)S(1)} async-done(((f32[16,14,4,128]{3,2,1,0:T(4,128)}), f32[16,14,4,128]{3,2,1,0:T(4,128)S(1)}, u32[]{:S(2)}, u32[]{:S(2)}) %all-to-all-start) | async-done | bytes 458784 | tf_op jit(solution)/shard_map/all_to_all | solution.py:889
  24.6 8.8 %spread.1 = (f32[384,256]{1,0:T(8,128)S(1)}, f32[34,16,128]{2,1,0:T(8,128)S(1)}, s32[33]{0:T(128)S(1)}, f32[19,16,16,128]{3,2,1,0:T(8,128)S(1)}) custom-call(s32[9]{0:T(128)S(1)} %stack.27.place_ref, f32[16,14,4,128]{3,2,1,0:T(4,128)S(1)} %all-to-all-done.table_ref, f32[19,16,16,128]{3,2,1,0:T(8,128)} %pop_any.1), custom_call_target="tpu_custom_call" | custom-call | flops 14495514624 | bytes 1048576 | tf_op jit(solution)/shard_map/spread/pallas_call | solution.py:384
  33.4 0.0 copy-done
  33.4 0.2 x_faces.1
  33.6 1.2 %collective-permute-start = (f32[10,16,128]{2,1,0:T(8,128)S(1)}, f32[10,16,128]{2,1,0:T(8,128)S(1)}, u32[]{:S(2)}, u32[]{:S(2)}) collective-permute-start(f32[10,16,128]{2,1,0:T(8,128)S(1)} %get-tuple-element.26), channel_id=1, source_target_pairs={{0,16},{16,0},{1,17},{17,1},{2,18},{18,2},{3,19},{19,3},{4,20},{20... | collective-permute-start | bytes 245768 | tf_op jit(solution)/shard_map/ppermute | solution.py:885
  34.8 2.0 %collide.1 = (f32[19,16,16,128]{3,2,1,0:T(8,128)S(1)}, f32[5,16,128]{2,1,0:T(8,128)S(1)}, f32[5,16,128]{2,1,0:T(8,128)S(1)}, f32[16,128]{1,0:T(8,128)S(1)}, f32[...) custom-call(f32[3,256,128]{2,1,0:T(8,128)S(1)} %get-tuple-element.24.field, ...), custom_call_target="tpu_custom_call" | custom-call | flops 16777216 | bytes 8388608 | tf_op jit(solution)/shard_map/collide/pallas_call | solution.py:520
  36.8 1.4 %collective-permute-done.xr_ref.refs_0_ = f32[10,16,128]{2,1,0:T(8,128)S(1)} collective-permute-done((f32[10,16,128]{2,1,0:T(8,128)S(1)}, f32[10,16,128]{2,1,0:T(8,128)S(1)}, u32[]{:S(2)}, u32[]{:S(2)}) %collective-permute-start) | collective-permute-done | bytes 81952 | tf_op jit(solution)/shard_map/ppermute | solution.py:885
  38.1 1.1 %collective-permute-start.1 = (f32[6,16,128]{2,1,0:T(8,128)S(1)}, f32[6,16,128]{2,1,0:T(8,128)S(1)}, u32[]{:S(2)}, u32[]{:S(2)}) collective-permute-start(f32[6,16,128]{2,1,0:T(8,128)S(1)} %get-tuple-element.29), channel_id=1, source_target_pairs={{0,4},{4,8},{8,12},{12,0},{1,5},{5,9},{9,13},{13,1},{2,6},{6,10},{... | collective-permute-start | bytes 147464 | tf_op jit(solution)/shard_map/ppermute | solution.py:885
  39.3 2.7 %collective-permute-start.2 = (f32[6,16,128]{2,1,0:T(8,128)S(1)}, f32[6,16,128]{2,1,0:T(8,128)S(1)}, u32[]{:S(2)}, u32[]{:S(2)}) collective-permute-start(f32[6,16,128]{2,1,0:T(8,128)S(1)} %get-tuple-element.30), channel_id=1, source_target_pairs={{0,12},{4,0},{8,4},{12,8},{1,13},{5,1},{9,5},{13,9},{2,14},{6,2},{... | collective-permute-start | bytes 147464 | tf_op jit(solution)/shard_map/ppermute | solution.py:885
  42.0 3.8 %sample_part.1.part_ref = f32[12,3,2,128]{3,2,1,0:T(2,128)S(1)} custom-call(s32[9]{0:T(128)S(1)} %stack.27.place_ref, f32[16,14,4,128]{3,2,1,0:T(4,128)S(1)} %all-to-all-done.table_ref, bf16[768,256]{1,0:T(8,128)(2,1)S(1)} %get-tuple-element.39.unit_ref, f32[10,16,128]{2,1,0:T(8,128)S(1)} %collective-permute-done.xr_ref.refs_0_), custom_call_target="tpu_custom_call" | custom-call | flops 2415919104 | bytes 1048576 | tf_op jit(solution)/shard_map/sample_part/pallas_call | solution.py:651
  45.8 0.0 collective-permute-done.1.yrp_ref.refs_0_
  45.8 0.0 collective-permute-done.2.yrm_ref.refs_1_
  45.8 3.4 %sample_velocity.1 = f32[16,3,4,128]{3,2,1,0:T(4,128)} custom-call(s32[9]{0:T(128)S(1)} %stack.27.place_ref, s32[33]{0:T(128)S(1)} %get-tuple-element.37.spot_ref, f32[16,14,4,128]{3,2,1,0:T(4,128)S(1)} %all-to-all-done.table_ref, f32[34,16,128]{2,1,0:T(8,128)S(1)} %get-tuple-element.38.packed, bf16[768,256]{1,0:T(8,128)(2,1)S(1)} %get-tuple-element.39.unit_ref, ...), custom_call_target="tpu_custom_call" | custom-call | flops 1610612736 | bytes 1048576 | tf_op jit(solution)/shard_map/sample_velocity/pallas_call | solution.py:710
  49.2 3.5 %all-to-all-start.1 = ((f32[16,3,4,128]{3,2,1,0:T(4,128)}), f32[16,3,4,128]{3,2,1,0:T(4,128)S(1)}, u32[]{:S(2)}, u32[]{:S(2)}) async-start(f32[16,3,4,128]{3,2,1,0:T(4,128)} %sample_velocity.1), calls=%async_computation.1 | async-start | bytes 196608 | tf_op jit(solution)/shard_map/all_to_all | solution.py:889
  52.7 0.1 z_messages.1
  52.8 0.3 collective-permute-start.3
  53.1 1.5 %collective-permute-start.4 = (f32[16,128]{1,0:T(8,128)S(1)}, f32[16,128]{1,0:T(8,128)S(1)}, u32[]{:S(2)}, u32[]{:S(2)}) collective-permute-start(f32[16,128]{1,0:T(8,128)S(1)} %get-tuple-element.34), channel_id=1, source_target_pairs={{0,3},{1,0},{2,1},{3,2},{4,7},{5,4},{6,5},{7,6},{8,11},{9,8},{10,9... | collective-permute-start | bytes 24584 | tf_op jit(solution)/shard_map/ppermute | solution.py:885
  54.5 1.4 %collective-permute-done.3.zrp_ref = f32[16,128]{1,0:T(8,128)S(1)} collective-permute-done((f32[16,128]{1,0:T(8,128)S(1)}, f32[16,128]{1,0:T(8,128)S(1)}, u32[]{:S(2)}, u32[]{:S(2)}) %collective-permute-start.3) | collective-permute-done | bytes 8224 | tf_op jit(solution)/shard_map/ppermute | solution.py:885
  55.9 0.0 collective-permute-done.4.zrm_ref
  55.9 0.0 copy-start.1
  55.9 0.0 copy-start.2
  55.9 0.0 copy-start.3
  55.9 1.7 %stream_populations.1 = f32[19,16,16,128]{3,2,1,0:T(8,128)} custom-call(f32[19,16,16,128]{3,2,1,0:T(8,128)S(1)} %get-tuple-element.25.post, f32[10,16,128]{2,1,0:T(8,128)S(1)} %collective-permute-done.xr_ref.refs_0_, f32[6,16,128]{2,1,0:T(8,128)S(1)} %collective-permute-done.1.yrp_ref.refs_0_, f32[6,16,128]{2,1,0:T(8,128)S(1)} %collective-permute-done.2.yrm_ref.refs_1_, ...), custom_call_target="tpu_custom_call" | custom-call | flops 1048576 | bytes 16777216 | tf_op jit(solution)/shard_map/stream_populations/pallas_call | solution.py:834
  57.6 2.5 %all-to-all-done.1.back_ref = f32[16,3,4,128]{3,2,1,0:T(4,128)S(1)} async-done(((f32[16,3,4,128]{3,2,1,0:T(4,128)}), f32[16,3,4,128]{3,2,1,0:T(4,128)S(1)}, u32[]{:S(2)}, u32[]{:S(2)}) %all-to-all-start.1) | async-done | bytes 98336 | tf_op jit(solution)/shard_map/all_to_all | solution.py:889
  60.0 0.0 copy-done.1
  60.0 0.0 copy-done.2
  60.1 0.0 copy-done.3
  60.1 1.4 %collect_velocity.1 = f32[3,14,128]{2,1,0:T(8,128)} custom-call(s32[2,14]{1,0:T(2,128)S(1)} %bitcast.12, s32[28]{0:T(128)S(1)} %copy-done.3, s32[2,14,128]{2,1,0:T(8,128)S(1)} %copy-done.1, f32[16,3,4,128]{3,2,1,0:T(4,128)S(1)} %all-to-all-done.1.back_ref), custom_call_target="tpu_custom_call" | custom-call | tf_op jit(solution)/shard_map/collect_velocity/pallas_call | solution.py:873
  (2 shorter events, 0.0 us)
Async XLA Ops:
  3.9 20.6 %all-to-all-start = ((f32[16,14,4,128]{3,2,1,0:T(4,128)}), f32[16,14,4,128]{3,2,1,0:T(4,128)S(1)}, u32[]{:S(2)}, u32[]{:S(2)}) async-start(f32[16,14,4,128]{3,2,1,0:T(4,128)} %get-tuple-element.21), calls=%async_computation | async-start | bytes 917504 | tf_op jit(solution)/shard_map/all_to_all | solution.py:889
  11.4 22.0 %copy-start = (s32[16,16,128]{2,1,0:T(8,128)S(1)}, s32[16,16,128]{2,1,0:T(8,128)}, u32[]{:S(2)}) copy-start(s32[16,16,128]{2,1,0:T(8,128)} %solid.3) | copy-start | bytes 393220
  33.6 4.5 %collective-permute-start = (f32[10,16,128]{2,1,0:T(8,128)S(1)}, f32[10,16,128]{2,1,0:T(8,128)S(1)}, u32[]{:S(2)}, u32[]{:S(2)}) collective-permute-start(f32[10,16,128]{2,1,0:T(8,128)S(1)} %get-tuple-element.26), channel_id=1, source_target_pairs={{0,16},{16,0},{1,17},{17,1},{2,18},{18,2},{3,19},{19,3},{4,20},{20... | collective-permute-start | bytes 245768 | tf_op jit(solution)/shard_map/ppermute | solution.py:885
  38.1 7.7 %collective-permute-start.1 = (f32[6,16,128]{2,1,0:T(8,128)S(1)}, f32[6,16,128]{2,1,0:T(8,128)S(1)}, u32[]{:S(2)}, u32[]{:S(2)}) collective-permute-start(f32[6,16,128]{2,1,0:T(8,128)S(1)} %get-tuple-element.29), channel_id=1, source_target_pairs={{0,4},{4,8},{8,12},{12,0},{1,5},{5,9},{9,13},{13,1},{2,6},{6,10},{... | collective-permute-start | bytes 147464 | tf_op jit(solution)/shard_map/ppermute | solution.py:885
  39.3 6.5 %collective-permute-start.2 = (f32[6,16,128]{2,1,0:T(8,128)S(1)}, f32[6,16,128]{2,1,0:T(8,128)S(1)}, u32[]{:S(2)}, u32[]{:S(2)}) collective-permute-start(f32[6,16,128]{2,1,0:T(8,128)S(1)} %get-tuple-element.30), channel_id=1, source_target_pairs={{0,12},{4,0},{8,4},{12,8},{1,13},{5,1},{9,5},{13,9},{2,14},{6,2},{... | collective-permute-start | bytes 147464 | tf_op jit(solution)/shard_map/ppermute | solution.py:885
  49.2 10.9 %all-to-all-start.1 = ((f32[16,3,4,128]{3,2,1,0:T(4,128)}), f32[16,3,4,128]{3,2,1,0:T(4,128)S(1)}, u32[]{:S(2)}, u32[]{:S(2)}) async-start(f32[16,3,4,128]{3,2,1,0:T(4,128)} %sample_velocity.1), calls=%async_computation.1 | async-start | bytes 196608 | tf_op jit(solution)/shard_map/all_to_all | solution.py:889
  52.8 3.2 %collective-permute-start.3 = (f32[16,128]{1,0:T(8,128)S(1)}, f32[16,128]{1,0:T(8,128)S(1)}, u32[]{:S(2)}, u32[]{:S(2)}) collective-permute-start(f32[16,128]{1,0:T(8,128)S(1)} %get-tuple-element.33), channel_id=1, source_target_pairs={{0,1},{1,2},{2,3},{3,0},{4,5},{5,6},{6,7},{7,4},{8,9},{9,10},{10,1... | collective-permute-start | bytes 24584 | tf_op jit(solution)/shard_map/ppermute | solution.py:885
  53.1 2.8 %collective-permute-start.4 = (f32[16,128]{1,0:T(8,128)S(1)}, f32[16,128]{1,0:T(8,128)S(1)}, u32[]{:S(2)}, u32[]{:S(2)}) collective-permute-start(f32[16,128]{1,0:T(8,128)S(1)} %get-tuple-element.34), channel_id=1, source_target_pairs={{0,3},{1,0},{2,1},{3,2},{4,7},{5,4},{6,5},{7,6},{8,11},{9,8},{10,9... | collective-permute-start | bytes 24584 | tf_op jit(solution)/shard_map/ppermute | solution.py:885
  55.9 4.1 %copy-start.1 = (s32[2,14,128]{2,1,0:T(8,128)S(1)}, s32[2,14,128]{2,1,0:T(8,128)}, u32[]{:S(2)}) copy-start(s32[2,14,128]{2,1,0:T(8,128)} %get-tuple-element.36.rank_ref) | copy-start | bytes 43012
  55.9 4.1 %copy-start.2 = (s32[14,2]{0,1:T(2,128)S(1)}, s32[14,2]{0,1:T(2,128)}, u32[]{:S(2)}) copy-start(s32[14,2]{0,1:T(2,128)} %param.13) | copy-start | bytes 340
  55.9 4.1 %copy-start.3 = (s32[28]{0:T(128)S(1)}, s32[28]{0:T(128)}, u32[]{:S(2)}) copy-start(s32[28]{0:T(128)} %get-tuple-element.35.base_ref) | copy-start | bytes 340

commit v6 on v5

--- a/solution.py
+++ b/solution.py
@@ -9,6 +9,8 @@
 
 SLOT_CAP = 4
 GROUPS = 7
+SPREAD_OWNERS = 4
+SPREAD_BLOCKS = 2 * SPREAD_OWNERS
 EDGE_LANE = 80
 
 RELAXATION = 0.8
@@ -244,13 +246,13 @@
 
 def spread_scratch(extent, verts):
     size_x, size_y, size_z = extent
-    depth = SLOT_CAP * 2 * verts
+    depth = SPREAD_BLOCKS * 2 * verts
     return [
         pltpu.VMEM((2, 2, size_x * size_y, depth), BF),
         pltpu.VMEM((2, 6 * size_z, depth), BF),
-        pltpu.VMEM((2, SLOT_CAP, 16, verts), F32),
-        pltpu.VMEM((2, SLOT_CAP, 8, verts), F32),
-        pltpu.VMEM((2, SLOT_CAP, 8, verts), F32),
+        pltpu.VMEM((2, SPREAD_BLOCKS, 16, verts), F32),
+        pltpu.VMEM((2, SPREAD_BLOCKS, 8, verts), F32),
+        pltpu.VMEM((2, SPREAD_BLOCKS, 8, verts), F32),
     ]
 
 
@@ -312,7 +314,7 @@
                                 at_z, force[part * 3 + c], zero
                             )
 
-    def product(slot, blocks=SLOT_CAP):
+    def product(slot, blocks=SPREAD_BLOCKS):
         lines = 3 * size_z
         depth = blocks * 2 * verts
         high = lax.dot_general(
@@ -329,8 +331,8 @@
     return build, product
 
 
-def pair_blocks(table_ref, step):
-    return [block_rows(table_ref, 2 * step + oo, j) for oo in range(2) for j in range(2)]
+def pair_blocks(table_ref, step, owners=2):
+    return [block_rows(table_ref, owners * step + o, j) for o in range(owners) for j in range(2)]
 
 
 def spread_kernel(
@@ -349,21 +351,27 @@
     load.start()
     owners, _, _, verts = table_ref.shape
     build, product = spread_tools(place_ref, extent, verts, total, *scratch)
-    steps = owners // 2
+    steps = owners // SPREAD_OWNERS
     total[...] = jnp.zeros(total.shape, F32)
     packed[...] = jnp.zeros(packed.shape, F32)
-    build(pair_blocks(table_ref, 0), 0)
+
+    def fill(step, slot):
+        build(pair_blocks(table_ref, step, SPREAD_OWNERS), slot)
+
+    def pack(step, spot):
+        for o in range(SPREAD_OWNERS):
+            spot = pack_far(table_ref, packed, spot_ref, SPREAD_OWNERS * step + o, spot)
+        return spot
+
+    fill(0, 0)
 
     def near(i, spot):
-        build(pair_blocks(table_ref, 2 * i + 1), 1)
+        fill(2 * i + 1, 1)
         product(0)
-        for owner in range(2):
-            spot = pack_far(table_ref, packed, spot_ref, 4 * i + owner, spot)
-        build(pair_blocks(table_ref, jnp.minimum(2 * i + 2, steps - 1)), 0)
+        spot = pack(2 * i, spot)
+        fill(jnp.minimum(2 * i + 2, steps - 1), 0)
         product(1)
-        for owner in range(2, 4):
-            spot = pack_far(table_ref, packed, spot_ref, 4 * i + owner, spot)
-        return spot
+        return pack(2 * i + 1, spot)
 
     spot_ref[2 * owners] = lax.fori_loop(0, steps // 2, near, jnp.int32(0))
 

time: 61.5 us -> 61.8 us (level)
  starting transfers between devices: 17.7 us -> 19.5 us
  Pallas kernels: 24.5 us -> 23.5 us
  waiting for transfers between devices: 18.3 us -> 17.6 us
    all_to_all x2, starting transfers between devices: 10.9 us -> 11.8 us  [exchanged(): lax.all_to_all(value, ('gy', 'gz'), split_axis=0, concat_axis=0, tiled=True)]
    ppermute x5, starting transfers between devices: 6.85 us -> 7.66 us  [shifted(): lax.ppermute(value, axis, [(i, (i + step) % count) for i in range(count)])]
    ppermute x5, waiting for transfers between devices: 2.73 us -> 2.04 us  [shifted(): lax.ppermute(value, axis, [(i, (i + step) % count) for i in range(count)])]
    pallas_call x1, Pallas kernels: 3.37 us -> 2.73 us  [sample(): pl.pallas_call(functools.partial(sample_kernel, extent), out_shape=jax.Sh...]
where the time goes in v6:
time: 61.8 us; the launch traced here: 61.4 us
  Pallas kernels  23.5 us (38%)
  starting transfers between devices  19.5 us (32%)
  waiting for transfers between devices  17.6 us (28%)
  between operations  0.75 us (1%)
    all_to_all x2, waiting for transfers between devices, exchanged(): lax.all_to_all(value, ('gy', 'gz'), split_axis=0, concat_axis=0, tiled=True)  15.5 us
    all_to_all x2, starting transfers between devices, exchanged(): lax.all_to_all(value, ('gy', 'gz'), split_axis=0, concat_axis=0, tiled=True)  11.8 us
    pallas_call x1, Pallas kernels, spread(): pl.pallas_call(functools.partial(spread_kernel, extent), out_shape=(jax.S...  8.41 us
    ppermute x5, starting transfers between devices, shifted(): lax.ppermute(value, axis, [(i, (i + step) % count) for i in range(count)])  7.66 us
    pallas_call x1, Pallas kernels, sample_part(): pl.pallas_call(functools.partial(sample_part_kernel, extent, first, last)...  3.77 us
    pallas_call x1, Pallas kernels, build_lists(): pl.pallas_call(kernel, out_shape=(jax.ShapeDtypeStruct((bricks, 2 * GROUP...  3.31 us
    pallas_call x1, Pallas kernels, sample(): pl.pallas_call(functools.partial(sample_kernel, extent), out_shape=jax.Sh...  2.73 us
    ppermute x5, waiting for transfers between devices, shifted(): lax.ppermute(value, axis, [(i, (i + step) % count) for i in range(count)])  2.04 us
  transfers between devices with their start and end apart: 7, of which 4 were waited for; matrix products, arithmetic and copies ran while one was open for 0% of the time, Pallas kernels for 12%

profile of v6, /device:TPU:0, one launch (start us, length us, event | category | flops | bytes accessed | tf_op | source)
XLA Modules:
  0.0 61.4 jit_solution(10560870629352713923)
XLA Ops:
  0.6 3.3 %vertex_lists.1 = (f32[16,14,4,128]{3,2,1,0:T(4,128)}, s32[2,14,128]{2,1,0:T(8,128)}, s32[28]{0:T(128)}) custom-call(s32[2,14]{1,0:T(2,128)} %bitcast.11, f32[3,14,128]{2,1,0:T(8,128)} %bitcast.13, f32[3,14,128]{2,1,0:T(8,128)} %bitcast.14, s32[3,14,128]{2,1,0:T(8,128)} %bitcast.15, f32[14,8,128]{2,1,0:T(8,128)} %refs_4_.1), custom_call_target="tpu_custom_call" | custom-call | tf_op jit(solution)/shard_map/vertex_lists/pallas_call | solution.py:176
  3.9 7.4 %all-to-all-start = ((f32[16,14,4,128]{3,2,1,0:T(4,128)}), f32[16,14,4,128]{3,2,1,0:T(4,128)S(1)}, u32[]{:S(2)}, u32[]{:S(2)}) async-start(f32[16,14,4,128]{3,2,1,0:T(4,128)} %get-tuple-element.21), calls=%async_computation | async-start | bytes 917504 | tf_op jit(solution)/shard_map/all_to_all | solution.py:897
  11.3 0.1 stack.27.place_ref
  11.4 0.0 copy-start
  11.4 13.1 %all-to-all-done.table_ref = f32[16,14,4,128]{3,2,1,0:T(4,128)S(1)} async-done(((f32[16,14,4,128]{3,2,1,0:T(4,128)}), f32[16,14,4,128]{3,2,1,0:T(4,128)S(1)}, u32[]{:S(2)}, u32[]{:S(2)}) %all-to-all-start) | async-done | bytes 458784 | tf_op jit(solution)/shard_map/all_to_all | solution.py:897
  24.6 8.4 %spread.1 = (f32[384,256]{1,0:T(8,128)S(1)}, f32[34,16,128]{2,1,0:T(8,128)S(1)}, s32[33]{0:T(128)S(1)}, f32[19,16,16,128]{3,2,1,0:T(8,128)S(1)}) custom-call(s32[9]{0:T(128)S(1)} %stack.27.place_ref, f32[16,14,4,128]{3,2,1,0:T(4,128)S(1)} %all-to-all-done.table_ref, f32[19,16,16,128]{3,2,1,0:T(8,128)} %pop_any.1), custom_call_target="tpu_custom_call" | custom-call | flops 14495514624 | bytes 1048576 | tf_op jit(solution)/shard_map/spread/pallas_call | solution.py:392
  33.0 0.0 copy-done
  33.0 0.2 x_faces.1
  33.2 2.0 %collective-permute-start = (f32[10,16,128]{2,1,0:T(8,128)S(1)}, f32[10,16,128]{2,1,0:T(8,128)S(1)}, u32[]{:S(2)}, u32[]{:S(2)}) collective-permute-start(f32[10,16,128]{2,1,0:T(8,128)S(1)} %get-tuple-element.26), channel_id=1, source_target_pairs={{0,16},{16,0},{1,17},{17,1},{2,18},{18,2},{3,19},{19,3},{4,20},{20... | collective-permute-start | bytes 245768 | tf_op jit(solution)/shard_map/ppermute | solution.py:893
  35.2 2.0 %collide.1 = (f32[19,16,16,128]{3,2,1,0:T(8,128)S(1)}, f32[5,16,128]{2,1,0:T(8,128)S(1)}, f32[5,16,128]{2,1,0:T(8,128)S(1)}, f32[16,128]{1,0:T(8,128)S(1)}, f32[...) custom-call(f32[3,256,128]{2,1,0:T(8,128)S(1)} %get-tuple-element.24.field, ...), custom_call_target="tpu_custom_call" | custom-call | flops 16777216 | bytes 8388608 | tf_op jit(solution)/shard_map/collide/pallas_call | solution.py:528
  37.2 0.6 collective-permute-done.xr_ref.refs_0_
  37.7 1.5 %collective-permute-start.1 = (f32[6,16,128]{2,1,0:T(8,128)S(1)}, f32[6,16,128]{2,1,0:T(8,128)S(1)}, u32[]{:S(2)}, u32[]{:S(2)}) collective-permute-start(f32[6,16,128]{2,1,0:T(8,128)S(1)} %get-tuple-element.29), channel_id=1, source_target_pairs={{0,4},{4,8},{8,12},{12,0},{1,5},{5,9},{9,13},{13,1},{2,6},{6,10},{... | collective-permute-start | bytes 147464 | tf_op jit(solution)/shard_map/ppermute | solution.py:893
  39.3 2.4 %collective-permute-start.2 = (f32[6,16,128]{2,1,0:T(8,128)S(1)}, f32[6,16,128]{2,1,0:T(8,128)S(1)}, u32[]{:S(2)}, u32[]{:S(2)}) collective-permute-start(f32[6,16,128]{2,1,0:T(8,128)S(1)} %get-tuple-element.30), channel_id=1, source_target_pairs={{0,12},{4,0},{8,4},{12,8},{1,13},{5,1},{9,5},{13,9},{2,14},{6,2},{... | collective-permute-start | bytes 147464 | tf_op jit(solution)/shard_map/ppermute | solution.py:893
  41.6 3.8 %sample_part.1.part_ref = f32[12,3,2,128]{3,2,1,0:T(2,128)S(1)} custom-call(s32[9]{0:T(128)S(1)} %stack.27.place_ref, f32[16,14,4,128]{3,2,1,0:T(4,128)S(1)} %all-to-all-done.table_ref, bf16[768,256]{1,0:T(8,128)(2,1)S(1)} %get-tuple-element.39.unit_ref, f32[10,16,128]{2,1,0:T(8,128)S(1)} %collective-permute-done.xr_ref.refs_0_), custom_call_target="tpu_custom_call" | custom-call | flops 2415919104 | bytes 1048576 | tf_op jit(solution)/shard_map/sample_part/pallas_call | solution.py:659
  45.4 0.0 collective-permute-done.1.yrp_ref.refs_0_
  45.4 0.0 collective-permute-done.2.yrm_ref.refs_1_
  45.4 2.7 %sample_velocity.1 = f32[16,3,4,128]{3,2,1,0:T(4,128)} custom-call(s32[9]{0:T(128)S(1)} %stack.27.place_ref, s32[33]{0:T(128)S(1)} %get-tuple-element.37.spot_ref, f32[16,14,4,128]{3,2,1,0:T(4,128)S(1)} %all-to-all-done.table_ref, f32[34,16,128]{2,1,0:T(8,128)S(1)} %get-tuple-element.38.packed, bf16[768,256]{1,0:T(8,128)(2,1)S(1)} %get-tuple-element.39.unit_ref, ...), custom_call_target="tpu_custom_call" | custom-call | flops 1610612736 | bytes 1048576 | tf_op jit(solution)/shard_map/sample_velocity/pallas_call | solution.py:718
  48.1 4.4 %all-to-all-start.1 = ((f32[16,3,4,128]{3,2,1,0:T(4,128)}), f32[16,3,4,128]{3,2,1,0:T(4,128)S(1)}, u32[]{:S(2)}, u32[]{:S(2)}) async-start(f32[16,3,4,128]{3,2,1,0:T(4,128)} %sample_velocity.1), calls=%async_computation.1 | async-start | bytes 196608 | tf_op jit(solution)/shard_map/all_to_all | solution.py:897
  52.6 0.1 z_messages.1
  52.7 0.5 collective-permute-start.3
  53.1 1.3 %collective-permute-start.4 = (f32[16,128]{1,0:T(8,128)S(1)}, f32[16,128]{1,0:T(8,128)S(1)}, u32[]{:S(2)}, u32[]{:S(2)}) collective-permute-start(f32[16,128]{1,0:T(8,128)S(1)} %get-tuple-element.34), channel_id=1, source_target_pairs={{0,3},{1,0},{2,1},{3,2},{4,7},{5,4},{6,5},{7,6},{8,11},{9,8},{10,9... | collective-permute-start | bytes 24584 | tf_op jit(solution)/shard_map/ppermute | solution.py:893
  54.5 1.5 %collective-permute-done.3.zrp_ref = f32[16,128]{1,0:T(8,128)S(1)} collective-permute-done((f32[16,128]{1,0:T(8,128)S(1)}, f32[16,128]{1,0:T(8,128)S(1)}, u32[]{:S(2)}, u32[]{:S(2)}) %collective-permute-start.3) | collective-permute-done | bytes 8224 | tf_op jit(solution)/shard_map/ppermute | solution.py:893
  55.9 0.0 collective-permute-done.4.zrm_ref
  55.9 0.0 copy-start.1
  55.9 0.0 copy-start.2
  55.9 0.0 copy-start.3
  55.9 1.7 %stream_populations.1 = f32[19,16,16,128]{3,2,1,0:T(8,128)} custom-call(f32[19,16,16,128]{3,2,1,0:T(8,128)S(1)} %get-tuple-element.25.post, f32[10,16,128]{2,1,0:T(8,128)S(1)} %collective-permute-done.xr_ref.refs_0_, f32[6,16,128]{2,1,0:T(8,128)S(1)} %collective-permute-done.1.yrp_ref.refs_0_, f32[6,16,128]{2,1,0:T(8,128)S(1)} %collective-permute-done.2.yrm_ref.refs_1_, ...), custom_call_target="tpu_custom_call" | custom-call | flops 1048576 | bytes 16777216 | tf_op jit(solution)/shard_map/stream_populations/pallas_call | solution.py:842
  57.6 2.4 %all-to-all-done.1.back_ref = f32[16,3,4,128]{3,2,1,0:T(4,128)S(1)} async-done(((f32[16,3,4,128]{3,2,1,0:T(4,128)}), f32[16,3,4,128]{3,2,1,0:T(4,128)S(1)}, u32[]{:S(2)}, u32[]{:S(2)}) %all-to-all-start.1) | async-done | bytes 98336 | tf_op jit(solution)/shard_map/all_to_all | solution.py:897
  60.0 0.0 copy-done.1
  60.0 0.0 copy-done.2
  60.0 0.0 copy-done.3
  60.0 1.4 %collect_velocity.1 = f32[3,14,128]{2,1,0:T(8,128)} custom-call(s32[2,14]{1,0:T(2,128)S(1)} %bitcast.12, s32[28]{0:T(128)S(1)} %copy-done.3, s32[2,14,128]{2,1,0:T(8,128)S(1)} %copy-done.1, f32[16,3,4,128]{3,2,1,0:T(4,128)S(1)} %all-to-all-done.1.back_ref), custom_call_target="tpu_custom_call" | custom-call | tf_op jit(solution)/shard_map/collect_velocity/pallas_call | solution.py:881
  (2 shorter events, 0.0 us)
Async XLA Ops:
  3.9 20.6 %all-to-all-start = ((f32[16,14,4,128]{3,2,1,0:T(4,128)}), f32[16,14,4,128]{3,2,1,0:T(4,128)S(1)}, u32[]{:S(2)}, u32[]{:S(2)}) async-start(f32[16,14,4,128]{3,2,1,0:T(4,128)} %get-tuple-element.21), calls=%async_computation | async-start | bytes 917504 | tf_op jit(solution)/shard_map/all_to_all | solution.py:897
  11.4 21.6 %copy-start = (s32[16,16,128]{2,1,0:T(8,128)S(1)}, s32[16,16,128]{2,1,0:T(8,128)}, u32[]{:S(2)}) copy-start(s32[16,16,128]{2,1,0:T(8,128)} %solid.3) | copy-start | bytes 393220
  33.2 4.5 %collective-permute-start = (f32[10,16,128]{2,1,0:T(8,128)S(1)}, f32[10,16,128]{2,1,0:T(8,128)S(1)}, u32[]{:S(2)}, u32[]{:S(2)}) collective-permute-start(f32[10,16,128]{2,1,0:T(8,128)S(1)} %get-tuple-element.26), channel_id=1, source_target_pairs={{0,16},{16,0},{1,17},{17,1},{2,18},{18,2},{3,19},{19,3},{4,20},{20... | collective-permute-start | bytes 245768 | tf_op jit(solution)/shard_map/ppermute | solution.py:893
  37.7 7.7 %collective-permute-start.1 = (f32[6,16,128]{2,1,0:T(8,128)S(1)}, f32[6,16,128]{2,1,0:T(8,128)S(1)}, u32[]{:S(2)}, u32[]{:S(2)}) collective-permute-start(f32[6,16,128]{2,1,0:T(8,128)S(1)} %get-tuple-element.29), channel_id=1, source_target_pairs={{0,4},{4,8},{8,12},{12,0},{1,5},{5,9},{9,13},{13,1},{2,6},{6,10},{... | collective-permute-start | bytes 147464 | tf_op jit(solution)/shard_map/ppermute | solution.py:893
  39.3 6.1 %collective-permute-start.2 = (f32[6,16,128]{2,1,0:T(8,128)S(1)}, f32[6,16,128]{2,1,0:T(8,128)S(1)}, u32[]{:S(2)}, u32[]{:S(2)}) collective-permute-start(f32[6,16,128]{2,1,0:T(8,128)S(1)} %get-tuple-element.30), channel_id=1, source_target_pairs={{0,12},{4,0},{8,4},{12,8},{1,13},{5,1},{9,5},{13,9},{2,14},{6,2},{... | collective-permute-start | bytes 147464 | tf_op jit(solution)/shard_map/ppermute | solution.py:893
  48.1 11.8 %all-to-all-start.1 = ((f32[16,3,4,128]{3,2,1,0:T(4,128)}), f32[16,3,4,128]{3,2,1,0:T(4,128)S(1)}, u32[]{:S(2)}, u32[]{:S(2)}) async-start(f32[16,3,4,128]{3,2,1,0:T(4,128)} %sample_velocity.1), calls=%async_computation.1 | async-start | bytes 196608 | tf_op jit(solution)/shard_map/all_to_all | solution.py:897
  52.7 3.3 %collective-permute-start.3 = (f32[16,128]{1,0:T(8,128)S(1)}, f32[16,128]{1,0:T(8,128)S(1)}, u32[]{:S(2)}, u32[]{:S(2)}) collective-permute-start(f32[16,128]{1,0:T(8,128)S(1)} %get-tuple-element.33), channel_id=1, source_target_pairs={{0,1},{1,2},{2,3},{3,0},{4,5},{5,6},{6,7},{7,4},{8,9},{9,10},{10,1... | collective-permute-start | bytes 24584 | tf_op jit(solution)/shard_map/ppermute | solution.py:893
  53.1 2.8 %collective-permute-start.4 = (f32[16,128]{1,0:T(8,128)S(1)}, f32[16,128]{1,0:T(8,128)S(1)}, u32[]{:S(2)}, u32[]{:S(2)}) collective-permute-start(f32[16,128]{1,0:T(8,128)S(1)} %get-tuple-element.34), channel_id=1, source_target_pairs={{0,3},{1,0},{2,1},{3,2},{4,7},{5,4},{6,5},{7,6},{8,11},{9,8},{10,9... | collective-permute-start | bytes 24584 | tf_op jit(solution)/shard_map/ppermute | solution.py:893
  55.9 4.1 %copy-start.1 = (s32[2,14,128]{2,1,0:T(8,128)S(1)}, s32[2,14,128]{2,1,0:T(8,128)}, u32[]{:S(2)}) copy-start(s32[2,14,128]{2,1,0:T(8,128)} %get-tuple-element.36.rank_ref) | copy-start | bytes 43012
  55.9 4.1 %copy-start.2 = (s32[14,2]{0,1:T(2,128)S(1)}, s32[14,2]{0,1:T(2,128)}, u32[]{:S(2)}) copy-start(s32[14,2]{0,1:T(2,128)} %param.13) | copy-start | bytes 340
  55.9 4.1 %copy-start.3 = (s32[28]{0:T(128)S(1)}, s32[28]{0:T(128)}, u32[]{:S(2)}) copy-start(s32[28]{0:T(128)} %get-tuple-element.35.base_ref) | copy-start | bytes 340

commit v7 on v6

--- a/solution.py
+++ b/solution.py
@@ -369,11 +369,16 @@
         fill(2 * i + 1, 1)
         product(0)
         spot = pack(2 * i, spot)
-        fill(jnp.minimum(2 * i + 2, steps - 1), 0)
+        fill(2 * i + 2, 0)
         product(1)
         return pack(2 * i + 1, spot)
 
-    spot_ref[2 * owners] = lax.fori_loop(0, steps // 2, near, jnp.int32(0))
+    spot = lax.fori_loop(0, steps // 2 - 1, near, jnp.int32(0))
+    fill(steps - 1, 1)
+    product(0)
+    spot = pack(steps - 2, spot)
+    product(1)
+    spot_ref[2 * owners] = pack(steps - 1, spot)
 
     @pl.loop(0, packed_blocks(spot_ref[2 * owners], verts))
     def _(block):

time: 61.8 us -> 62.3 us (level)
  starting transfers between devices: 19.5 us -> 18.6 us
  Pallas kernels: 23.5 us -> 24.3 us
    pallas_call x1, Pallas kernels: 8.41 us -> 9.19 us  [spread(): pl.pallas_call(functools.partial(spread_kernel, extent), out_shape=(jax.S...]
where the time goes in v7:
time: 62.3 us; the launch traced here: 61.7 us
  Pallas kernels  24.3 us (39%)
  starting transfers between devices  18.6 us (30%)
  waiting for transfers between devices  18 us (29%)
  between operations  0.75 us (1%)
    all_to_all x2, waiting for transfers between devices, exchanged(): lax.all_to_all(value, ('gy', 'gz'), split_axis=0, concat_axis=0, tiled=True)  15.5 us
    all_to_all x2, starting transfers between devices, exchanged(): lax.all_to_all(value, ('gy', 'gz'), split_axis=0, concat_axis=0, tiled=True)  11.3 us
    pallas_call x1, Pallas kernels, spread(): pl.pallas_call(functools.partial(spread_kernel, extent), out_shape=(jax.S...  9.19 us
    ppermute x5, starting transfers between devices, shifted(): lax.ppermute(value, axis, [(i, (i + step) % count) for i in range(count)])  7.25 us
    pallas_call x1, Pallas kernels, sample_part(): pl.pallas_call(functools.partial(sample_part_kernel, extent, first, last)...  3.77 us
    pallas_call x1, Pallas kernels, build_lists(): pl.pallas_call(kernel, out_shape=(jax.ShapeDtypeStruct((bricks, 2 * GROUP...  3.31 us
    pallas_call x1, Pallas kernels, sample(): pl.pallas_call(functools.partial(sample_kernel, extent), out_shape=jax.Sh...  2.73 us
    ppermute x5, waiting for transfers between devices, shifted(): lax.ppermute(value, axis, [(i, (i + step) % count) for i in range(count)])  2.45 us
  transfers between devices with their start and end apart: 7, of which 4 were waited for; matrix products, arithmetic and copies ran while one was open for 0% of the time, Pallas kernels for 12%

profile of v7, /device:TPU:0, one launch (start us, length us, event | category | flops | bytes accessed | tf_op | source)
XLA Modules:
  0.0 61.7 jit_solution(16302964744212667901)
XLA Ops:
  0.6 3.3 %vertex_lists.1 = (f32[16,14,4,128]{3,2,1,0:T(4,128)}, s32[2,14,128]{2,1,0:T(8,128)}, s32[28]{0:T(128)}) custom-call(s32[2,14]{1,0:T(2,128)} %bitcast.11, f32[3,14,128]{2,1,0:T(8,128)} %bitcast.13, f32[3,14,128]{2,1,0:T(8,128)} %bitcast.14, s32[3,14,128]{2,1,0:T(8,128)} %bitcast.15, f32[14,8,128]{2,1,0:T(8,128)} %refs_4_.1), custom_call_target="tpu_custom_call" | custom-call | tf_op jit(solution)/shard_map/vertex_lists/pallas_call | solution.py:176
  3.9 7.4 %all-to-all-start = ((f32[16,14,4,128]{3,2,1,0:T(4,128)}), f32[16,14,4,128]{3,2,1,0:T(4,128)S(1)}, u32[]{:S(2)}, u32[]{:S(2)}) async-start(f32[16,14,4,128]{3,2,1,0:T(4,128)} %get-tuple-element.21), calls=%async_computation | async-start | bytes 917504 | tf_op jit(solution)/shard_map/all_to_all | solution.py:902
  11.3 0.1 stack.27.place_ref
  11.4 0.0 copy-start
  11.4 13.1 %all-to-all-done.table_ref = f32[16,14,4,128]{3,2,1,0:T(4,128)S(1)} async-done(((f32[16,14,4,128]{3,2,1,0:T(4,128)}), f32[16,14,4,128]{3,2,1,0:T(4,128)S(1)}, u32[]{:S(2)}, u32[]{:S(2)}) %all-to-all-start) | async-done | bytes 458784 | tf_op jit(solution)/shard_map/all_to_all | solution.py:902
  24.6 9.2 %spread.1 = (f32[384,256]{1,0:T(8,128)S(1)}, f32[34,16,128]{2,1,0:T(8,128)S(1)}, s32[33]{0:T(128)S(1)}, f32[19,16,16,128]{3,2,1,0:T(8,128)S(1)}) custom-call(s32[9]{0:T(128)S(1)} %stack.27.place_ref, f32[16,14,4,128]{3,2,1,0:T(4,128)S(1)} %all-to-all-done.table_ref, f32[19,16,16,128]{3,2,1,0:T(8,128)} %pop_any.1), custom_call_target="tpu_custom_call" | custom-call | flops 14495514624 | bytes 1048576 | tf_op jit(solution)/shard_map/spread/pallas_call | solution.py:397
  33.8 0.0 copy-done
  33.8 0.2 x_faces.1
  34.0 1.6 %collective-permute-start = (f32[10,16,128]{2,1,0:T(8,128)S(1)}, f32[10,16,128]{2,1,0:T(8,128)S(1)}, u32[]{:S(2)}, u32[]{:S(2)}) collective-permute-start(f32[10,16,128]{2,1,0:T(8,128)S(1)} %get-tuple-element.26), channel_id=1, source_target_pairs={{0,16},{16,0},{1,17},{17,1},{2,18},{18,2},{3,19},{19,3},{4,20},{20... | collective-permute-start | bytes 245768 | tf_op jit(solution)/shard_map/ppermute | solution.py:898
  35.6 2.0 %collide.1 = (f32[19,16,16,128]{3,2,1,0:T(8,128)S(1)}, f32[5,16,128]{2,1,0:T(8,128)S(1)}, f32[5,16,128]{2,1,0:T(8,128)S(1)}, f32[16,128]{1,0:T(8,128)S(1)}, f32[...) custom-call(f32[3,256,128]{2,1,0:T(8,128)S(1)} %get-tuple-element.24.field, ...), custom_call_target="tpu_custom_call" | custom-call | flops 16777216 | bytes 8388608 | tf_op jit(solution)/shard_map/collide/pallas_call | solution.py:533
  37.5 1.0 %collective-permute-done.xr_ref.refs_0_ = f32[10,16,128]{2,1,0:T(8,128)S(1)} collective-permute-done((f32[10,16,128]{2,1,0:T(8,128)S(1)}, f32[10,16,128]{2,1,0:T(8,128)S(1)}, u32[]{:S(2)}, u32[]{:S(2)}) %collective-permute-start) | collective-permute-done | bytes 81952 | tf_op jit(solution)/shard_map/ppermute | solution.py:898
  38.5 1.5 %collective-permute-start.1 = (f32[6,16,128]{2,1,0:T(8,128)S(1)}, f32[6,16,128]{2,1,0:T(8,128)S(1)}, u32[]{:S(2)}, u32[]{:S(2)}) collective-permute-start(f32[6,16,128]{2,1,0:T(8,128)S(1)} %get-tuple-element.29), channel_id=1, source_target_pairs={{0,4},{4,8},{8,12},{12,0},{1,5},{5,9},{9,13},{13,1},{2,6},{6,10},{... | collective-permute-start | bytes 147464 | tf_op jit(solution)/shard_map/ppermute | solution.py:898
  40.0 2.4 %collective-permute-start.2 = (f32[6,16,128]{2,1,0:T(8,128)S(1)}, f32[6,16,128]{2,1,0:T(8,128)S(1)}, u32[]{:S(2)}, u32[]{:S(2)}) collective-permute-start(f32[6,16,128]{2,1,0:T(8,128)S(1)} %get-tuple-element.30), channel_id=1, source_target_pairs={{0,12},{4,0},{8,4},{12,8},{1,13},{5,1},{9,5},{13,9},{2,14},{6,2},{... | collective-permute-start | bytes 147464 | tf_op jit(solution)/shard_map/ppermute | solution.py:898
  42.4 3.8 %sample_part.1.part_ref = f32[12,3,2,128]{3,2,1,0:T(2,128)S(1)} custom-call(s32[9]{0:T(128)S(1)} %stack.27.place_ref, f32[16,14,4,128]{3,2,1,0:T(4,128)S(1)} %all-to-all-done.table_ref, bf16[768,256]{1,0:T(8,128)(2,1)S(1)} %get-tuple-element.39.unit_ref, f32[10,16,128]{2,1,0:T(8,128)S(1)} %collective-permute-done.xr_ref.refs_0_), custom_call_target="tpu_custom_call" | custom-call | flops 2415919104 | bytes 1048576 | tf_op jit(solution)/shard_map/sample_part/pallas_call | solution.py:664
  46.2 0.0 collective-permute-done.1.yrp_ref.refs_0_
  46.2 0.0 collective-permute-done.2.yrm_ref.refs_1_
  46.2 2.7 %sample_velocity.1 = f32[16,3,4,128]{3,2,1,0:T(4,128)} custom-call(s32[9]{0:T(128)S(1)} %stack.27.place_ref, s32[33]{0:T(128)S(1)} %get-tuple-element.37.spot_ref, f32[16,14,4,128]{3,2,1,0:T(4,128)S(1)} %all-to-all-done.table_ref, f32[34,16,128]{2,1,0:T(8,128)S(1)} %get-tuple-element.38.packed, bf16[768,256]{1,0:T(8,128)(2,1)S(1)} %get-tuple-element.39.unit_ref, ...), custom_call_target="tpu_custom_call" | custom-call | flops 1610612736 | bytes 1048576 | tf_op jit(solution)/shard_map/sample_velocity/pallas_call | solution.py:723
  48.9 3.9 %all-to-all-start.1 = ((f32[16,3,4,128]{3,2,1,0:T(4,128)}), f32[16,3,4,128]{3,2,1,0:T(4,128)S(1)}, u32[]{:S(2)}, u32[]{:S(2)}) async-start(f32[16,3,4,128]{3,2,1,0:T(4,128)} %sample_velocity.1), calls=%async_computation.1 | async-start | bytes 196608 | tf_op jit(solution)/shard_map/all_to_all | solution.py:902
  52.9 0.1 z_messages.1
  52.9 0.5 collective-permute-start.3
  53.4 1.3 %collective-permute-start.4 = (f32[16,128]{1,0:T(8,128)S(1)}, f32[16,128]{1,0:T(8,128)S(1)}, u32[]{:S(2)}, u32[]{:S(2)}) collective-permute-start(f32[16,128]{1,0:T(8,128)S(1)} %get-tuple-element.34), channel_id=1, source_target_pairs={{0,3},{1,0},{2,1},{3,2},{4,7},{5,4},{6,5},{7,6},{8,11},{9,8},{10,9... | collective-permute-start | bytes 24584 | tf_op jit(solution)/shard_map/ppermute | solution.py:898
  54.7 1.5 %collective-permute-done.3.zrp_ref = f32[16,128]{1,0:T(8,128)S(1)} collective-permute-done((f32[16,128]{1,0:T(8,128)S(1)}, f32[16,128]{1,0:T(8,128)S(1)}, u32[]{:S(2)}, u32[]{:S(2)}) %collective-permute-start.3) | collective-permute-done | bytes 8224 | tf_op jit(solution)/shard_map/ppermute | solution.py:898
  56.2 0.0 collective-permute-done.4.zrm_ref
  56.2 0.0 copy-start.1
  56.2 0.0 copy-start.2
  56.2 0.0 copy-start.3
  56.2 1.7 %stream_populations.1 = f32[19,16,16,128]{3,2,1,0:T(8,128)} custom-call(f32[19,16,16,128]{3,2,1,0:T(8,128)S(1)} %get-tuple-element.25.post, f32[10,16,128]{2,1,0:T(8,128)S(1)} %collective-permute-done.xr_ref.refs_0_, f32[6,16,128]{2,1,0:T(8,128)S(1)} %collective-permute-done.1.yrp_ref.refs_0_, f32[6,16,128]{2,1,0:T(8,128)S(1)} %collective-permute-done.2.yrm_ref.refs_1_, ...), custom_call_target="tpu_custom_call" | custom-call | flops 1048576 | bytes 16777216 | tf_op jit(solution)/shard_map/stream_populations/pallas_call | solution.py:847
  57.9 2.4 %all-to-all-done.1.back_ref = f32[16,3,4,128]{3,2,1,0:T(4,128)S(1)} async-done(((f32[16,3,4,128]{3,2,1,0:T(4,128)}), f32[16,3,4,128]{3,2,1,0:T(4,128)S(1)}, u32[]{:S(2)}, u32[]{:S(2)}) %all-to-all-start.1) | async-done | bytes 98336 | tf_op jit(solution)/shard_map/all_to_all | solution.py:902
  60.3 0.0 copy-done.1
  60.3 0.0 copy-done.2
  60.3 0.0 copy-done.3
  60.3 1.4 %collect_velocity.1 = f32[3,14,128]{2,1,0:T(8,128)} custom-call(s32[2,14]{1,0:T(2,128)S(1)} %bitcast.12, s32[28]{0:T(128)S(1)} %copy-done.3, s32[2,14,128]{2,1,0:T(8,128)S(1)} %copy-done.1, f32[16,3,4,128]{3,2,1,0:T(4,128)S(1)} %all-to-all-done.1.back_ref), custom_call_target="tpu_custom_call" | custom-call | tf_op jit(solution)/shard_map/collect_velocity/pallas_call | solution.py:886
  (2 shorter events, 0.0 us)
Async XLA Ops:
  3.9 20.6 %all-to-all-start = ((f32[16,14,4,128]{3,2,1,0:T(4,128)}), f32[16,14,4,128]{3,2,1,0:T(4,128)S(1)}, u32[]{:S(2)}, u32[]{:S(2)}) async-start(f32[16,14,4,128]{3,2,1,0:T(4,128)} %get-tuple-element.21), calls=%async_computation | async-start | bytes 917504 | tf_op jit(solution)/shard_map/all_to_all | solution.py:902
  11.4 22.3 %copy-start = (s32[16,16,128]{2,1,0:T(8,128)S(1)}, s32[16,16,128]{2,1,0:T(8,128)}, u32[]{:S(2)}) copy-start(s32[16,16,128]{2,1,0:T(8,128)} %solid.3) | copy-start | bytes 393220
  34.0 4.5 %collective-permute-start = (f32[10,16,128]{2,1,0:T(8,128)S(1)}, f32[10,16,128]{2,1,0:T(8,128)S(1)}, u32[]{:S(2)}, u32[]{:S(2)}) collective-permute-start(f32[10,16,128]{2,1,0:T(8,128)S(1)} %get-tuple-element.26), channel_id=1, source_target_pairs={{0,16},{16,0},{1,17},{17,1},{2,18},{18,2},{3,19},{19,3},{4,20},{20... | collective-permute-start | bytes 245768 | tf_op jit(solution)/shard_map/ppermute | solution.py:898
  38.5 7.7 %collective-permute-start.1 = (f32[6,16,128]{2,1,0:T(8,128)S(1)}, f32[6,16,128]{2,1,0:T(8,128)S(1)}, u32[]{:S(2)}, u32[]{:S(2)}) collective-permute-start(f32[6,16,128]{2,1,0:T(8,128)S(1)} %get-tuple-element.29), channel_id=1, source_target_pairs={{0,4},{4,8},{8,12},{12,0},{1,5},{5,9},{9,13},{13,1},{2,6},{6,10},{... | collective-permute-start | bytes 147464 | tf_op jit(solution)/shard_map/ppermute | solution.py:898
  40.0 6.1 %collective-permute-start.2 = (f32[6,16,128]{2,1,0:T(8,128)S(1)}, f32[6,16,128]{2,1,0:T(8,128)S(1)}, u32[]{:S(2)}, u32[]{:S(2)}) collective-permute-start(f32[6,16,128]{2,1,0:T(8,128)S(1)} %get-tuple-element.30), channel_id=1, source_target_pairs={{0,12},{4,0},{8,4},{12,8},{1,13},{5,1},{9,5},{13,9},{2,14},{6,2},{... | collective-permute-start | bytes 147464 | tf_op jit(solution)/shard_map/ppermute | solution.py:898
  48.9 11.3 %all-to-all-start.1 = ((f32[16,3,4,128]{3,2,1,0:T(4,128)}), f32[16,3,4,128]{3,2,1,0:T(4,128)S(1)}, u32[]{:S(2)}, u32[]{:S(2)}) async-start(f32[16,3,4,128]{3,2,1,0:T(4,128)} %sample_velocity.1), calls=%async_computation.1 | async-start | bytes 196608 | tf_op jit(solution)/shard_map/all_to_all | solution.py:902
  52.9 3.3 %collective-permute-start.3 = (f32[16,128]{1,0:T(8,128)S(1)}, f32[16,128]{1,0:T(8,128)S(1)}, u32[]{:S(2)}, u32[]{:S(2)}) collective-permute-start(f32[16,128]{1,0:T(8,128)S(1)} %get-tuple-element.33), channel_id=1, source_target_pairs={{0,1},{1,2},{2,3},{3,0},{4,5},{5,6},{6,7},{7,4},{8,9},{9,10},{10,1... | collective-permute-start | bytes 24584 | tf_op jit(solution)/shard_map/ppermute | solution.py:898
  53.4 2.8 %collective-permute-start.4 = (f32[16,128]{1,0:T(8,128)S(1)}, f32[16,128]{1,0:T(8,128)S(1)}, u32[]{:S(2)}, u32[]{:S(2)}) collective-permute-start(f32[16,128]{1,0:T(8,128)S(1)} %get-tuple-element.34), channel_id=1, source_target_pairs={{0,3},{1,0},{2,1},{3,2},{4,7},{5,4},{6,5},{7,6},{8,11},{9,8},{10,9... | collective-permute-start | bytes 24584 | tf_op jit(solution)/shard_map/ppermute | solution.py:898
  56.2 4.1 %copy-start.1 = (s32[2,14,128]{2,1,0:T(8,128)S(1)}, s32[2,14,128]{2,1,0:T(8,128)}, u32[]{:S(2)}) copy-start(s32[2,14,128]{2,1,0:T(8,128)} %get-tuple-element.36.rank_ref) | copy-start | bytes 43012
  56.2 4.1 %copy-start.2 = (s32[14,2]{0,1:T(2,128)S(1)}, s32[14,2]{0,1:T(2,128)}, u32[]{:S(2)}) copy-start(s32[14,2]{0,1:T(2,128)} %param.13) | copy-start | bytes 340
  56.2 4.1 %copy-start.3 = (s32[28]{0:T(128)S(1)}, s32[28]{0:T(128)}, u32[]{:S(2)}) copy-start(s32[28]{0:T(128)} %get-tuple-element.35.base_ref) | copy-start | bytes 340
